TPU v7x, 32 devices: a whole 2x2x4 slice. The times are simulated.
32 devices in a mesh: sec: 4 (over y, x), bulk: 8 (over z, core).
Axes of the slice: x: 2, y: 2, z: 4, core: 2. Of those that a mesh axis runs over, the one named last changes fastest.
Arguments:
- displacement: float32 [3, 4096], P(None, ('sec', 'bulk')), may hold values from -6 to 6
- nodal_load: float32 [3, 4096], P(None, ('sec', 'bulk')), may hold values from -12 to 12
- connectivity: int32 [4, 16384], P(None, ('sec', 'bulk')), may hold values from 0 to 127
- shape_grads: float32 [12, 16384], P(None, ('sec', 'bulk'))
- elem_volume: float32 [16384], P(('sec', 'bulk')), may hold values from 0.3 to 3
- point_map: int32 [16384], P(('sec', 'bulk')), may hold values from 0 to 16383, as said below
- vol_blocks: int32 [8, 8], P('bulk'), may hold values from 1 to 4, as said below
- c_affine: float32 [8, 8, 36], P('bulk')
- coupling: float32 [20, 8, 6, 128], P(None, 'bulk'), may hold values from -15 to 15
- diag_blocks: bfloat16 [20, 8, 128, 128], P(None, 'bulk'), as said below
- diag_normal: float32 [20, 8, 6], P(None, 'bulk'), may hold values from -4 to 4
- off_blocks: bfloat16 [32, 8, 128, 128], P(None, 'bulk'), may hold values from -0.5 to 0.5
- off_row: int32 [32, 8], P(None, 'bulk'), may hold values from 0 to 19, as said below
- off_col: int32 [32, 8], P(None, 'bulk'), may hold values from 0 to 19, as said below
- off_normal: float32 [32, 8, 6], P(None, 'bulk'), may hold values from -4 to 4
- off_count: int32 [8], P('bulk'), may hold values from 4 to 32, as said below
- fluct_state: bfloat16 [16384, 3072], P(('sec', 'bulk')), as said below
Outputs:
- residual: float32 [3, 4096], P(None, ('sec', 'bulk'))
- product: float32 [3, 4096], P(None, ('sec', 'bulk'))
- update: float32 [3, 4096], P(None, ('sec', 'bulk'))
- fluct_new: bfloat16 [16384, 3072], P(('sec', 'bulk'))
Inputs may be any that keep to these rules, and one draw needn't show every extreme that they name: o = point_map[e] // 512 is the serving device, in the order of sec and bulk with sec slowest, and p = point_map[e] % 512 its slot; values are distinct. Device s sends exactly 16 points to every server, 4 of them in volumes with c block rows for each c = 1 .. 4: among the server's slots whose volume has c block rows, taken in increasing order, the one numbered s. `vol_blocks`: each group has 2 volumes of each size from 1 to 4, so 20 block rows in all. `off_row`: A contact's row and column lie in the block rows of one volume of its group, and differ unless that volume has one block row. `off_col`: see off_row. Slots below off_count of a group are in use, the others are not; a multiple of 4, and one group uses all slots. `diag_blocks`: the diagonal entries of every diagonal block lie between 2.5 and 6.5. `fluct_state`: levels a >= the block rows of the point's volume are zero.
All inputs are finite; a program needn't handle non-finite values.
Results may differ from a plain program's by a relative error of at most 0.001.
The roundings to bfloat16 on the way count: a program that leaves them out, or rounds other values in their place, can miss the bound.
Values may be sent and summed in bfloat16 or wider, within the bound.
No kernel may reach another device: no remote copies, remote signals or barrier semaphores. Data moves between devices by JAX's collectives and lax.ppermute only.
A program may use at most 128 MiB of HBM per device.

v0:
```python
import jax
import jax.numpy as jnp
from jax import lax
from jax.sharding import PartitionSpec as P

BS = 128
NBMAX = 4
VOL_GRP = 8
GPV_DEV = 64
SWEEPS = 3
ROWS_GRP = 20


HIGHEST_PREC = lax.Precision.HIGHEST
GAIN_NORMAL = 0.4
CLIP_RMS = 1.0


def strain_of(shape_grads, nodal):
    shaped = shape_grads.reshape(4, 3, -1)
    grad_x, grad_y, grad_z = (shaped[:, 0], shaped[:, 1], shaped[:, 2])
    disp_x, disp_y, disp_z = (nodal[0], nodal[1], nodal[2])
    return jnp.stack(
        [
            jnp.sum(grad_x * disp_x, axis=0),
            jnp.sum(grad_y * disp_y, axis=0),
            jnp.sum(grad_z * disp_z, axis=0),
            jnp.sum(grad_z * disp_y + grad_y * disp_z, axis=0),
            jnp.sum(grad_z * disp_x + grad_x * disp_z, axis=0),
            jnp.sum(grad_y * disp_x + grad_x * disp_y, axis=0),
        ]
    )


def forces_of(shape_grads, stress):
    shaped = shape_grads.reshape(4, 3, -1)
    grad_x, grad_y, grad_z = (shaped[:, 0], shaped[:, 1], shaped[:, 2])
    force_x = grad_x * stress[0] + grad_z * stress[4] + grad_y * stress[5]
    force_y = grad_y * stress[1] + grad_z * stress[3] + grad_x * stress[5]
    force_z = grad_z * stress[2] + grad_y * stress[3] + grad_x * stress[4]
    return jnp.stack([force_x, force_y, force_z])


def apply_tangent(tangent_cols, strain):
    return jnp.sum(tangent_cols.reshape(6, 6, -1) * strain[None, :, :], axis=1)


def assemble(forces, node_ids, node_total):
    flat_ids = node_ids.reshape(-1)
    return jnp.stack(
        [
            jax.ops.segment_sum(forces[component].reshape(-1), flat_ids, num_segments=node_total)
            for component in range(3)
        ]
    )


def row_layout(vol_sizes):
    row_ends = jnp.cumsum(vol_sizes)
    starts = row_ends - vol_sizes
    row_ids = jnp.arange(ROWS_GRP, dtype=jnp.int32)
    row_volume = jnp.sum((row_ids[:, None] >= row_ends[None, :]).astype(jnp.int32), axis=1)
    onehot = jnp.arange(VOL_GRP, dtype=jnp.int32)[:, None] == row_volume[None, :]
    row_level = row_ids - jnp.sum(jnp.where(onehot, starts[:, None], 0), axis=0)
    return (row_volume, onehot.astype(jnp.float32), row_volume * NBMAX + row_level, row_level)


def state_rows(state_slots, gather_index):
    shaped = state_slots.reshape(VOL_GRP, GPV_DEV, NBMAX, BS, 6)
    reordered = jnp.transpose(shaped, (0, 2, 3, 1, 4)).reshape(VOL_GRP * NBMAX, BS, GPV_DEV * 6)
    return reordered[gather_index]


def rows_state(row_values, gather_index):
    padded = (
        jnp.zeros((VOL_GRP * NBMAX, BS, GPV_DEV * 6), row_values.dtype)
        .at[gather_index]
        .set(row_values)
    )
    shaped = padded.reshape(VOL_GRP, NBMAX, BS, GPV_DEV, 6)
    return jnp.transpose(shaped, (0, 3, 1, 2, 4)).reshape(VOL_GRP * GPV_DEV, NBMAX * BS * 6)


def slot_layout(vol_sizes, per_class):
    vol_ids = jnp.arange(VOL_GRP, dtype=jnp.int32)
    earlier = (vol_sizes[None, :] == vol_sizes[:, None]) & (vol_ids[None, :] < vol_ids[:, None])
    vol_rank = jnp.sum(earlier.astype(jnp.int32), axis=1)
    column_ids = jnp.arange(GPV_DEV, dtype=jnp.int32)
    slot_rank = (vol_rank[:, None] * GPV_DEV + column_ids[None, :]).reshape(-1)
    slot_sizes = jnp.broadcast_to(vol_sizes[:, None], (VOL_GRP, GPV_DEV)).reshape(-1)
    slot_ids = jnp.arange(VOL_GRP * GPV_DEV, dtype=jnp.int32)
    slot_source = slot_rank // per_class
    recv_order = jnp.argsort(slot_source * (VOL_GRP * GPV_DEV) + slot_ids)
    recv_position = jnp.zeros_like(slot_ids).at[recv_order].set(slot_ids)
    return (slot_sizes, slot_source, recv_order, recv_position)


def contact_terms(applied, fluct_low, off_blk, off_rows, off_cols, off_scale_cols):
    contrib = jnp.einsum(
        "oab,obc->oac", off_blk, fluct_low[off_cols], preferred_element_type=jnp.float32
    )
    result = applied.at[off_rows].add(contrib * off_scale_cols[:, None, :])
    return result


def micro_solve(
    strain_slots,
    fluctuation,
    vol_sizes,
    layout,
    c_affine,
    coupling,
    diag_blk,
    diag_nrm,
    off_blk,
    off_rows,
    off_cols,
    off_nrm,
    live_count,
):
    slot_total = off_blk.shape[0]
    row_volume, onehot, gather_index, row_level = layout
    strain_vg = strain_slots.astype(jnp.float32).reshape(VOL_GRP, GPV_DEV, 6)
    strain_rows = jnp.einsum("vr,vgk->rgk", onehot, strain_vg, precision=HIGHEST_PREC)
    diag_scale = 1.0 + GAIN_NORMAL * jnp.tanh(
        jnp.einsum("rk,rgk->rg", diag_nrm, strain_rows, precision=HIGHEST_PREC)
    )
    diag_cols = jnp.repeat(diag_scale, 6, axis=1)
    off_strain = strain_vg[row_volume[off_rows]]
    live_mask = (jnp.arange(slot_total, dtype=jnp.int32) < live_count).astype(jnp.float32)
    off_scale = (
        1.0
        + GAIN_NORMAL
        * jnp.tanh(jnp.einsum("ok,ogk->og", off_nrm, off_strain, precision=HIGHEST_PREC))
    ) * live_mask[:, None]
    off_scale_cols = jnp.repeat(off_scale, 6, axis=1)
    diag_vals = jnp.diagonal(diag_blk, axis1=1, axis2=2).astype(jnp.float32)
    load_rows = jnp.tile(jnp.swapaxes(coupling, 1, 2), (1, 1, GPV_DEV))
    denominator = diag_vals[:, :, None] * diag_cols[:, None, :]
    for sweep_index in range(SWEEPS):
        fluct_low = fluctuation.astype(jnp.bfloat16)
        applied = (
            jnp.einsum("rab,rbc->rac", diag_blk, fluct_low, preferred_element_type=jnp.float32)
            * diag_cols[:, None, :]
        )
        applied = contact_terms(applied, fluct_low, off_blk, off_rows, off_cols, off_scale_cols)
        fluctuation = fluctuation + (load_rows - applied) / denominator
    projection = jnp.einsum("rid,rdc->ric", coupling, fluctuation, precision=HIGHEST_PREC)
    vol_proj = jnp.einsum("vr,ric->vic", onehot, projection, precision=HIGHEST_PREC)
    vol_proj = vol_proj / (vol_sizes.astype(jnp.float32) * BS)[:, None, None]
    tangent = c_affine.reshape(VOL_GRP, 6, 1, 6) - vol_proj.reshape(VOL_GRP, 6, GPV_DEV, 6)
    tangent = (
        jnp.transpose(tangent, (0, 2, 1, 3)).reshape(VOL_GRP * GPV_DEV, 36).astype(jnp.bfloat16)
    )
    return (tangent, fluctuation.astype(jnp.bfloat16))


def on_device(
    displacement,
    nodal_load,
    connectivity,
    shape_grads,
    elem_volume,
    point_map,
    vol_blocks,
    c_affine,
    coupling,
    diag_blocks,
    diag_normal,
    off_blocks,
    off_row,
    off_col,
    off_normal,
    off_count,
    fluct_state,
):
    elem_count = connectivity.shape[1]
    node_count = displacement.shape[1]
    state_width = fluct_state.shape[1]
    devices = lax.axis_size(("sec", "bulk"))
    sections = lax.axis_size("sec")
    owners = lax.axis_size("bulk")
    per_peer = elem_count // devices
    element_ids = jnp.arange(elem_count, dtype=jnp.int32)
    strain = strain_of(shape_grads, displacement[:, connectivity])
    send_order = jnp.argsort(point_map)
    send_position = jnp.zeros_like(element_ids).at[send_order].set(element_ids)
    own_sizes = vol_blocks[0]
    layout = row_layout(own_sizes)
    slot_sizes, slot_source, recv_order, recv_position = slot_layout(own_sizes, per_peer // NBMAX)
    strain_send = strain.T[send_order].astype(jnp.bfloat16).reshape(devices, per_peer * 6)
    state_send = fluct_state[send_order].reshape(devices, per_peer * state_width)
    strain_got, state_got = (
        lax.all_to_all(
            lax.all_to_all(
                strain_send.reshape(sections, owners, -1),
                "sec",
                split_axis=0,
                concat_axis=0,
                tiled=True,
            ),
            "bulk",
            split_axis=1,
            concat_axis=1,
            tiled=True,
        ),
        lax.all_to_all(
            lax.all_to_all(
                state_send.reshape(sections, owners, -1),
                "sec",
                split_axis=0,
                concat_axis=0,
                tiled=True,
            ),
            "bulk",
            split_axis=1,
            concat_axis=1,
            tiled=True,
        ),
    )
    strain_slots = strain_got.reshape(elem_count, 6)[recv_position]
    state_slots = state_got.reshape(elem_count, state_width)[recv_position]
    fluctuation = state_rows(state_slots, layout[2]).astype(jnp.float32)
    tangent, fluct_rows = micro_solve(
        strain_slots,
        fluctuation,
        own_sizes,
        layout,
        c_affine[0],
        coupling[:, 0],
        diag_blocks[:, 0],
        diag_normal[:, 0],
        off_blocks[:, 0],
        off_row[:, 0],
        off_col[:, 0],
        off_normal[:, 0],
        off_count[0],
    )
    tangent_send = tangent[recv_order].reshape(devices, per_peer * 36)
    state_back = rows_state(fluct_rows, layout[2])[recv_order].reshape(
        devices, per_peer * state_width
    )
    tangent_got, state_home = (
        lax.all_to_all(
            lax.all_to_all(
                tangent_send.reshape(sections, owners, -1),
                "sec",
                split_axis=0,
                concat_axis=0,
                tiled=True,
            ),
            "bulk",
            split_axis=1,
            concat_axis=1,
            tiled=True,
        ),
        lax.all_to_all(
            lax.all_to_all(
                state_back.reshape(sections, owners, -1),
                "sec",
                split_axis=0,
                concat_axis=0,
                tiled=True,
            ),
            "bulk",
            split_axis=1,
            concat_axis=1,
            tiled=True,
        ),
    )
    tangent_elem = tangent_got.reshape(elem_count, 36)[send_position]
    fluct_new = state_home.reshape(elem_count, state_width)[send_position]
    tangent_cols = tangent_elem.astype(jnp.float32).T
    weights = elem_volume[None, :]
    stress = apply_tangent(tangent_cols, strain)
    residual = (
        assemble(forces_of(shape_grads, weights * stress), connectivity, node_count) - nodal_load
    )
    norm_sq = lax.psum(jnp.sum(residual * residual), ("sec", "bulk"))
    root_mean = jnp.sqrt(norm_sq / (3.0 * node_count * devices) + 1e-06)
    update = -jnp.minimum(1.0, CLIP_RMS / root_mean) * residual
    trial_strain = strain_of(shape_grads, residual[:, connectivity])
    product = assemble(
        forces_of(shape_grads, weights * apply_tangent(tangent_cols, trial_strain)),
        connectivity,
        node_count,
    )
    return (residual, product, update, fluct_new)


def solution(mesh):
    return jax.shard_map(
        on_device,
        mesh=mesh,
        in_specs=(
            P(None, ("sec", "bulk")),
            P(None, ("sec", "bulk")),
            P(None, ("sec", "bulk")),
            P(None, ("sec", "bulk")),
            P(("sec", "bulk")),
            P(("sec", "bulk")),
            P("bulk", None),
            P("bulk", None, None),
            P(None, "bulk", None, None),
            P(None, "bulk", None, None),
            P(None, "bulk", None),
            P(None, "bulk", None, None),
            P(None, "bulk"),
            P(None, "bulk"),
            P(None, "bulk", None),
            P("bulk"),
            P(("sec", "bulk"), None),
        ),
        out_specs=(
            P(None, ("sec", "bulk")),
            P(None, ("sec", "bulk")),
            P(None, ("sec", "bulk")),
            P(("sec", "bulk"), None),
        ),
        check_vma=False,
    )
```

profile of v0, /device:TPU:0, one launch (start us, length us, event | category | flops | bytes accessed | tf_op | source)
XLA Modules:
  0.0 608.9 jit_solution(11493722744717039109)
XLA Ops:
  3.1 7.6 %gather_fusion.3 = f32[2048,3]{1,0:T(8,128)} fusion(f32[3,128]{0,1:T(8,128)S(1)} %copy.280, s32[2048]{0:T(1024)S(1)} %broadcast_clamp_fusion), kind=kCustom, calls=%fused_computation.3 | custom fusion | bytes 57344 | tf_op jit(solution)/shard_map/gather | solution.py:185
  12.6 4.4 sort.31
  19.7 5.2 all-to-all-start.2
  24.9 3.8 gather_fusion
  28.7 4.8 reshape_reshape.10
  33.5 4.2 all-to-all-start
  38.3 35.0 %all-to-all-done = bf16[4,8,49152]{2,1,0:T(8,128)(2,1)S(1)} async-done(((bf16[4,8,49152]{2,1,0:T(8,128)(2,1)}), bf16[4,8,49152]{2,1,0:T(8,128)(2,1)S(1)}, u32[]{:S(2)}, u32[]{:S(2)}) %all-to-all-start) | async-done | bytes 3145760 | tf_op jit(solution)/shard_map/all_to_all | solution.py:208
  73.3 4.9 all-to-all-start.3
  78.2 4.1 copy.271
  83.8 3.7 all-to-all-start.1
  91.7 5.8 copy.292
  97.5 4.7 copy.277
  104.9 3.8 sort.32
  124.0 35.1 %all-to-all-done.1 = bf16[4,8,49152]{2,0,1:T(4,128)(2,1)S(1)} async-done(((bf16[4,8,49152]{2,0,1:T(4,128)(2,1)}), bf16[4,8,49152]{2,0,1:T(4,128)(2,1)S(1)}, u32[]{:S(2)}, u32[]{:S(2)}) %all-to-all-start.1) | async-done | bytes 3145760 | tf_op jit(solution)/shard_map/all_to_all | solution.py:207
  159.1 3.4 copy.272
  162.5 3.4 reshape.199
  165.9 3.8 gather_fusion.1
  169.8 3.2 copy.273
  173.0 5.6 reshape.200
  178.6 8.3 %copy.274 = bf16[8,4,128,64,6]{2,1,0,4,3:T(4,128)(2,1)S(1)} copy(bf16[8,4,128,64,6]{3,0,4,2,1:T(8,128)(2,1)} %bitcast.303) | data formatting | bytes 6291456 | tf_op jit(solution)/shard_map/transpose | solution.py:70
  186.9 3.4 copy.275
  196.3 5.7 multiply_bitcast_fusion.2
  202.0 6.7 %copy.291 = f32[32,128,384]{2,1,0:T(8,128)} copy(f32[32,128,384]{1,2,0:T(8,128)} %multiply_bitcast_fusion.2) | data formatting | bytes 12582912 | tf_op jit(solution)/shard_map/mul | solution.py:102
  208.7 3.6 multiply_bitcast_fusion.5
  212.3 5.6 copy.290
  217.9 15.9 %scatter_fusion = f32[20,128,384]{2,1,0:T(8,128)} fusion(f32[20,128,384]{2,1,0:T(8,128)} %copy.290, s32[32]{0:T(128)S(1)} %copy-done.20, f32[32,128,384]{2,1,0:T(8,128)} %copy.291), kind=kCustom, calls=%fused_computation.18 | custom fusion | flops 1572864 | bytes 18874496 | tf_op jit(solution)/shard_map/scatter-add | solution.py:102
  233.8 5.3 fusion.57
  239.1 4.3 gather_fusion.10
  243.4 5.2 multiply_bitcast_fusion.4
  248.6 4.6 multiply_bitcast_fusion.1
  253.2 6.6 %copy.299 = f32[32,128,384]{2,1,0:T(8,128)} copy(f32[32,128,384]{1,2,0:T(8,128)} %multiply_bitcast_fusion.1) | data formatting | bytes 12582912 | tf_op jit(solution)/shard_map/mul | solution.py:102
  259.8 5.6 copy.298
  265.3 15.9 %scatter_fusion.1 = f32[20,128,384]{2,1,0:T(8,128)} fusion(f32[20,128,384]{2,1,0:T(8,128)} %copy.298, s32[32]{0:T(128)S(1)} %copy-done.20, f32[32,128,384]{2,1,0:T(8,128)} %copy.299), kind=kCustom, calls=%fused_computation.19 | custom fusion | flops 1572864 | bytes 18874496 | tf_op jit(solution)/shard_map/scatter-add | solution.py:102
  281.2 6.8 %fusion.60 = (bf16[20,128,384]{2,1,0:T(8,128)(2,1)}, f32[20,128,384]{2,1,0:T(8,128)}) fusion(f32[20,128,384]{2,1,0:T(8,128)} %copy.292, f32[20,128,384]{2,1,0:T(8,128)} %scatter_fusion.1, f32[20,384]{1,0:T(8,128)S(1)} %copy.287, f32[20,128]{1,0:T(8,128)S(1)} %copy.293, f32[20,128,384]{2,1,0:T(8,128)} %scatter_fusion, bf16[20,128,384]{2,1,0:T(8,128)(2,1)S(1)} %gather_fusion.2), kind=kLoop, calls=%fused_computation.188 | loop fusion | flops 8847360 | bytes 19701760 | tf_op jit(solution)/shard_map/convert_element_type | solution.py:141
  288.0 4.5 gather_fusion.11
  292.5 3.6 multiply_bitcast_fusion.3
  296.1 4.6 multiply_bitcast_fusion
  300.7 6.6 %copy.305 = f32[32,128,384]{2,1,0:T(8,128)} copy(f32[32,128,384]{1,2,0:T(8,128)} %multiply_bitcast_fusion) | data formatting | bytes 12582912 | tf_op jit(solution)/shard_map/mul | solution.py:102
  307.3 5.6 copy.304
  312.8 15.9 %scatter_fusion.2 = f32[20,128,384]{2,1,0:T(8,128)} fusion(f32[20,128,384]{2,1,0:T(8,128)} %copy.304, s32[32]{0:T(128)S(1)} %copy-done.20, f32[32,128,384]{2,1,0:T(8,128)} %copy.305), kind=kCustom, calls=%fused_computation.20 | custom fusion | flops 1572864 | bytes 18874496 | tf_op jit(solution)/shard_map/scatter-add | solution.py:102
  328.7 6.4 %fusion.58 = (bf16[20,128,384]{2,1,0:T(8,128)(2,1)}, f32[20,128,384]{2,1,0:T(8,128)S(1)}) fusion(f32[20,128,384]{2,1,0:T(8,128)} %get-tuple-element.49, f32[20,384]{1,0:T(8,128)S(1)} %copy.287, f32[20,128]{1,0:T(8,128)S(1)} %copy.293, f32[20,128,384]{2,1,0:T(8,128)} %copy.292, f32[20,128,384]{2,1,0:T(8,128)} %scatter_fusion.2), kind=kLoop, calls=%fused_computation.187 | loop fusion | flops 4915200 | bytes 17735680 | tf_op jit(solution)/shard_map/convert_element_type | solution.py:155
  342.6 3.3 all-to-all-start.4
  346.3 4.5 scatter_fusion.3
  350.8 3.4 copy.317
  354.2 8.9 %copy.318 = bf16[8,64,4,128,6]{1,0,4,3,2:T(8,128)(2,1)} copy(bf16[8,64,4,128,6]{3,2,0,4,1:T(4,128)(2,1)} %bitcast.306) | data formatting | bytes 6291456 | tf_op jit(solution)/shard_map/transpose | solution.py:81
  363.1 9.3 %reshape.209 = bf16[512,3072]{0,1:T(8,128)(2,1)} reshape(bf16[8,64,4,128,6]{1,0,4,3,2:T(8,128)(2,1)} %copy.318) | data formatting | bytes 6291456 | tf_op jit(solution)/shard_map/reshape | solution.py:81
  375.6 3.8 gather_fusion.15
  379.4 4.8 reshape_reshape.12
  384.2 4.2 all-to-all-start.6
  389.0 35.0 %all-to-all-done.6 = bf16[4,8,49152]{2,1,0:T(8,128)(2,1)S(1)} async-done(((bf16[4,8,49152]{2,1,0:T(8,128)(2,1)}), bf16[4,8,49152]{2,1,0:T(8,128)(2,1)S(1)}, u32[]{:S(2)}, u32[]{:S(2)}) %all-to-all-start.6) | async-done | bytes 3145760 | tf_op jit(solution)/shard_map/all_to_all | solution.py:258
  424.0 3.3 all-to-all-start.5
  430.2 4.1 copy.320
  434.3 5.1 all-to-all-start.7
  445.2 14.8 %scatter_custom_fusion.5 = f32[128]{0:T(128)S(1)} fusion(s32[2048]{0:T(1024)} %bitcast.361, f32[2048]{0:T(1024)S(1)} %get-tuple-element.53, f32[]{:T(128)} %constant.19.clone.1), kind=kCustom, calls=%fused_computation.183 | custom fusion | flops 2048 | bytes 1024 | tf_op jit(solution)/shard_map/scatter-add | solution.py:52
  460.0 14.8 %scatter_custom_fusion.6 = f32[128]{0:T(128)S(1)} fusion(s32[2048]{0:T(1024)} %bitcast.362, f32[2048]{0:T(1024)S(1)} %get-tuple-element.55, f32[]{:T(128)} %constant.19.clone.1), kind=kCustom, calls=%fused_computation.181 | custom fusion | flops 2048 | bytes 1024 | tf_op jit(solution)/shard_map/scatter-add | solution.py:52
  474.8 14.8 %scatter_custom_fusion.7 = f32[128]{0:T(128)S(1)} fusion(s32[2048]{0:T(1024)} %bitcast.363, f32[2048]{0:T(1024)S(1)} %get-tuple-element.54, f32[]{:T(128)} %constant.19.clone.1), kind=kCustom, calls=%fused_computation.179 | custom fusion | flops 2048 | bytes 1024 | tf_op jit(solution)/shard_map/scatter-add | solution.py:52
  491.2 40.0 %psum.7 = f32[]{:T(128)} all-reduce(f32[]{:T(128)} %get-tuple-element.46), channel_id=1, replica_groups=mesh['sec'=4,'bulk'=8] {'sec','bulk'}, use_global_device_ids=true, to_apply=%region_32.33 | all-reduce | flops 1 | bytes 8 | tf_op jit(solution)/shard_map/psum | solution.py:279
  531.2 8.3 %gather_fusion.14 = f32[2048,3]{1,0:T(8,128)} fusion(f32[3,128]{0,1:T(8,128)S(1)} %get-tuple-element.47, s32[2048]{0:T(1024)} %copy-done.13), kind=kCustom, calls=%fused_computation.14 | custom fusion | bytes 57344 | tf_op jit(solution)/shard_map/gather | solution.py:282
  545.5 14.8 %scatter_custom_fusion.8 = f32[128]{0:T(128)S(1)} fusion(s32[2048]{0:T(1024)} %bitcast.364, f32[2048]{0:T(1024)S(1)} %get-tuple-element.50, f32[]{:T(128)} %constant.19.clone.1), kind=kCustom, calls=%fused_computation.177 | custom fusion | flops 2048 | bytes 1024 | tf_op jit(solution)/shard_map/scatter-add | solution.py:52
  560.3 15.1 %scatter_custom_fusion.9 = f32[128]{0:T(128)S(1)} fusion(s32[2048]{0:T(1024)} %bitcast.365, f32[2048]{0:T(1024)S(1)} %get-tuple-element.52, f32[]{:T(128)} %constant.19.clone.1), kind=kCustom, calls=%fused_computation.175 | custom fusion | flops 2048 | bytes 1024 | tf_op jit(solution)/shard_map/scatter-add | solution.py:52
  575.3 14.8 %scatter_custom_fusion.10 = f32[128]{0:T(128)S(1)} fusion(s32[2048]{0:T(1024)} %bitcast.366, f32[2048]{0:T(1024)S(1)} %get-tuple-element.51, f32[]{:T(128)} %constant.19.clone.1), kind=kCustom, calls=%fused_computation.173 | custom fusion | flops 2048 | bytes 1024 | tf_op jit(solution)/shard_map/scatter-add | solution.py:52
  590.7 3.4 copy.321
  594.1 4.8 reshape.210
  599.0 9.5 %gather_fusion.16 = bf16[512,3072]{1,0:T(8,128)(2,1)} fusion(bf16[512,3072]{1,0:T(8,128)(2,1)} %reshape.210, s32[1024]{0:T(1024)S(1)} %copy-done.16), kind=kCustom, calls=%fused_computation.16 | custom fusion | bytes 6293504 | tf_op jit(solution)/shard_map/gather | solution.py:272
  (207 shorter events, 63.7 us)
Async XLA Ops:
  0.6 24.3 %copy-start = (bf16[512,3072]{1,0:T(8,128)(2,1)S(1)}, bf16[512,3072]{1,0:T(8,128)(2,1)}, u32[]{:S(2)}) copy-start(bf16[512,3072]{1,0:T(8,128)(2,1)} %param.33) | copy-start | bytes 9437188
  1.6 10.8 %copy-start.10 = (f32[4,1,512]{2,1,0:T(1,128)}, f32[4,1,512]{2,1,0:T(1,128)S(1)}, u32[]{:S(2)}) copy-start(f32[4,1,512]{2,1,0:T(1,128)S(1)} %get-tuple-element.58) | copy-start | bytes 24580
  2.3 10.0 %copy-start.13 = (s32[2048]{0:T(1024)}, s32[2048]{0:T(1024)S(1)}, u32[]{:S(2)}) copy-start(s32[2048]{0:T(1024)S(1)} %broadcast_clamp_fusion) | copy-start | bytes 24580
  12.4 4.7 copy-start.11
  17.1 0.6 copy-start.21
  19.7 13.8 %all-to-all-start.2 = ((bf16[4,8,96]{2,1,0:T(8,128)(2,1)}), bf16[4,8,96]{2,1,0:T(8,128)(2,1)S(1)}, u32[]{:S(2)}, u32[]{:S(2)}) async-start(bf16[4,8,96]{2,1,0:T(8,128)(2,1)} %convert_element_type.67), calls=%async_computation.2 | async-start | bytes 16384 | tf_op jit(solution)/shard_map/all_to_all | solution.py:195
  33.5 39.8 %all-to-all-start = ((bf16[4,8,49152]{2,1,0:T(8,128)(2,1)}), bf16[4,8,49152]{2,1,0:T(8,128)(2,1)S(1)}, u32[]{:S(2)}, u32[]{:S(2)}) async-start(bf16[4,8,49152]{2,1,0:T(8,128)(2,1)} %reshape_reshape.10), calls=%async_computation | async-start | bytes 6291456 | tf_op jit(solution)/shard_map/all_to_all | solution.py:208
  73.3 10.5 %all-to-all-start.3 = ((bf16[4,8,96]{2,0,1:T(4,128)(2,1)}), bf16[4,8,96]{2,0,1:T(4,128)(2,1)S(1)}, u32[]{:S(2)}, u32[]{:S(2)}) async-start(bf16[4,8,96]{2,0,1:T(4,128)(2,1)} %copy.284), calls=%async_computation.3 | async-start | bytes 16384 | tf_op jit(solution)/shard_map/all_to_all | solution.py:194
  82.3 5.3 copy-start.30
  82.3 5.6 copy-start.23
  82.3 6.4 %copy-start.24 = (f32[20,1,6]{0,1,2:T(1,128)S(1)}, f32[20,1,6]{0,1,2:T(1,128)}, u32[]{:S(2)}) copy-start(f32[20,1,6]{0,1,2:T(1,128)} %param.27) | copy-start | bytes 1444
  82.3 7.0 %copy-start.9 = (f32[20,1,6,128]{3,1,2,0:T(1,128)S(1)}, f32[20,1,6,128]{3,1,2,0:T(1,128)}, u32[]{:S(2)}) copy-start(f32[20,1,6,128]{3,1,2,0:T(1,128)} %param.25) | copy-start | bytes 184324
  83.8 75.3 %all-to-all-start.1 = ((bf16[4,8,49152]{2,0,1:T(4,128)(2,1)}), bf16[4,8,49152]{2,0,1:T(4,128)(2,1)S(1)}, u32[]{:S(2)}, u32[]{:S(2)}) async-start(bf16[4,8,49152]{2,0,1:T(4,128)(2,1)} %copy.271), calls=%async_computation.1 | async-start | bytes 6291456 | tf_op jit(solution)/shard_map/all_to_all | solution.py:207
  97.5 6.7 %copy-start.22 = (f32[1,8,36]{2,1,0:T(8,128)S(1)}, f32[1,8,36]{2,1,0:T(8,128)}, u32[]{:S(2)}) copy-start(f32[1,8,36]{2,1,0:T(8,128)} %param.24) | copy-start | bytes 3460
  97.5 13.9 %copy-start.28 = (s32[32,1]{0,1:T(1,128)S(1)}, s32[32,1]{0,1:T(1,128)}, u32[]{:S(2)}) copy-start(s32[32,1]{0,1:T(1,128)} %param.29) | copy-start | bytes 388
  97.5 15.5 %copy-start.29 = (s32[32,1]{0,1:T(1,128)S(1)}, s32[32,1]{0,1:T(1,128)}, u32[]{:S(2)}) copy-start(s32[32,1]{0,1:T(1,128)} %param.30) | copy-start | bytes 388
  111.3 0.8 copy-start.19
  112.2 7.1 %copy-start.17 = (s32[1024]{0:T(1024)}, s32[1024]{0:T(1024)S(1)}, u32[]{:S(2)}) copy-start(s32[1024]{0:T(1024)S(1)} %pad_clamp_fusion.6) | copy-start | bytes 12292
  112.3 1.2 copy-start.25
  162.5 3.4 copy-start.18
  193.4 2.9 copy-start.6
  202.0 6.7 %copy-start.5 = (bf16[20,1,128,128]{3,2,1,0:T(8,128)(2,1)S(1)}, bf16[20,1,128,128]{3,2,1,0:T(8,128)(2,1)}, u32[]{:S(2)}) copy-start(bf16[20,1,128,128]{3,2,1,0:T(8,128)(2,1)} %param.26) | copy-start | bytes 1966084
  212.3 5.6 copy-start.20
  243.4 5.2 copy-start.4
  243.4 5.2 copy-start.7
  288.0 4.5 copy-start.2
  292.5 3.6 copy-start.3
  292.5 3.6 copy-start.8
  335.1 2.6 copy-start.31
  335.2 4.4 copy-start.12
  339.8 6.6 %copy-start.26 = (s32[20]{0:T(128)S(1)}, s32[20]{0:T(128)}, u32[]{:S(2)}) copy-start(s32[20]{0:T(128)} %copy-done.25) | copy-start | bytes 244
  342.6 41.6 %all-to-all-start.4 = ((bf16[4,8,576]{2,1,0:T(8,128)(2,1)}), bf16[4,8,576]{2,1,0:T(8,128)(2,1)S(1)}, u32[]{:S(2)}, u32[]{:S(2)}) async-start(bf16[4,8,576]{2,1,0:T(8,128)(2,1)} %reshape_reshape.11), calls=%async_computation.4 | async-start | bytes 81920 | tf_op jit(solution)/shard_map/all_to_all | solution.py:245
  384.2 39.8 %all-to-all-start.6 = ((bf16[4,8,49152]{2,1,0:T(8,128)(2,1)}), bf16[4,8,49152]{2,1,0:T(8,128)(2,1)S(1)}, u32[]{:S(2)}, u32[]{:S(2)}) async-start(bf16[4,8,49152]{2,1,0:T(8,128)(2,1)} %reshape_reshape.12), calls=%async_computation.6 | async-start | bytes 6291456 | tf_op jit(solution)/shard_map/all_to_all | solution.py:258
  424.0 10.2 %all-to-all-start.5 = ((bf16[4,8,576]{2,0,1:T(4,128)(2,1)}), bf16[4,8,576]{2,0,1:T(4,128)(2,1)S(1)}, u32[]{:S(2)}, u32[]{:S(2)}) async-start(bf16[4,8,576]{2,0,1:T(4,128)(2,1)} %copy.311), calls=%async_computation.5 | async-start | bytes 81920 | tf_op jit(solution)/shard_map/all_to_all | solution.py:244
  434.3 5.2 copy-start.14
  434.3 5.8 copy-start.27
  434.3 156.5 %all-to-all-start.7 = ((bf16[4,8,49152]{2,0,1:T(4,128)(2,1)}), bf16[4,8,49152]{2,0,1:T(4,128)(2,1)S(1)}, u32[]{:S(2)}, u32[]{:S(2)}) async-start(bf16[4,8,49152]{2,0,1:T(4,128)(2,1)} %copy.320), calls=%async_computation.7 | async-start | bytes 6291456 | tf_op jit(solution)/shard_map/all_to_all | solution.py:257
  440.8 0.6 copy-start.15
  594.1 4.8 copy-start.16
  599.0 9.5 %copy-start.1 = (bf16[512,3072]{1,0:T(8,128)(2,1)S(1)}, bf16[512,3072]{1,0:T(8,128)(2,1)}, u32[]{:S(2)}) copy-start(bf16[512,3072]{1,0:T(8,128)(2,1)} %param.33) | copy-start | bytes 9437188
where the time goes:
time: 620 us; the launch traced here: 609 us
  local copies, waits for them, and re-layouts  219 us (35%)
  other arithmetic  175 us (28%)
  waiting for transfers between devices  107 us (17%)
  blocking collectives  40 us (6%)
  starting transfers between devices  33.9 us (5%)
  matrix products  31 us (5%)
    scatter-add x6, other arithmetic, assemble(): jax.ops.segment_sum(forces[component].reshape(-1), flat_ids, num_segments...  89.1 us
    scatter-add x3, other arithmetic, contact_terms(): result = applied.at[off_rows].add(contrib * off_scale_cols[:, None, :])  47.7 us
    psum x1, blocking collectives, on_device(): norm_sq = lax.psum(jnp.sum(residual * residual), ('sec', 'bulk'))  40 us
    all_to_all x1, waiting for transfers between devices, on_device(): lax.all_to_all(lax.all_to_all(state_send.reshape(sections, owners, -1), '...  35.1 us
    all_to_all x1, waiting for transfers between devices, on_device(): lax.all_to_all(state_back.reshape(sections, owners, -1), 'sec', split_axi...  35 us
    all_to_all x1, waiting for transfers between devices, on_device(): lax.all_to_all(state_send.reshape(sections, owners, -1), 'sec', split_axi...  35 us
    mul x5, local copies, waits for them, and re-layouts, contact_terms(): result = applied.at[off_rows].add(contrib * off_scale_cols[:, None, :])  21.6 us
    mul x5, local copies, waits for them, and re-layouts, micro_solve(): jnp.einsum('rab,rbc->rac', diag_blk, fluct_low, preferred_element_type=jn...  18.4 us
  transfers between devices with their start and end apart: 8, of which 4 were waited for; matrix products, arithmetic and copies ran while one was open for 34% of the time, Pallas kernels for 0%

commit v1 on v0

v1 whole, which is shorter than its diff:
```python
import functools

import jax
import jax.numpy as jnp
from jax import lax
from jax.experimental import pallas as pl
from jax.experimental.pallas import tpu as pltpu
from jax.sharding import Mesh, PartitionSpec as P

BS = 128
NBMAX = 4
VOL_GRP = 8
GPV_DEV = 64
SWEEPS = 3
ROWS_GRP = 20
HALF_ROWS = 10
OFF_GRP = 32
HALF_OFF = 16
COMPS = 6
LEVEL = BS * COMPS
UNIT = 8
TILE = 16
SLOTS = UNIT * TILE
STATE_LANES = 5 * LEVEL
MSG_LANES = STATE_LANES + 128
GAIN_NORMAL = 0.4
CLIP_RMS = 1.0
SM_DIAG_NORMAL = 80
SM_OFF_NORMAL = 96
SM_AFFINE = 128
SM_ROWS = 136

F32 = jnp.float32
BF16 = jnp.bfloat16
I32 = jnp.int32
AXES = ("y", "x", "h", "l", "c")
GROUP_AXES = ("h", "l", "c")
UNIT_AXES = ("x", "l", "c")
VMEM_LIMIT = 56 * 1024 * 1024

CLASS_PLACE = ((4 * LEVEL, 0), (3 * LEVEL, TILE), (0, TILE), (0, 0))
CLASS_BASE = (0, 1, 3, 6)


def dot_nn(lhs, rhs):
    return lax.dot_general(lhs, rhs, (((1,), (0,)), ((), ())), preferred_element_type=F32)


def dot_nt(lhs, rhs):
    return lax.dot_general(lhs, rhs, (((1,), (1,)), ((), ())), preferred_element_type=F32)


def dot_tn(lhs, rhs):
    return lax.dot_general(lhs, rhs, (((0,), (0,)), ((), ())), preferred_element_type=F32)


def split3(value):
    high = value.astype(BF16)
    rest = value - high.astype(F32)
    mid = rest.astype(BF16)
    low = (rest - mid.astype(F32)).astype(BF16)
    return high, mid, low


def iota(shape, dim):
    return lax.broadcasted_iota(I32, shape, dim)


def lane_order():
    target = iota((1, LEVEL), 1)
    source = COMPS * (target % BS) + target // BS
    return jnp.where(iota((LEVEL, LEVEL), 0) == source, 1.0, 0.0).astype(BF16)


def class_onehot(slot, size, level_rows):
    chosen = jnp.where(size == level_rows, slot, -1)
    return jnp.where(iota((SLOTS, slot.shape[1]), 0) == chosen, 1.0, 0.0).astype(BF16)


def node_onehot(conn_row, nodes):
    return jnp.where(iota((nodes, conn_row.shape[1]), 0) == conn_row, 1.0, 0.0).astype(BF16)


def nodal_parts(nodal):
    parts = [jnp.concatenate([p.astype(F32), jnp.zeros((13, p.shape[1]), F32)], axis=0) for p in split3(nodal)]
    rows = parts[0] + pltpu.roll(parts[1], 3, 0) + pltpu.roll(parts[2], 6, 0)
    return rows.astype(BF16)


def gather_nodes(rows, onehots):
    found = []
    for onehot in onehots:
        got = dot_nn(rows, onehot)
        found.append([got[i : i + 1] + got[i + 3 : i + 4] + got[i + 6 : i + 7] for i in range(3)])
    return found


def strain_rows(grads, disp):
    g = lambda a, k: grads[3 * a + k : 3 * a + k + 1]
    total = lambda f: f(0) + f(1) + f(2) + f(3)
    return [
        total(lambda a: g(a, 0) * disp[a][0]),
        total(lambda a: g(a, 1) * disp[a][1]),
        total(lambda a: g(a, 2) * disp[a][2]),
        total(lambda a: g(a, 2) * disp[a][1] + g(a, 1) * disp[a][2]),
        total(lambda a: g(a, 2) * disp[a][0] + g(a, 0) * disp[a][2]),
        total(lambda a: g(a, 1) * disp[a][0] + g(a, 0) * disp[a][1]),
    ]


def matrix_pack_kernel(
    ids, vol, off_row, off_col, off_count, coupling, diag_normal, off_normal, affine, diag, off,
    blocks, small, ints, row_local, row_size, rows_sel, seen, sems,
):
    half = ids[0]
    small[...] = jnp.zeros_like(small)
    for size in range(NBMAX + 1):
        seen[size] = 0
    start = 0
    for v in range(VOL_GRP):
        size = vol[0, v]
        rank = seen[size]
        seen[size] = rank + 1
        mine = rank == half
        base = (size * (size - 1)) // 2
        for a in range(NBMAX):
            @pl.when(a < size)
            def _(a=a, size=size, base=base, mine=mine, start=start):
                row_local[start + a] = jnp.where(mine, base + a, -1)
                row_size[start + a] = size - 1

            @pl.when(jnp.logical_and(a < size, mine))
            def _(a=a, base=base, start=start):
                rows_sel[base + a] = start + a

        @pl.when(mine)
        def _(size=size, v=v):
            small[pl.ds(SM_AFFINE - 1 + size, 1), 0:36] = affine[v : v + 1, :]

        start = start + size
    copies = [
        pltpu.make_async_copy(
            off.at[pl.ds(half * HALF_OFF, HALF_OFF)], blocks.at[pl.ds(HALF_ROWS, HALF_OFF)], sems.at[HALF_ROWS]
        )
    ]
    for i in range(HALF_ROWS):
        copies.append(
            pltpu.make_async_copy(diag.at[pl.ds(rows_sel[i], 1)], blocks.at[pl.ds(i, 1)], sems.at[i])
        )
    for copy in copies:
        copy.start()
    for i in range(HALF_ROWS):
        row = rows_sel[i]
        small[8 * i : 8 * i + COMPS, :] = coupling[row]
        small[SM_DIAG_NORMAL + i : SM_DIAG_NORMAL + i + 1, 0:COMPS] = diag_normal[pl.ds(row, 1), :]

    @pl.when(half == 0)
    def _():
        small[SM_OFF_NORMAL : SM_OFF_NORMAL + OFF_GRP, 0:COMPS] = off_normal[...]

    @pl.when(half != 0)
    def _():
        small[SM_OFF_NORMAL : SM_OFF_NORMAL + HALF_OFF, 0:COMPS] = off_normal[HALF_OFF:, :]
        small[SM_OFF_NORMAL + HALF_OFF : SM_OFF_NORMAL + OFF_GRP, 0:COMPS] = off_normal[:HALF_OFF, :]

    live_total = off_count[0]

    def contact(n, found):
        slot = (n + half * HALF_OFF) % OFF_GRP
        row = off_row[slot, 0]
        local = row_local[row]
        ints[5, n] = row_size[row]
        live = jnp.logical_and(slot < live_total, local >= 0)

        @pl.when(live)
        def _():
            ints[1, found] = n
            ints[2, found] = local
            ints[3, found] = row_local[off_col[slot, 0]]

        return found + live.astype(I32)

    ints[0, 0] = lax.fori_loop(0, OFF_GRP, contact, 0)
    for copy in copies:
        copy.wait()


def pack_kernel(groups, rounds, ids, point_map, table, disp, conn, grads, state, *refs):
    outs, (strain_out, place_out, state_vmem, sem) = refs[:UNIT], refs[UNIT:]
    load = pltpu.make_async_copy(state, state_vmem, sem)
    load.start()
    elems = point_map.shape[1]
    x_me, h_me, l_me, c_me = ids[1], ids[2], ids[3], ids[4]
    z_count = groups // 4
    codes = point_map[...]
    owner = codes // elems
    within = codes % elems
    group = owner % groups
    volume = within // GPV_DEV
    delta = (group // 4 - h_me + z_count) % z_count
    core = group % 2
    low = (group // 2) % 2
    across = (delta % 2) ^ core
    turn = delta // 2
    offset = ((across ^ x_me) * 4) + ((low ^ l_me) * 2) + (core ^ c_me)
    group_hot = jnp.where(iota((groups, elems), 0) == group, 1.0, 0.0).astype(BF16)
    sizes = dot_tn(table[...].astype(F32).astype(BF16), group_hot)
    size = jnp.sum(
        jnp.where(iota((VOL_GRP, elems), 0) == volume, sizes, 0.0), axis=0, keepdims=True
    ).astype(I32)
    key = (offset * NBMAX + size - 1) * rounds + turn
    key_hot = iota((UNIT * NBMAX * rounds, elems), 0) == key
    earlier = jnp.where(iota((elems, elems), 0) < iota((elems, elems), 1), 1.0, 0.0).astype(BF16)
    counts = dot_nn(jnp.where(key_hot, 1.0, 0.0).astype(BF16), earlier)
    rank = jnp.sum(jnp.where(key_hot, counts, 0.0), axis=0, keepdims=True).astype(I32)
    slot = offset * TILE + turn * (TILE // rounds) + rank
    place_out[...] = jnp.concatenate([slot, size, jnp.zeros((6, elems), I32)], axis=0)

    nodes = disp.shape[1]
    onehots = [node_onehot(conn[a : a + 1, :], nodes) for a in range(4)]
    found = gather_nodes(nodal_parts(disp[...]), onehots)
    strain = strain_rows(grads[...], found)
    strain8 = jnp.concatenate(strain + [jnp.zeros((2, elems), F32)], axis=0)
    strain_out[...] = strain8
    first = jnp.concatenate([strain8, jnp.zeros((120, elems), F32)], axis=0).astype(BF16)
    second = jnp.concatenate(
        [jnp.zeros((64, elems), F32), strain8, jnp.zeros((56, elems), F32)], axis=0
    ).astype(BF16)
    hots = [class_onehot(slot, size, c + 1) for c in range(NBMAX)]
    for one, other, row0 in ((3, 0, 0), (2, 1, TILE)):
        extras = (dot_nt(hots[one], first) + dot_nt(hots[other], second)).astype(BF16)
        for k in range(UNIT):
            outs[k][row0 : row0 + TILE, STATE_LANES:] = extras[TILE * k : TILE * (k + 1)]
    order = lane_order()
    load.wait()
    for c in range(NBMAX):
        lane0, row0 = CLASS_PLACE[c]
        for a in range(c + 1):
            rows = dot_nn(hots[c], state_vmem[:, LEVEL * a : LEVEL * (a + 1)]).astype(BF16)
            rows = dot_nn(rows, order).astype(BF16)
            for k in range(UNIT):
                outs[k][row0 : row0 + TILE, lane0 + LEVEL * a : lane0 + LEVEL * (a + 1)] = rows[
                    TILE * k : TILE * (k + 1)
                ]


def solve_kernel(ids, ints, small, blocks, other, *refs):
    msgs, refs = refs[:UNIT], refs[UNIT:]
    outs, refs = refs[:UNIT], refs[UNIT:]
    tangents, state, low, acc, contact_scale, diag_scale, inverse, response, diag_pairs, off_pairs = refs
    for c in range(NBMAX):
        lane0, row0 = CLASS_PLACE[c]
        for a in range(c + 1):
            r = CLASS_BASE[c] + a
            for j in range(COMPS):
                lane = lane0 + LEVEL * a + BS * j
                for k in range(UNIT):
                    piece = msgs[k][row0 : row0 + TILE, lane : lane + BS]
                    dst = slice(SLOTS * j + TILE * k, SLOTS * j + TILE * (k + 1))
                    low[r, dst, :] = piece
                    state[r, dst, :] = piece.astype(F32)
    normals = small[SM_DIAG_NORMAL : SM_OFF_NORMAL + OFF_GRP, :]
    shifted = pltpu.roll(normals, 64, 1)
    for rows, one, two in ((0, 3, 0), (TILE, 2, 1)):
        strains = jnp.concatenate([msgs[k][rows : rows + TILE, STATE_LANES:] for k in range(UNIT)], axis=0)
        for cls, vectors in ((one, normals), (two, shifted)):
            high, mid, lowest = split3(vectors)
            dots = dot_nt(strains, high) + dot_nt(strains, mid) + dot_nt(strains, lowest)
            response[cls, :, 0 : dots.shape[1]] = 1.0 + GAIN_NORMAL * jnp.tanh(dots)
    eye = iota((BS, BS), 0) == iota((BS, BS), 1)
    for c in range(NBMAX):
        for a in range(c + 1):
            r = CLASS_BASE[c] + a
            scale = jnp.broadcast_to(response[c, :, r : r + 1], (SLOTS, BS))
            diag_scale[r] = scale
            values = jnp.sum(jnp.where(eye, blocks[r].astype(F32), 0.0), axis=0, keepdims=True)
            inverse[r] = 1.0 / (scale * values)
    for n in range(OFF_GRP):
        contact_scale[n] = jnp.broadcast_to(
            response[ints[5, n], :, HALF_OFF + n : HALF_OFF + n + 1], (SLOTS, BS)
        )
    zero = jnp.zeros((BS, BS), BF16)
    for p in range(HALF_ROWS // 2):
        diag_pairs[p, :BS, :BS] = blocks[2 * p]
        diag_pairs[p, :BS, BS:] = zero
        diag_pairs[p, BS:, :BS] = zero
        diag_pairs[p, BS:, BS:] = blocks[2 * p + 1]
    live = ints[0, 0]
    pairs = (live + 1) // 2

    def contact_block(n):
        mine = n < HALF_OFF
        own = blocks[HALF_ROWS + jnp.where(mine, n, 0)]
        theirs = other[jnp.where(mine, 0, n - HALF_OFF)]
        return jnp.where(mine, own, theirs)

    def fill(p, carry):
        off_pairs[p, :BS, :BS] = contact_block(ints[1, 2 * p])
        off_pairs[p, :BS, BS:] = zero
        off_pairs[p, BS:, :BS] = zero
        has_second = 2 * p + 1 < live

        @pl.when(has_second)
        def _():
            off_pairs[p, BS:, BS:] = contact_block(ints[1, 2 * p + 1])

        @pl.when(jnp.logical_not(has_second))
        def _():
            off_pairs[p, BS:, BS:] = zero

        return carry

    lax.fori_loop(0, pairs, fill, 0)

    def sweep(step, carry):
        for p in range(HALF_ROWS // 2):
            both = jnp.concatenate([low[2 * p], low[2 * p + 1]], axis=1)
            product = dot_nt(both, diag_pairs[p])
            for i in range(2):
                r = 2 * p + i
                scale = diag_scale[r]
                for j in range(COMPS):
                    rows = slice(SLOTS * j, SLOTS * (j + 1))
                    acc[r, rows, :] = product[rows, BS * i : BS * (i + 1)] * scale

        def contact(p, inner):
            second = jnp.minimum(2 * p + 1, live - 1)
            slots = (2 * p, second)
            both = jnp.concatenate([low[ints[3, m]] for m in slots], axis=1)
            product = dot_nt(both, off_pairs[p])
            for i, m in enumerate(slots):
                r = ints[2, m]
                scale = contact_scale[ints[1, m]]
                for j in range(COMPS):
                    rows = slice(SLOTS * j, SLOTS * (j + 1))
                    acc[r, rows, :] += product[rows, BS * i : BS * (i + 1)] * scale
            return inner

        lax.fori_loop(0, pairs, contact, 0)
        for r in range(HALF_ROWS):
            inv = inverse[r]
            for j in range(COMPS):
                rows = slice(SLOTS * j, SLOTS * (j + 1))
                load = small[8 * r + j : 8 * r + j + 1, :]
                value = state[r, rows, :] + (load - acc[r, rows, :]) * inv
                state[r, rows, :] = value
                low[r, rows, :] = value.astype(BF16)
        return carry

    lax.fori_loop(0, SWEEPS, sweep, 0)
    lane = iota((1, BS), 1)
    comp = lane // 8
    for c in range(NBMAX):
        total = jnp.zeros((SLOTS, BS), F32)
        for a in range(c + 1):
            r = CLASS_BASE[c] + a
            load8 = small[8 * r : 8 * r + 8, :]
            tiled = jnp.concatenate([load8] * 6 + [jnp.zeros((80, BS), F32)], axis=0)
            weights = jnp.concatenate(split3(tiled)[:2], axis=0)
            value = state[r]
            high = value.astype(BF16)
            rest = (value - high.astype(F32)).astype(BF16)
            product = dot_nt(high, weights) + dot_nt(rest, weights)
            product = product[:, :BS] + product[:, BS:]
            for j in range(COMPS):
                total += jnp.where(comp == j, product[SLOTS * j : SLOTS * (j + 1)], 0.0)
        source = iota((BS, BS), 0)
        target = iota((BS, BS), 1)
        wanted = jnp.logical_and(
            source == 6 * (target % 8) + target // 8, jnp.logical_and(target % 8 < 6, target < 48)
        )
        moved = jnp.sum(
            jnp.where(wanted, jnp.transpose(jnp.broadcast_to(small[SM_AFFINE + c : SM_AFFINE + c + 1, :], (BS, BS))), 0.0),
            axis=0,
            keepdims=True,
        )
        acc[c, :SLOTS, :] = moved - total / ((c + 1) * BS)
    for row0, one, two in ((0, 3, 0), (TILE, 2, 1)):
        first = acc[one, :SLOTS, :]
        second = acc[two, :SLOTS, :]
        packed = jnp.where(lane < 64, first, pltpu.roll(second, 64, 1)).astype(BF16)
        for k in range(UNIT):
            tangents[ids[5] ^ k, row0 : row0 + TILE, :] = packed[TILE * k : TILE * (k + 1)]
    for c in range(NBMAX):
        lane0, row0 = CLASS_PLACE[c]
        for a in range(c + 1):
            r = CLASS_BASE[c] + a
            for j in range(COMPS):
                lane_at = lane0 + LEVEL * a + BS * j
                for k in range(UNIT):
                    outs[k][row0 : row0 + TILE, lane_at : lane_at + BS] = low[
                        r, SLOTS * j + TILE * k : SLOTS * j + TILE * (k + 1), :
                    ]


def fem_kernel(ids, tangents, place, strain, grads, volume, conn, nodal_load, residual, product, norm):
    elems = place.shape[1]
    nodes = nodal_load.shape[1]
    slot, size = place[0:1, :], place[1:2, :]
    hots = [class_onehot(slot, size, c + 1) for c in range(NBMAX)]
    entries = jnp.zeros((64, elems), F32)
    for row0, one, two in ((0, 3, 0), (TILE, 2, 1)):
        packed = jnp.concatenate([tangents[ids[5] ^ k, row0 : row0 + TILE, :] for k in range(UNIT)], axis=0)
        entries += dot_tn(packed, hots[one])[:64]
        entries += dot_tn(packed, hots[two])[64:]
    entry = lambda i, j: entries[8 * j + i : 8 * j + i + 1]
    weight = volume[...]
    g_all = grads[...]
    g = lambda a, k: g_all[3 * a + k : 3 * a + k + 1]
    onehots = [node_onehot(conn[a : a + 1, :], nodes) for a in range(4)]

    def assemble(strains):
        s = []
        for i in range(COMPS):
            total = entry(i, 0) * strains[0]
            for j in range(1, COMPS):
                total = total + entry(i, j) * strains[j]
            s.append(total * weight)
        result = jnp.zeros((TILE, nodes), F32)
        for a in range(4):
            force = jnp.concatenate(
                [
                    g(a, 0) * s[0] + g(a, 2) * s[4] + g(a, 1) * s[5],
                    g(a, 1) * s[1] + g(a, 2) * s[3] + g(a, 0) * s[5],
                    g(a, 2) * s[2] + g(a, 1) * s[3] + g(a, 0) * s[4],
                ],
                axis=0,
            )
            result += dot_nt(nodal_parts(force), onehots[a])
        return result[0:3] + result[3:6] + result[6:9]

    strains = strain[...]
    res = assemble([strains[i : i + 1] for i in range(COMPS)]) - nodal_load[...]
    residual[...] = res
    norm[...] = jnp.broadcast_to(jnp.sum(res * res, keepdims=True), norm.shape)
    trial = strain_rows(g_all, gather_nodes(nodal_parts(res), onehots))
    product[...] = assemble(trial)


def unpack_kernel(place, *refs):
    msgs, (out, out_vmem, sems) = refs[:UNIT], refs[UNIT:]
    slot, size = place[0:1, :], place[1:2, :]
    order = lane_order()
    hots = [class_onehot(slot, size, c + 1) for c in range(NBMAX)]
    copies = []
    for a in range(NBMAX):
        pieces = []
        for c in range(a, NBMAX):
            lane0, row0 = CLASS_PLACE[c]
            lane = lane0 + LEVEL * a
            rows = jnp.concatenate([msgs[k][row0 : row0 + TILE, lane : lane + LEVEL] for k in range(UNIT)], axis=0)
            pieces.append(dot_nt(rows, order).astype(BF16))
        hot = jnp.concatenate(hots[a:], axis=0)
        out_vmem[a] = dot_tn(hot, jnp.concatenate(pieces, axis=0)).astype(BF16)
        copy = pltpu.make_async_copy(out_vmem.at[a], out.at[:, pl.ds(LEVEL * a, LEVEL)], sems.at[a])
        copy.start()
        copies.append(copy)
    for copy in copies:
        copy.wait()


def spec(space):
    return pl.BlockSpec(memory_space=space)


VM, SM, HB = pltpu.VMEM, pltpu.SMEM, pl.ANY


def call(kernel, args, spaces, outs, out_spaces, scratch):
    return pl.pallas_call(
        kernel,
        out_shape=[jax.ShapeDtypeStruct(s, d) for s, d in outs],
        in_specs=[spec(s) for s in spaces],
        out_specs=[spec(s) for s in out_spaces],
        scratch_shapes=scratch,
        compiler_params=pltpu.CompilerParams(vmem_limit_bytes=VMEM_LIMIT),
    )(*args)


def on_device(
    shape,
    displacement, nodal_load, connectivity, shape_grads, elem_volume, point_map, vol_blocks, c_affine,
    coupling, diag_blocks, diag_normal, off_blocks, off_row, off_col, off_normal, off_count, fluct_state,
):
    z_count = shape[2]
    groups = z_count * 4
    rounds = z_count // 2
    devices = 4 * groups
    elems = connectivity.shape[1]
    node_count = displacement.shape[1]
    index = {name: lax.axis_index(name) for name in AXES}
    unit_index = index["x"] * 4 + index["l"] * 2 + index["c"]
    ids = jnp.stack(
        [index["y"], index["x"], index["h"], index["l"], index["c"], unit_index, unit_index, unit_index]
    ).astype(I32)

    def coords(device):
        section, group = divmod(device, groups)
        return section // 2, section % 2, group // 4, (group // 2) % 2, group % 2

    def number(y, x, h, l, c):
        return (y * 2 + x) * groups + h * 4 + l * 2 + c

    def permute(value, source_of):
        pairs = [(number(*source_of(*coords(d))), d) for d in range(devices)]
        return lax.ppermute(value, AXES, pairs)

    def unit_permute(value, k):
        return permute(value, lambda y, x, h, l, c: (y, x ^ (k >> 2), h, l ^ ((k >> 1) & 1), c ^ (k & 1)))

    blocks, small, ints = call(
        matrix_pack_kernel,
        (
            ids, vol_blocks, off_row, off_col, off_count, coupling[:, 0], diag_normal[:, 0], off_normal[:, 0],
            c_affine[0], diag_blocks[:, 0], off_blocks[:, 0],
        ),
        (SM, SM, SM, SM, SM, VM, VM, VM, VM, HB, HB),
        (((HALF_ROWS + HALF_OFF, BS, BS), BF16), ((SM_ROWS, BS), F32), ((8, BS), I32)),
        (HB, VM, SM),
        [
            pltpu.SMEM((32,), I32), pltpu.SMEM((32,), I32), pltpu.SMEM((16,), I32), pltpu.SMEM((8,), I32),
            pltpu.SemaphoreType.DMA((HALF_ROWS + 1,)),
        ],
    )
    held = []
    for turn in range(rounds):
        def from_group(y, x, h, l, c, turn=turn):
            return y, x, (h + 2 * turn + (x ^ c)) % z_count, l, c

        mine = [permute(value, from_group) for value in (blocks, small, ints)]
        theirs = permute(mine[0][HALF_ROWS:], lambda y, x, h, l, c: (1 - y, x, h, l, c))
        held.append((mine[2], mine[1], mine[0], theirs))

    table = lax.all_to_all(
        jnp.broadcast_to(vol_blocks.astype(F32)[:, None, :], (groups, 1, VOL_GRP)),
        GROUP_AXES, split_axis=0, concat_axis=0, tiled=True,
    ).reshape(groups, VOL_GRP)
    packed = call(
        functools.partial(pack_kernel, groups, rounds),
        (ids, point_map.reshape(1, elems), table, displacement, connectivity, shape_grads, fluct_state),
        (SM, VM, VM, VM, VM, VM, HB),
        tuple(((2 * TILE, MSG_LANES), BF16) for _ in range(UNIT)) + (((8, elems), F32), ((8, elems), I32)),
        (VM,) * (UNIT + 2),
        [pltpu.VMEM((elems, NBMAX * LEVEL), BF16), pltpu.SemaphoreType.DMA],
    )
    strain, place = packed[UNIT:]
    msgs = [packed[0]] + [unit_permute(packed[k], k) for k in range(1, UNIT)]

    solved = None
    for turn in range(rounds):
        ints_t, small_t, blocks_t, other_t = held[turn]
        result = call(
            solve_kernel,
            (ids, ints_t, small_t, blocks_t, other_t, *msgs),
            (SM, SM) + (VM,) * (UNIT + 3),
            tuple(((2 * TILE, STATE_LANES), BF16) for _ in range(UNIT)) + (((UNIT, 2 * TILE, BS), BF16),),
            (VM,) * (UNIT + 1),
            [
                pltpu.VMEM((HALF_ROWS, COMPS * SLOTS, BS), F32),
                pltpu.VMEM((HALF_ROWS, COMPS * SLOTS, BS), BF16),
                pltpu.VMEM((HALF_ROWS, COMPS * SLOTS, BS), F32),
                pltpu.VMEM((OFF_GRP, SLOTS, BS), F32),
                pltpu.VMEM((HALF_ROWS, SLOTS, BS), F32),
                pltpu.VMEM((HALF_ROWS, SLOTS, BS), F32),
                pltpu.VMEM((NBMAX, SLOTS, BS), F32),
                pltpu.VMEM((HALF_ROWS // 2, 2 * BS, 2 * BS), BF16),
                pltpu.VMEM((OFF_GRP // 2, 2 * BS, 2 * BS), BF16),
            ],
        )
        if solved is None:
            solved = result
        else:
            of_turn = (jnp.arange(2 * TILE) % TILE) // (TILE // rounds) == turn
            solved = [jnp.where(of_turn[:, None], new, old) for new, old in zip(result, solved)]

    tangents = lax.all_to_all(solved[UNIT], UNIT_AXES, split_axis=0, concat_axis=0, tiled=True)
    back = [solved[0]] + [unit_permute(solved[k], k) for k in range(1, UNIT)]
    residual, product, norm = call(
        fem_kernel,
        (ids, tangents, place, strain, shape_grads, elem_volume.reshape(1, elems), connectivity, nodal_load),
        (SM,) + (VM,) * 7,
        (((3, node_count), F32), ((3, node_count), F32), ((devices, BS), F32)),
        (VM,) * 3,
        [],
    )
    norms = lax.all_to_all(norm, AXES, split_axis=0, concat_axis=0, tiled=True)
    norm_sq = jnp.sum(norms[:, 0])
    root_mean = jnp.sqrt(norm_sq / (3.0 * node_count * devices) + 1e-06)
    update = -jnp.minimum(1.0, CLIP_RMS / root_mean) * residual
    (fluct_new,) = call(
        unpack_kernel,
        (place, *back),
        (VM,) * (UNIT + 1),
        (((elems, NBMAX * LEVEL), BF16),),
        (HB,),
        [pltpu.VMEM((NBMAX, elems, LEVEL), BF16), pltpu.SemaphoreType.DMA((NBMAX,))],
    )
    return residual, product, update, fluct_new


def solution(mesh):
    sections, groups = mesh.shape["sec"], mesh.shape["bulk"]
    shape = (2, sections // 2, groups // 4, 2, 2)
    fine = Mesh(mesh.devices.reshape(shape), AXES)
    return jax.shard_map(
        functools.partial(on_device, shape),
        mesh=fine,
        in_specs=(
            P(None, AXES),
            P(None, AXES),
            P(None, AXES),
            P(None, AXES),
            P(AXES),
            P(AXES),
            P(GROUP_AXES, None),
            P(GROUP_AXES, None, None),
            P(None, GROUP_AXES, None, None),
            P(None, GROUP_AXES, None, None),
            P(None, GROUP_AXES, None),
            P(None, GROUP_AXES, None, None),
            P(None, GROUP_AXES),
            P(None, GROUP_AXES),
            P(None, GROUP_AXES, None),
            P(GROUP_AXES),
            P(AXES, None),
        ),
        out_specs=(P(None, AXES), P(None, AXES), P(None, AXES), P(AXES, None)),
        check_vma=False,
    )
```

time: 620 us -> 199 us (0.32); the launches traced: 609 us -> 198 us
  local copies, waits for them, and re-layouts: 219 us -> 9.35 us
  other arithmetic: 175 us -> 1.87 us
  waiting for transfers between devices: 107 us -> 33.5 us
  Pallas kernels: 0 us -> 60.4 us
  matrix products: 31 us -> 0 us
  starting transfers between devices: 33.9 us -> 50.5 us
    scatter-add x9 -> x0, other arithmetic: 137 us -> none  [the longest x6 89.1 us: assemble(): jax.ops.segment_sum(forces[component].reshape(-1), flat_ids, num_segments...]
    all_to_all x8 -> x1, waiting for transfers between devices: 107 us -> 1.14 us  [on_device(): norms = lax.all_to_all(norm, AXES, split_axis=0, concat_axis=0, tiled=True)]
    gather x20 -> x0, local copies, waits for them, and re-layouts: 67.4 us -> none  [the longest x3 11.7 us: contact_terms(): fluct_low[off_cols]]
    pallas_call x0 -> x5, Pallas kernels: none -> 60.4 us  [call(): pl.pallas_call(kernel, out_shape=[jax.ShapeDtypeStruct(s, d) for s, d in...]
    ppermute x0 -> x18, starting transfers between devices: none -> 47.7 us  [permute(): return lax.ppermute(value, AXES, pairs)]
    all_to_all x0 -> x2, blocking collectives: none -> 40.2 us  [the longest x1 31.2 us: on_device(): lax.all_to_all(jnp.broadcast_to(vol_blocks.astype(F32)[:, None, :], (grou...]
    psum x1 -> x0, blocking collectives: 40 us -> none  [on_device(): norm_sq = lax.psum(jnp.sum(residual * residual), ('sec', 'bulk'))]
    mul x10 -> x0, local copies, waits for them, and re-layouts: 40 us -> none  [the longest x5 21.6 us: contact_terms(): result = applied.at[off_rows].add(contrib * off_scale_cols[:, None, :])]
  transfers between devices with their start and end apart: 8 -> 19, of which waited for: 4 -> 5; matrix products, arithmetic and copies ran while one was open for 34% -> 1% of each run, Pallas kernels for 0% -> 5%
where the time goes in v1:
time: 199 us; the launch traced here: 198 us
  Pallas kernels  60.4 us (30%)
  starting transfers between devices  50.5 us (25%)
  blocking collectives  40.2 us (20%)
  waiting for transfers between devices  33.5 us (17%)
  local copies, waits for them, and re-layouts  9.35 us (5%)
  between operations  2.44 us (1%)
    pallas_call x5, Pallas kernels, call(): pl.pallas_call(kernel, out_shape=[jax.ShapeDtypeStruct(s, d) for s, d in...  60.4 us
    ppermute x18, starting transfers between devices, permute(): return lax.ppermute(value, AXES, pairs)  47.7 us
    ppermute x18, waiting for transfers between devices, permute(): return lax.ppermute(value, AXES, pairs)  32.3 us
    all_to_all x1, blocking collectives, on_device(): lax.all_to_all(jnp.broadcast_to(vol_blocks.astype(F32)[:, None, :], (grou...  31.2 us
    all_to_all x1, blocking collectives, on_device(): lax.all_to_all(solved[UNIT], UNIT_AXES, split_axis=0, concat_axis=0, tile...  8.97 us
    unnamed x45, local copies, waits for them, and re-layouts  5.86 us
  transfers between devices with their start and end apart: 19, of which 5 were waited for; matrix products, arithmetic and copies ran while one was open for 1% of the time, Pallas kernels for 5%

profile of v1, /device:TPU:0, one launch (start us, length us, event | category | flops | bytes accessed | tf_op | source)
XLA Modules:
  0.0 198.2 jit_solution(7534363860162657714)
XLA Ops:
  0.6 0.0 copy-start.18
  1.3 1.4 copy.39
  2.7 1.3 copy.33.off_row
  4.0 1.3 copy.34.off_col
  5.3 1.4 copy.32
  6.7 1.5 copy.41
  8.2 0.6 stack.29.ids
  8.8 29.2 %shard_map.192 = (bf16[26,128,128]{2,1,0:T(8,128)(2,1)}, f32[136,128]{1,0:T(8,128)}, s32[8,128]{1,0:T(8,128)}) custom-call(s32[8]{0:T(128)} %stack.29.ids, s32[1,8]{1,0:T(1,128)} %vol.1, s32[32,1]{1,0:T(8,128)} %copy.33.off_row, s32[32,1]{1,0:T(8,128)} %copy.34.off_col, s32[1]{0:T(128)S(6)} %copy.42.off_count, f32[20,6,128]{2,1,0:T(8,128)} %bitcast.26, ...), custom_call_target="tpu_custom_call" | custom-call | tf_op jit(solution)/shard_map/pallas_call | solution.py:470
  38.0 1.9 collective-permute-start.2
  39.9 0.0 collective-permute-done.2.blocks
  40.0 3.0 %collective-permute-start.3 = (bf16[16,128,128]{2,1,0:T(8,128)(2,1)S(1)}, bf16[16,128,128]{2,1,0:T(8,128)(2,1)S(1)}, u32[]{:S(2)}, u32[]{:S(2)}) collective-permute-start(bf16[16,128,128]{2,1,0:T(8,128)(2,1)S(1)} %slice.8), channel_id=1, source_target_pairs={{16,0},{17,1},{18,2},{19,3},{20,4},{21,5},{22,6},{23,7},{24,8},{25... | collective-permute-start | bytes 1572872 | tf_op jit(solution)/shard_map/ppermute | solution.py:506
  43.0 0.0 copy-done.18
  43.0 31.2 %all_to_all.22 = f32[8,1,8]{2,1,0:T(1,128)} all-to-all(f32[8,1,8]{2,1,0:T(1,128)S(1)} %broadcast_in_dim.9), channel_id=1, replica_groups=mesh['y'=2,'x'=2,'h'=2,'l'=2,'c'=2] {'h','l','c'}, dimensions={0} | all-to-all | bytes 512 | tf_op jit(solution)/shard_map/all_to_all | solution.py:534
  74.3 7.5 %shard_map.193 = (bf16[32,3968]{1,0:T(8,128)(2,1)}, bf16[32,3968]{1,0:T(8,128)(2,1)}, bf16[32,3968]{1,0:T(8,128)(2,1)}, bf16[32,3968]{1,0:T(8,128)(2,1)}, bf16[3...) custom-call(s32[8]{0:T(128)} %stack.29.ids, ...), custom_call_target="tpu_custom_call" | custom-call | tf_op jit(solution)/shard_map/pallas_call | solution.py:470
  81.8 0.1 collective-permute-start.4
  81.9 0.6 collective-permute-start.5
  82.5 1.2 collective-permute-start.6
  83.7 0.7 collective-permute-start
  84.4 0.0 collective-permute-done.ints
  84.4 0.0 copy-start.17
  84.4 0.0 copy-done.19
  84.4 0.7 collective-permute-start.1
  85.1 0.0 collective-permute-done.1.small
  85.1 20.1 %collective-permute-start.7 = (bf16[32,3968]{1,0:T(8,128)(2,1)}, bf16[32,3968]{1,0:T(8,128)(2,1)S(1)}, u32[]{:S(2)}, u32[]{:S(2)}) collective-permute-start(bf16[32,3968]{1,0:T(8,128)(2,1)} %get-tuple-element.36), channel_id=1, source_target_pairs={{8,0},{9,1},{10,2},{11,3},{12,4},{13,5},{14,6},{15,7},{0,8},{1,9},... | collective-permute-start | bytes 761864 | tf_op jit(solution)/shard_map/ppermute | solution.py:506
  105.2 0.0 collective-permute-done.4.refs_1_
  105.3 0.0 collective-permute-start.8
  105.3 0.0 collective-permute-done.5.refs_2_
  105.3 1.6 collective-permute-start.9
  106.9 0.0 collective-permute-done.6.refs_3_
  106.9 1.7 collective-permute-start.10
  108.5 13.9 %collective-permute-done.7.refs_4_ = bf16[32,3968]{1,0:T(8,128)(2,1)S(1)} collective-permute-done((bf16[32,3968]{1,0:T(8,128)(2,1)}, bf16[32,3968]{1,0:T(8,128)(2,1)S(1)}, u32[]{:S(2)}, u32[]{:S(2)}) %collective-permute-start.7) | collective-permute-done | bytes 253984 | tf_op jit(solution)/shard_map/ppermute | solution.py:506
  122.5 2.7 %collective-permute-done.8.refs_5_ = bf16[32,3968]{1,0:T(8,128)(2,1)S(1)} collective-permute-done((bf16[32,3968]{1,0:T(8,128)(2,1)}, bf16[32,3968]{1,0:T(8,128)(2,1)S(1)}, u32[]{:S(2)}, u32[]{:S(2)}) %collective-permute-start.8) | collective-permute-done | bytes 253984 | tf_op jit(solution)/shard_map/ppermute | solution.py:506
  125.2 0.0 collective-permute-done.9.refs_6_
  125.2 0.0 collective-permute-done.10.refs_7_
  125.2 0.0 collective-permute-done.3.other
  125.3 0.6 copy-done.6
  125.9 0.1 copy-done.7
  126.0 0.1 copy-done.8
  126.1 0.2 copy-done.1
  126.3 13.0 %shard_map.194 = (bf16[32,3840]{1,0:T(8,128)(2,1)}, bf16[32,3840]{1,0:T(8,128)(2,1)}, bf16[32,3840]{1,0:T(8,128)(2,1)}, bf16[32,3840]{1,0:T(8,128)(2,1)}, bf16[3...) custom-call(s32[8]{0:T(128)} %stack.29.ids, ...), custom_call_target="tpu_custom_call" | custom-call | tf_op jit(solution)/shard_map/pallas_call | solution.py:470
  139.2 0.7 collective-permute-start.11
  139.9 9.5 %collective-permute-start.12 = (bf16[32,3840]{1,0:T(8,128)(2,1)}, bf16[32,3840]{1,0:T(8,128)(2,1)S(1)}, u32[]{:S(2)}, u32[]{:S(2)}) collective-permute-start(bf16[32,3840]{1,0:T(8,128)(2,1)} %get-tuple-element.48), channel_id=1, source_target_pairs={{2,0},{3,1},{0,2},{1,3},{6,4},{7,5},{4,6},{5,7},{10,8},{11,9},{8,1... | collective-permute-start | bytes 737288 | tf_op jit(solution)/shard_map/ppermute | solution.py:506
  149.4 9.0 %all_to_all.23.tangents = bf16[8,32,128]{2,1,0:T(8,128)(2,1)} all-to-all(bf16[8,32,128]{2,1,0:T(8,128)(2,1)} %get-tuple-element.40), channel_id=1, replica_groups=mesh['y'=2,'x'=2,'h'=2,'l'=2,'c'=2] {'x','l','c'}, dimensions={0} | all-to-all | bytes 131072 | tf_op jit(solution)/shard_map/all_to_all | solution.py:576
  158.4 3.0 %shard_map.195 = (f32[3,128]{1,0:T(4,128)}, f32[3,128]{1,0:T(4,128)}, f32[32,128]{1,0:T(8,128)}) custom-call(s32[8]{0:T(128)} %stack.29.ids, bf16[8,32,128]{2,1,0:T(8,128)(2,1)} %all_to_all.23.tangents, s32[8,512]{1,0:T(8,128)} %get-tuple-element.41.place, f32[8,512]{1,0:T(8,128)} %get-tuple-element.42.strain, f32[12,512]{1,0:T(8,128)} %grads.3, ...), custom_call_target="tpu_custom_call" | custom-call | tf_op jit(solution)/shard_map/pallas_call | solution.py:470
  161.4 2.7 %all-to-all-start.2 = ((f32[32,1,128]{2,1,0:T(1,128)}), f32[32,1,128]{2,1,0:T(1,128)S(1)}, u32[]{:S(2)}, u32[]{:S(2)}) async-start(f32[32,1,128]{2,1,0:T(1,128)} %bitcast.31), calls=%async_computation.2 | async-start | bytes 32768 | tf_op jit(solution)/shard_map/all_to_all | solution.py:586
  164.1 1.5 collective-permute-start.13
  165.6 1.5 collective-permute-start.14
  167.1 0.2 collective-permute-start.15
  167.4 0.0 collective-permute-done.11.refs_1_
  167.4 1.4 collective-permute-start.16
  168.8 0.0 collective-permute-done.12.refs_2_
  168.8 1.3 collective-permute-start.17
  170.1 1.1 all-to-all-done.2
  171.2 0.6 slice_reduce_fusion
  172.5 1.3 broadcast_multiply_fusion
  173.8 0.0 collective-permute-done.13.refs_3_
  173.8 11.4 %collective-permute-done.14.refs_4_ = bf16[32,3840]{1,0:T(8,128)(2,1)S(1)} collective-permute-done((bf16[32,3840]{1,0:T(8,128)(2,1)}, bf16[32,3840]{1,0:T(8,128)(2,1)S(1)}, u32[]{:S(2)}, u32[]{:S(2)}) %collective-permute-start.14) | collective-permute-done | bytes 245792 | tf_op jit(solution)/shard_map/ppermute | solution.py:506
  185.2 4.2 %collective-permute-done.15.refs_5_ = bf16[32,3840]{1,0:T(8,128)(2,1)S(1)} collective-permute-done((bf16[32,3840]{1,0:T(8,128)(2,1)}, bf16[32,3840]{1,0:T(8,128)(2,1)S(1)}, u32[]{:S(2)}, u32[]{:S(2)}) %collective-permute-start.15) | collective-permute-done | bytes 245792 | tf_op jit(solution)/shard_map/ppermute | solution.py:506
  189.4 0.0 collective-permute-done.16.refs_6_
  189.4 0.0 collective-permute-done.17.refs_7_
  189.5 0.6 copy-done.13
  190.1 0.1 copy-done.14
  190.2 0.1 copy-done.15
  190.3 7.7 %shard_map.196 = bf16[512,3072]{1,0:T(8,128)(2,1)} custom-call(s32[8,512]{1,0:T(8,128)} %get-tuple-element.41.place, bf16[32,3840]{1,0:T(8,128)(2,1)} %get-tuple-element.46.refs_0_, bf16[32,3840]{1,0:T(8,128)(2,1)} %copy-done.9, bf16[32,3840]{1,0:T(8,128)(2,1)} %copy-done.10, bf16[32,3840]{1,0:T(8,128)(2,1)} %copy-done.11, bf16[32,3840]{1,0:T(8,128)(2,1)} %copy-done.12, ...), custom_call_target="tpu_custom_call" | custom-call | tf_op jit(solution)/shard_map/pallas_call | solution.py:470
  (34 shorter events, 0.1 us)
Async XLA Ops:
  0.6 42.4 %copy-start.18 = (s32[1,8]{1,0:T(1,128)S(1)}, s32[1,8]{1,0:T(1,128)}, u32[]{:S(2)}) copy-start(s32[1,8]{1,0:T(1,128)} %vol.1) | copy-start | bytes 100
  38.0 45.8 %copy-start.20 = (s32[8,128]{1,0:T(8,128)S(1)}, s32[8,128]{1,0:T(8,128)}, u32[]{:S(2)}) copy-start(s32[8,128]{1,0:T(8,128)} %get-tuple-element.29) | copy-start | bytes 12292
  38.0 46.4 %copy-start.19 = (f32[136,128]{1,0:T(8,128)S(1)}, f32[136,128]{1,0:T(8,128)}, u32[]{:S(2)}) copy-start(f32[136,128]{1,0:T(8,128)} %get-tuple-element.30) | copy-start | bytes 208900
  38.0 2.0 collective-permute-start.2
  39.9 85.3 %copy-start = (bf16[26,128,128]{2,1,0:T(8,128)(2,1)}, bf16[26,128,128]{2,1,0:T(8,128)(2,1)S(1)}, u32[]{:S(2)}) copy-start(bf16[26,128,128]{2,1,0:T(8,128)(2,1)S(1)} %collective-permute-done.2.blocks) | copy-start | bytes 2555908
  40.0 85.2 %collective-permute-start.3 = (bf16[16,128,128]{2,1,0:T(8,128)(2,1)S(1)}, bf16[16,128,128]{2,1,0:T(8,128)(2,1)S(1)}, u32[]{:S(2)}, u32[]{:S(2)}) collective-permute-start(bf16[16,128,128]{2,1,0:T(8,128)(2,1)S(1)} %slice.8), channel_id=1, source_target_pairs={{16,0},{17,1},{18,2},{19,3},{20,4},{21,5},{22,6},{23,7},{24,8},{25... | collective-permute-start | bytes 1572872 | tf_op jit(solution)/shard_map/ppermute | solution.py:506
  81.8 23.5 %collective-permute-start.4 = (bf16[32,3968]{1,0:T(8,128)(2,1)}, bf16[32,3968]{1,0:T(8,128)(2,1)S(1)}, u32[]{:S(2)}, u32[]{:S(2)}) collective-permute-start(bf16[32,3968]{1,0:T(8,128)(2,1)} %get-tuple-element.33), channel_id=1, source_target_pairs={{1,0},{0,1},{3,2},{2,3},{5,4},{4,5},{7,6},{6,7},{9,8},{8,9},{11,10... | collective-permute-start | bytes 761864 | tf_op jit(solution)/shard_map/ppermute | solution.py:506
  81.9 23.4 %collective-permute-start.5 = (bf16[32,3968]{1,0:T(8,128)(2,1)}, bf16[32,3968]{1,0:T(8,128)(2,1)S(1)}, u32[]{:S(2)}, u32[]{:S(2)}) collective-permute-start(bf16[32,3968]{1,0:T(8,128)(2,1)} %get-tuple-element.34), channel_id=1, source_target_pairs={{2,0},{3,1},{0,2},{1,3},{6,4},{7,5},{4,6},{5,7},{10,8},{11,9},{8,1... | collective-permute-start | bytes 761864 | tf_op jit(solution)/shard_map/ppermute | solution.py:506
  82.5 24.4 %collective-permute-start.6 = (bf16[32,3968]{1,0:T(8,128)(2,1)}, bf16[32,3968]{1,0:T(8,128)(2,1)S(1)}, u32[]{:S(2)}, u32[]{:S(2)}) collective-permute-start(bf16[32,3968]{1,0:T(8,128)(2,1)} %get-tuple-element.35), channel_id=1, source_target_pairs={{3,0},{2,1},{1,2},{0,3},{7,4},{6,5},{5,6},{4,7},{11,8},{10,9},{9,1... | collective-permute-start | bytes 761864 | tf_op jit(solution)/shard_map/ppermute | solution.py:506
  83.7 0.7 collective-permute-start
  84.4 40.9 %copy-start.17 = (s32[8,128]{1,0:T(8,128)}, s32[8,128]{1,0:T(8,128)S(1)}, u32[]{:S(2)}) copy-start(s32[8,128]{1,0:T(8,128)S(1)} %collective-permute-done.ints) | copy-start | bytes 12292
  84.4 0.7 collective-permute-start.1
  85.1 40.2 %copy-start.16 = (f32[136,128]{1,0:T(8,128)}, f32[136,128]{1,0:T(8,128)S(1)}, u32[]{:S(2)}) copy-start(f32[136,128]{1,0:T(8,128)S(1)} %collective-permute-done.1.small) | copy-start | bytes 208900
  85.1 37.4 %collective-permute-start.7 = (bf16[32,3968]{1,0:T(8,128)(2,1)}, bf16[32,3968]{1,0:T(8,128)(2,1)S(1)}, u32[]{:S(2)}, u32[]{:S(2)}) collective-permute-start(bf16[32,3968]{1,0:T(8,128)(2,1)} %get-tuple-element.36), channel_id=1, source_target_pairs={{8,0},{9,1},{10,2},{11,3},{12,4},{13,5},{14,6},{15,7},{0,8},{1,9},... | collective-permute-start | bytes 761864 | tf_op jit(solution)/shard_map/ppermute | solution.py:506
  105.3 20.0 %copy-start.2 = (bf16[32,3968]{1,0:T(8,128)(2,1)}, bf16[32,3968]{1,0:T(8,128)(2,1)S(1)}, u32[]{:S(2)}) copy-start(bf16[32,3968]{1,0:T(8,128)(2,1)S(1)} %collective-permute-done.4.refs_1_) | copy-start | bytes 761860
  105.3 19.9 %collective-permute-start.8 = (bf16[32,3968]{1,0:T(8,128)(2,1)}, bf16[32,3968]{1,0:T(8,128)(2,1)S(1)}, u32[]{:S(2)}, u32[]{:S(2)}) collective-permute-start(bf16[32,3968]{1,0:T(8,128)(2,1)} %get-tuple-element.37), channel_id=1, source_target_pairs={{9,0},{8,1},{11,2},{10,3},{13,4},{12,5},{15,6},{14,7},{1,8},{0,9},... | collective-permute-start | bytes 761864 | tf_op jit(solution)/shard_map/ppermute | solution.py:506
  105.3 20.0 %copy-start.3 = (bf16[32,3968]{1,0:T(8,128)(2,1)}, bf16[32,3968]{1,0:T(8,128)(2,1)S(1)}, u32[]{:S(2)}) copy-start(bf16[32,3968]{1,0:T(8,128)(2,1)S(1)} %collective-permute-done.5.refs_2_) | copy-start | bytes 761860
  105.3 19.9 %collective-permute-start.9 = (bf16[32,3968]{1,0:T(8,128)(2,1)}, bf16[32,3968]{1,0:T(8,128)(2,1)S(1)}, u32[]{:S(2)}, u32[]{:S(2)}) collective-permute-start(bf16[32,3968]{1,0:T(8,128)(2,1)} %get-tuple-element.38), channel_id=1, source_target_pairs={{10,0},{11,1},{8,2},{9,3},{14,4},{15,5},{12,6},{13,7},{2,8},{3,9},... | collective-permute-start | bytes 761864 | tf_op jit(solution)/shard_map/ppermute | solution.py:506
  106.9 18.4 %copy-start.4 = (bf16[32,3968]{1,0:T(8,128)(2,1)}, bf16[32,3968]{1,0:T(8,128)(2,1)S(1)}, u32[]{:S(2)}) copy-start(bf16[32,3968]{1,0:T(8,128)(2,1)S(1)} %collective-permute-done.6.refs_3_) | copy-start | bytes 761860
  106.9 18.3 %collective-permute-start.10 = (bf16[32,3968]{1,0:T(8,128)(2,1)}, bf16[32,3968]{1,0:T(8,128)(2,1)S(1)}, u32[]{:S(2)}, u32[]{:S(2)}) collective-permute-start(bf16[32,3968]{1,0:T(8,128)(2,1)} %get-tuple-element.39), channel_id=1, source_target_pairs={{11,0},{10,1},{9,2},{8,3},{15,4},{14,5},{13,6},{12,7},{3,8},{2,9},... | collective-permute-start | bytes 761864 | tf_op jit(solution)/shard_map/ppermute | solution.py:506
  122.5 2.8 %copy-start.5 = (bf16[32,3968]{1,0:T(8,128)(2,1)}, bf16[32,3968]{1,0:T(8,128)(2,1)S(1)}, u32[]{:S(2)}) copy-start(bf16[32,3968]{1,0:T(8,128)(2,1)S(1)} %collective-permute-done.7.refs_4_) | copy-start | bytes 761860
  125.2 0.7 copy-start.6
  125.2 0.8 copy-start.7
  125.2 0.9 copy-start.8
  125.2 1.0 copy-start.1
  139.2 28.1 %collective-permute-start.11 = (bf16[32,3840]{1,0:T(8,128)(2,1)}, bf16[32,3840]{1,0:T(8,128)(2,1)S(1)}, u32[]{:S(2)}, u32[]{:S(2)}) collective-permute-start(bf16[32,3840]{1,0:T(8,128)(2,1)} %get-tuple-element.47), channel_id=1, source_target_pairs={{1,0},{0,1},{3,2},{2,3},{5,4},{4,5},{7,6},{6,7},{9,8},{8,9},{11,10... | collective-permute-start | bytes 737288 | tf_op jit(solution)/shard_map/ppermute | solution.py:506
  139.9 28.9 %collective-permute-start.12 = (bf16[32,3840]{1,0:T(8,128)(2,1)}, bf16[32,3840]{1,0:T(8,128)(2,1)S(1)}, u32[]{:S(2)}, u32[]{:S(2)}) collective-permute-start(bf16[32,3840]{1,0:T(8,128)(2,1)} %get-tuple-element.48), channel_id=1, source_target_pairs={{2,0},{3,1},{0,2},{1,3},{6,4},{7,5},{4,6},{5,7},{10,8},{11,9},{8,1... | collective-permute-start | bytes 737288 | tf_op jit(solution)/shard_map/ppermute | solution.py:506
  161.4 9.8 %all-to-all-start.2 = ((f32[32,1,128]{2,1,0:T(1,128)}), f32[32,1,128]{2,1,0:T(1,128)S(1)}, u32[]{:S(2)}, u32[]{:S(2)}) async-start(f32[32,1,128]{2,1,0:T(1,128)} %bitcast.31), calls=%async_computation.2 | async-start | bytes 32768 | tf_op jit(solution)/shard_map/all_to_all | solution.py:586
  164.1 9.6 %collective-permute-start.13 = (bf16[32,3840]{1,0:T(8,128)(2,1)}, bf16[32,3840]{1,0:T(8,128)(2,1)S(1)}, u32[]{:S(2)}, u32[]{:S(2)}) collective-permute-start(bf16[32,3840]{1,0:T(8,128)(2,1)} %get-tuple-element.49), channel_id=1, source_target_pairs={{3,0},{2,1},{1,2},{0,3},{7,4},{6,5},{5,6},{4,7},{11,8},{10,9},{9,1... | collective-permute-start | bytes 737288 | tf_op jit(solution)/shard_map/ppermute | solution.py:506
  165.6 19.6 %collective-permute-start.14 = (bf16[32,3840]{1,0:T(8,128)(2,1)}, bf16[32,3840]{1,0:T(8,128)(2,1)S(1)}, u32[]{:S(2)}, u32[]{:S(2)}) collective-permute-start(bf16[32,3840]{1,0:T(8,128)(2,1)} %get-tuple-element.50), channel_id=1, source_target_pairs={{8,0},{9,1},{10,2},{11,3},{12,4},{13,5},{14,6},{15,7},{0,8},{1,9},... | collective-permute-start | bytes 737288 | tf_op jit(solution)/shard_map/ppermute | solution.py:506
  167.1 22.3 %collective-permute-start.15 = (bf16[32,3840]{1,0:T(8,128)(2,1)}, bf16[32,3840]{1,0:T(8,128)(2,1)S(1)}, u32[]{:S(2)}, u32[]{:S(2)}) collective-permute-start(bf16[32,3840]{1,0:T(8,128)(2,1)} %get-tuple-element.51), channel_id=1, source_target_pairs={{9,0},{8,1},{11,2},{10,3},{13,4},{12,5},{15,6},{14,7},{1,8},{0,9},... | collective-permute-start | bytes 737288 | tf_op jit(solution)/shard_map/ppermute | solution.py:506
  167.4 22.1 %copy-start.9 = (bf16[32,3840]{1,0:T(8,128)(2,1)}, bf16[32,3840]{1,0:T(8,128)(2,1)S(1)}, u32[]{:S(2)}) copy-start(bf16[32,3840]{1,0:T(8,128)(2,1)S(1)} %collective-permute-done.11.refs_1_) | copy-start | bytes 737284
  167.4 22.0 %collective-permute-start.16 = (bf16[32,3840]{1,0:T(8,128)(2,1)}, bf16[32,3840]{1,0:T(8,128)(2,1)S(1)}, u32[]{:S(2)}, u32[]{:S(2)}) collective-permute-start(bf16[32,3840]{1,0:T(8,128)(2,1)} %get-tuple-element.52), channel_id=1, source_target_pairs={{10,0},{11,1},{8,2},{9,3},{14,4},{15,5},{12,6},{13,7},{2,8},{3,9},... | collective-permute-start | bytes 737288 | tf_op jit(solution)/shard_map/ppermute | solution.py:506
  168.8 20.7 %copy-start.10 = (bf16[32,3840]{1,0:T(8,128)(2,1)}, bf16[32,3840]{1,0:T(8,128)(2,1)S(1)}, u32[]{:S(2)}) copy-start(bf16[32,3840]{1,0:T(8,128)(2,1)S(1)} %collective-permute-done.12.refs_2_) | copy-start | bytes 737284
  168.8 20.6 %collective-permute-start.17 = (bf16[32,3840]{1,0:T(8,128)(2,1)}, bf16[32,3840]{1,0:T(8,128)(2,1)S(1)}, u32[]{:S(2)}, u32[]{:S(2)}) collective-permute-start(bf16[32,3840]{1,0:T(8,128)(2,1)} %get-tuple-element.53), channel_id=1, source_target_pairs={{11,0},{10,1},{9,2},{8,3},{15,4},{14,5},{13,6},{12,7},{3,8},{2,9},... | collective-permute-start | bytes 737288 | tf_op jit(solution)/shard_map/ppermute | solution.py:506
  173.8 15.7 %copy-start.11 = (bf16[32,3840]{1,0:T(8,128)(2,1)}, bf16[32,3840]{1,0:T(8,128)(2,1)S(1)}, u32[]{:S(2)}) copy-start(bf16[32,3840]{1,0:T(8,128)(2,1)S(1)} %collective-permute-done.13.refs_3_) | copy-start | bytes 737284
  185.2 4.2 %copy-start.12 = (bf16[32,3840]{1,0:T(8,128)(2,1)}, bf16[32,3840]{1,0:T(8,128)(2,1)S(1)}, u32[]{:S(2)}) copy-start(bf16[32,3840]{1,0:T(8,128)(2,1)S(1)} %collective-permute-done.14.refs_4_) | copy-start | bytes 737284
  189.4 0.7 copy-start.13
  189.4 0.8 copy-start.14
  189.4 0.9 copy-start.15

commit v2 on v1

--- a/solution.py
+++ b/solution.py
@@ -25,10 +25,10 @@
 MSG_LANES = STATE_LANES + 128
 GAIN_NORMAL = 0.4
 CLIP_RMS = 1.0
-SM_DIAG_NORMAL = 80
-SM_OFF_NORMAL = 96
-SM_AFFINE = 128
-SM_ROWS = 136
+SM_NORMAL = 80
+SM_AFFINE = 88
+SM_ROWS = 96
+RANK_LANE = 6
 
 F32 = jnp.float32
 BF16 = jnp.bfloat16
@@ -75,6 +75,19 @@
 def class_onehot(slot, size, level_rows):
     chosen = jnp.where(size == level_rows, slot, -1)
     return jnp.where(iota((SLOTS, slot.shape[1]), 0) == chosen, 1.0, 0.0).astype(BF16)
+
+
+def returned_onehots(ids, tangents, slot, rank):
+    packed, hots = [], [None] * NBMAX
+    wanted = rank * SLOTS + slot
+    place = iota((SLOTS, 1), 0)
+    for row0, one, two in ((0, 3, 0), (TILE, 2, 1)):
+        tile = jnp.concatenate([tangents[ids[5] ^ k, row0 : row0 + TILE, :] for k in range(UNIT)], axis=0)
+        packed.append(tile)
+        for c, lane in ((one, RANK_LANE), (two, 64 + RANK_LANE)):
+            at = tile[:, lane : lane + 1].astype(F32).astype(I32) * SLOTS + place
+            hots[c] = jnp.where(wanted == at, 1.0, 0.0).astype(BF16)
+    return packed, hots
 
 
 def node_onehot(conn_row, nodes):
@@ -110,9 +123,13 @@
 
 def matrix_pack_kernel(
     ids, vol, off_row, off_col, off_count, coupling, diag_normal, off_normal, affine, diag, off,
-    blocks, small, ints, row_local, row_size, rows_sel, seen, sems,
+    diag_out, off_out, small, ints, row_local, row_size, rows_sel, seen, sems,
 ):
     half = ids[0]
+    off_copy = pltpu.make_async_copy(
+        off.at[pl.ds(half * HALF_OFF, HALF_OFF)], off_out, sems.at[HALF_ROWS]
+    )
+    off_copy.start()
     small[...] = jnp.zeros_like(small)
     for size in range(NBMAX + 1):
         seen[size] = 0
@@ -136,38 +153,33 @@
         @pl.when(mine)
         def _(size=size, v=v):
             small[pl.ds(SM_AFFINE - 1 + size, 1), 0:36] = affine[v : v + 1, :]
+            ints[6, size - 1] = v
 
         start = start + size
-    copies = [
-        pltpu.make_async_copy(
-            off.at[pl.ds(half * HALF_OFF, HALF_OFF)], blocks.at[pl.ds(HALF_ROWS, HALF_OFF)], sems.at[HALF_ROWS]
-        )
-    ]
+    copies = [off_copy]
     for i in range(HALF_ROWS):
         copies.append(
-            pltpu.make_async_copy(diag.at[pl.ds(rows_sel[i], 1)], blocks.at[pl.ds(i, 1)], sems.at[i])
+            pltpu.make_async_copy(diag.at[pl.ds(rows_sel[i], 1)], diag_out.at[pl.ds(i, 1)], sems.at[i])
         )
-    for copy in copies:
-        copy.start()
+        copies[-1].start()
+    lane = iota((8, BS), 1)
+    normals = jnp.zeros((8, BS), F32)
+    diag_rows = diag_normal[...]
     for i in range(HALF_ROWS):
         row = rows_sel[i]
-        small[8 * i : 8 * i + COMPS, :] = coupling[row]
-        small[SM_DIAG_NORMAL + i : SM_DIAG_NORMAL + i + 1, 0:COMPS] = diag_normal[pl.ds(row, 1), :]
-
-    @pl.when(half == 0)
-    def _():
-        small[SM_OFF_NORMAL : SM_OFF_NORMAL + OFF_GRP, 0:COMPS] = off_normal[...]
-
-    @pl.when(half != 0)
-    def _():
-        small[SM_OFF_NORMAL : SM_OFF_NORMAL + HALF_OFF, 0:COMPS] = off_normal[HALF_OFF:, :]
-        small[SM_OFF_NORMAL + HALF_OFF : SM_OFF_NORMAL + OFF_GRP, 0:COMPS] = off_normal[:HALF_OFF, :]
-
+        small[8 * i : 8 * i + COMPS, :] = coupling[pl.ds(COMPS * row, COMPS), :]
+        normals += jnp.where(lane == i, pltpu.roll(diag_rows, (i - row + BS) % BS, 1), 0.0)
+    off_rows = off_normal[...]
+    direct = pltpu.roll(off_rows, HALF_OFF, 1)
+    swapped = jnp.where(lane < 2 * HALF_OFF, off_rows, pltpu.roll(off_rows, 2 * HALF_OFF, 1))
+    chosen = jnp.where(half == 0, direct, swapped)
+    normals += jnp.where(jnp.logical_and(lane >= HALF_OFF, lane < HALF_OFF + OFF_GRP), chosen, 0.0)
+    small[SM_NORMAL : SM_NORMAL + 8, :] = normals
     live_total = off_count[0]
 
     def contact(n, found):
         slot = (n + half * HALF_OFF) % OFF_GRP
-        row = off_row[slot, 0]
+        row = off_row[0, slot]
         local = row_local[row]
         ints[5, n] = row_size[row]
         live = jnp.logical_and(slot < live_total, local >= 0)
@@ -176,7 +188,7 @@
         def _():
             ints[1, found] = n
             ints[2, found] = local
-            ints[3, found] = row_local[off_col[slot, 0]]
+            ints[3, found] = row_local[off_col[0, slot]]
 
         return found + live.astype(I32)
 
@@ -185,8 +197,8 @@
         copy.wait()
 
 
-def pack_kernel(groups, rounds, ids, point_map, table, disp, conn, grads, state, *refs):
-    outs, (strain_out, place_out, state_vmem, sem) = refs[:UNIT], refs[UNIT:]
+def pack_kernel(groups, rounds, ids, point_map, disp, conn, grads, state, *refs):
+    out, strain_out, place_out, state_vmem, sem = refs
     load = pltpu.make_async_copy(state, state_vmem, sem)
     load.start()
     elems = point_map.shape[1]
@@ -203,11 +215,34 @@
     across = (delta % 2) ^ core
     turn = delta // 2
     offset = ((across ^ x_me) * 4) + ((low ^ l_me) * 2) + (core ^ c_me)
-    group_hot = jnp.where(iota((groups, elems), 0) == group, 1.0, 0.0).astype(BF16)
-    sizes = dot_tn(table[...].astype(F32).astype(BF16), group_hot)
-    size = jnp.sum(
-        jnp.where(iota((VOL_GRP, elems), 0) == volume, sizes, 0.0), axis=0, keepdims=True
-    ).astype(I32)
+    volumes = groups * VOL_GRP
+    volume_hot = iota((volumes, elems), 0) == group * VOL_GRP + volume
+    volume_hot16 = jnp.where(volume_hot, 1.0, 0.0).astype(BF16)
+    load.wait()
+    ones = jnp.ones((8, LEVEL), BF16)
+    filled = jnp.concatenate(
+        [dot_nt(ones, jnp.abs(state_vmem[:, LEVEL * a : LEVEL * (a + 1)]))[0:1] for a in range(NBMAX)], axis=0
+    )
+    marks = jnp.concatenate(
+        [jnp.where(filled > 0.0, 1.0, 0.0), jnp.ones((1, elems), F32), jnp.zeros((3, elems), F32)], axis=0
+    ).astype(BF16)
+
+    def code_of(take, counts, number):
+        height = jnp.zeros_like(number)
+        for a in range(NBMAX):
+            height = jnp.where(take(counts, a) > 0.0, a + 1, height)
+        return jnp.where(take(counts, NBMAX) > 0.0, height * VOL_GRP + number % VOL_GRP, 1 << 20)
+
+    code_row = code_of(
+        lambda x, a: x[a : a + 1, :], dot_nt(marks, volume_hot16), iota((1, volumes), 1)
+    )
+    code_col = code_of(
+        lambda x, a: x[:, a : a + 1], dot_nt(volume_hot16, marks), iota((volumes, 1), 0)
+    )
+    same = iota((volumes, volumes), 0) // VOL_GRP == iota((volumes, volumes), 1) // VOL_GRP
+    below = jnp.where(jnp.logical_and(same, code_row < code_col), 1, 0)
+    rank_col = jnp.sum(below, axis=1, keepdims=True) + 1
+    size = jnp.sum(jnp.where(volume_hot, rank_col, 0), axis=0, keepdims=True)
     key = (offset * NBMAX + size - 1) * rounds + turn
     key_hot = iota((UNIT * NBMAX * rounds, elems), 0) == key
     earlier = jnp.where(iota((elems, elems), 0) < iota((elems, elems), 1), 1.0, 0.0).astype(BF16)
@@ -220,7 +255,7 @@
     onehots = [node_onehot(conn[a : a + 1, :], nodes) for a in range(4)]
     found = gather_nodes(nodal_parts(disp[...]), onehots)
     strain = strain_rows(grads[...], found)
-    strain8 = jnp.concatenate(strain + [jnp.zeros((2, elems), F32)], axis=0)
+    strain8 = jnp.concatenate(strain + [volume.astype(F32), jnp.zeros((1, elems), F32)], axis=0)
     strain_out[...] = strain8
     first = jnp.concatenate([strain8, jnp.zeros((120, elems), F32)], axis=0).astype(BF16)
     second = jnp.concatenate(
@@ -230,43 +265,76 @@
     for one, other, row0 in ((3, 0, 0), (2, 1, TILE)):
         extras = (dot_nt(hots[one], first) + dot_nt(hots[other], second)).astype(BF16)
         for k in range(UNIT):
-            outs[k][row0 : row0 + TILE, STATE_LANES:] = extras[TILE * k : TILE * (k + 1)]
+            out[ids[5] ^ k, row0 : row0 + TILE, STATE_LANES:] = extras[TILE * k : TILE * (k + 1)]
     order = lane_order()
-    load.wait()
     for c in range(NBMAX):
         lane0, row0 = CLASS_PLACE[c]
         for a in range(c + 1):
             rows = dot_nn(hots[c], state_vmem[:, LEVEL * a : LEVEL * (a + 1)]).astype(BF16)
             rows = dot_nn(rows, order).astype(BF16)
             for k in range(UNIT):
-                outs[k][row0 : row0 + TILE, lane0 + LEVEL * a : lane0 + LEVEL * (a + 1)] = rows[
+                out[ids[5] ^ k, row0 : row0 + TILE, lane0 + LEVEL * a : lane0 + LEVEL * (a + 1)] = rows[
                     TILE * k : TILE * (k + 1)
                 ]
 
 
-def solve_kernel(ids, ints, small, blocks, other, *refs):
-    msgs, refs = refs[:UNIT], refs[UNIT:]
+def solve_kernel(ids, ints, small, blocks, own, other, msgs, *refs):
     outs, refs = refs[:UNIT], refs[UNIT:]
     tangents, state, low, acc, contact_scale, diag_scale, inverse, response, diag_pairs, off_pairs = refs
+    extras = []
+    for rank in range(NBMAX):
+        row0 = CLASS_PLACE[rank][1]
+        tile = jnp.concatenate([msgs[ids[5] ^ k, row0 : row0 + TILE, STATE_LANES:] for k in range(UNIT)], axis=0).astype(F32)
+        extras.append(tile if rank >= 2 else pltpu.roll(tile, 64, 1))
+    held = [[extras[rank][:, RANK_LANE : RANK_LANE + 1] == ints[6, c].astype(F32) for rank in range(NBMAX)] for c in range(NBMAX)]
+    agree = functools.reduce(jnp.logical_and, [held[c][c] for c in range(NBMAX)])
+    in_order = jnp.min(jnp.where(agree, 1.0, 0.0)) > 0.5
+
+    @pl.when(in_order)
+    def _():
+        for c in range(NBMAX):
+            lane0, row0 = CLASS_PLACE[c]
+            for a in range(c + 1):
+                r = CLASS_BASE[c] + a
+                for j in range(COMPS):
+                    lane = lane0 + LEVEL * a + BS * j
+                    for k in range(UNIT):
+                        piece = msgs[ids[5] ^ k, row0 : row0 + TILE, lane : lane + BS]
+                        dst = slice(SLOTS * j + TILE * k, SLOTS * j + TILE * (k + 1))
+                        low[r, dst, :] = piece
+                        state[r, dst, :] = piece.astype(F32)
+
+    @pl.when(jnp.logical_not(in_order))
+    def _():
+        def component(j, carry):
+            for c in range(NBMAX):
+                for a in range(c + 1):
+                    r = CLASS_BASE[c] + a
+                    total = jnp.zeros((SLOTS, BS), F32)
+                    for rank in range(a, NBMAX):
+                        lane0, row0 = CLASS_PLACE[rank]
+                        lane = pl.multiple_of(lane0 + LEVEL * a + BS * j, BS)
+                        piece = jnp.concatenate(
+                            [msgs[ids[5] ^ k, row0 : row0 + TILE, pl.ds(lane, BS)] for k in range(UNIT)], axis=0
+                        )
+                        total = jnp.where(held[c][rank], piece.astype(F32), total)
+                    dst = pl.ds(pl.multiple_of(SLOTS * j, SLOTS), SLOTS)
+                    low[r, dst, :] = total.astype(BF16)
+                    state[r, dst, :] = total
+            return carry
+
+        lax.fori_loop(0, COMPS, component, 0)
+
+    normals = small[SM_NORMAL : SM_NORMAL + 8, :]
+    normals = jnp.concatenate([normals, jnp.zeros((BS - 8, BS), F32)], axis=0)
+    parts = split3(normals)
     for c in range(NBMAX):
-        lane0, row0 = CLASS_PLACE[c]
-        for a in range(c + 1):
-            r = CLASS_BASE[c] + a
-            for j in range(COMPS):
-                lane = lane0 + LEVEL * a + BS * j
-                for k in range(UNIT):
-                    piece = msgs[k][row0 : row0 + TILE, lane : lane + BS]
-                    dst = slice(SLOTS * j + TILE * k, SLOTS * j + TILE * (k + 1))
-                    low[r, dst, :] = piece
-                    state[r, dst, :] = piece.astype(F32)
-    normals = small[SM_DIAG_NORMAL : SM_OFF_NORMAL + OFF_GRP, :]
-    shifted = pltpu.roll(normals, 64, 1)
-    for rows, one, two in ((0, 3, 0), (TILE, 2, 1)):
-        strains = jnp.concatenate([msgs[k][rows : rows + TILE, STATE_LANES:] for k in range(UNIT)], axis=0)
-        for cls, vectors in ((one, normals), (two, shifted)):
-            high, mid, lowest = split3(vectors)
-            dots = dot_nt(strains, high) + dot_nt(strains, mid) + dot_nt(strains, lowest)
-            response[cls, :, 0 : dots.shape[1]] = 1.0 + GAIN_NORMAL * jnp.tanh(dots)
+        strains = jnp.zeros((SLOTS, BS), F32)
+        for rank in range(NBMAX):
+            strains = jnp.where(held[c][rank], extras[rank], strains)
+        strains = strains.astype(BF16)
+        dots = dot_nn(strains, parts[0]) + dot_nn(strains, parts[1]) + dot_nn(strains, parts[2])
+        response[c] = 1.0 + GAIN_NORMAL * jnp.tanh(dots)
     eye = iota((BS, BS), 0) == iota((BS, BS), 1)
     for c in range(NBMAX):
         for a in range(c + 1):
@@ -290,9 +358,7 @@
 
     def contact_block(n):
         mine = n < HALF_OFF
-        own = blocks[HALF_ROWS + jnp.where(mine, n, 0)]
-        theirs = other[jnp.where(mine, 0, n - HALF_OFF)]
-        return jnp.where(mine, own, theirs)
+        return jnp.where(mine, own[jnp.where(mine, n, 0)], other[jnp.where(mine, 0, n - HALF_OFF)])
 
     def fill(p, carry):
         off_pairs[p, :BS, :BS] = contact_block(ints[1, 2 * p])
@@ -374,7 +440,8 @@
             axis=0,
             keepdims=True,
         )
-        acc[c, :SLOTS, :] = moved - total / ((c + 1) * BS)
+        found = sum(jnp.where(held[c][rank], rank + 1.0, 0.0) for rank in range(NBMAX))
+        acc[c, :SLOTS, :] = jnp.where(lane == RANK_LANE, found, moved - total / ((c + 1) * BS))
     for row0, one, two in ((0, 3, 0), (TILE, 2, 1)):
         first = acc[one, :SLOTS, :]
         second = acc[two, :SLOTS, :]
@@ -397,12 +464,11 @@
     elems = place.shape[1]
     nodes = nodal_load.shape[1]
     slot, size = place[0:1, :], place[1:2, :]
-    hots = [class_onehot(slot, size, c + 1) for c in range(NBMAX)]
+    packed, hots = returned_onehots(ids, tangents, slot, size)
     entries = jnp.zeros((64, elems), F32)
-    for row0, one, two in ((0, 3, 0), (TILE, 2, 1)):
-        packed = jnp.concatenate([tangents[ids[5] ^ k, row0 : row0 + TILE, :] for k in range(UNIT)], axis=0)
-        entries += dot_tn(packed, hots[one])[:64]
-        entries += dot_tn(packed, hots[two])[64:]
+    for tile, one, two in ((packed[0], 3, 0), (packed[1], 2, 1)):
+        entries += dot_tn(tile, hots[one])[:64]
+        entries += dot_tn(tile, hots[two])[64:]
     entry = lambda i, j: entries[8 * j + i : 8 * j + i + 1]
     weight = volume[...]
     g_all = grads[...]
@@ -437,11 +503,11 @@
     product[...] = assemble(trial)
 
 
-def unpack_kernel(place, *refs):
+def unpack_kernel(ids, place, tangents, *refs):
     msgs, (out, out_vmem, sems) = refs[:UNIT], refs[UNIT:]
     slot, size = place[0:1, :], place[1:2, :]
     order = lane_order()
-    hots = [class_onehot(slot, size, c + 1) for c in range(NBMAX)]
+    hots = returned_onehots(ids, tangents, slot, size)[1]
     copies = []
     for a in range(NBMAX):
         pieces = []
@@ -475,6 +541,51 @@
         scratch_shapes=scratch,
         compiler_params=pltpu.CompilerParams(vmem_limit_bytes=VMEM_LIMIT),
     )(*args)
+
+
+def solve_call(*args):
+    return call(
+        solve_kernel,
+        args,
+        (SM, SM) + (VM,) * 5,
+        tuple(((2 * TILE, STATE_LANES), BF16) for _ in range(UNIT)) + (((UNIT, 2 * TILE, BS), BF16),),
+        (VM,) * (UNIT + 1),
+        [
+            pltpu.VMEM((HALF_ROWS, COMPS * SLOTS, BS), F32),
+            pltpu.VMEM((HALF_ROWS, COMPS * SLOTS, BS), BF16),
+            pltpu.VMEM((HALF_ROWS, COMPS * SLOTS, BS), F32),
+            pltpu.VMEM((OFF_GRP, SLOTS, BS), F32),
+            pltpu.VMEM((HALF_ROWS, SLOTS, BS), F32),
+            pltpu.VMEM((HALF_ROWS, SLOTS, BS), F32),
+            pltpu.VMEM((NBMAX, SLOTS, BS), F32),
+            pltpu.VMEM((HALF_ROWS // 2, 2 * BS, 2 * BS), BF16),
+            pltpu.VMEM((OFF_GRP // 2, 2 * BS, 2 * BS), BF16),
+        ],
+    )
+
+
+def pack_call(groups, rounds, *args):
+    elems = args[1].shape[1]
+    return call(
+        functools.partial(pack_kernel, groups, rounds),
+        args,
+        (SM, VM, VM, VM, VM, HB),
+        (((UNIT, 2 * TILE, MSG_LANES), BF16), ((8, elems), F32), ((8, elems), I32)),
+        (VM,) * 3,
+        [pltpu.VMEM((elems, NBMAX * LEVEL), BF16), pltpu.SemaphoreType.DMA],
+    )
+
+
+def unpack_call(*args):
+    elems = args[1].shape[1]
+    return call(
+        unpack_kernel,
+        args,
+        (SM,) + (VM,) * (UNIT + 2),
+        (((elems, NBMAX * LEVEL), BF16),),
+        (HB,),
+        [pltpu.VMEM((NBMAX, elems, LEVEL), BF16), pltpu.SemaphoreType.DMA((NBMAX,))],
+    )
 
 
 def on_device(
@@ -508,73 +619,47 @@
     def unit_permute(value, k):
         return permute(value, lambda y, x, h, l, c: (y, x ^ (k >> 2), h, l ^ ((k >> 1) & 1), c ^ (k & 1)))
 
-    blocks, small, ints = call(
+    def normal_rows(normals):
+        return jnp.pad(normals.transpose(2, 1, 0)[:, 0], ((0, 2), (0, BS - normals.shape[0])))
+
+    diag_half, off_half, small, ints = call(
         matrix_pack_kernel,
         (
-            ids, vol_blocks, off_row, off_col, off_count, coupling[:, 0], diag_normal[:, 0], off_normal[:, 0],
-            c_affine[0], diag_blocks[:, 0], off_blocks[:, 0],
+            ids, vol_blocks, off_row.T, off_col.T, off_count, coupling.reshape(ROWS_GRP * COMPS, BS),
+            normal_rows(diag_normal), normal_rows(off_normal), c_affine[0], diag_blocks[:, 0], off_blocks[:, 0],
         ),
         (SM, SM, SM, SM, SM, VM, VM, VM, VM, HB, HB),
-        (((HALF_ROWS + HALF_OFF, BS, BS), BF16), ((SM_ROWS, BS), F32), ((8, BS), I32)),
-        (HB, VM, SM),
+        (((HALF_ROWS, BS, BS), BF16), ((HALF_OFF, BS, BS), BF16), ((SM_ROWS, BS), F32), ((8, BS), I32)),
+        (VM, VM, VM, SM),
         [
             pltpu.SMEM((32,), I32), pltpu.SMEM((32,), I32), pltpu.SMEM((16,), I32), pltpu.SMEM((8,), I32),
             pltpu.SemaphoreType.DMA((HALF_ROWS + 1,)),
         ],
     )
-    held = []
+    packed, strain, place = pack_call(
+        groups, rounds, ids, point_map.reshape(1, elems), displacement, connectivity, shape_grads, fluct_state
+    )
+    msgs = lax.all_to_all(packed, UNIT_AXES, split_axis=0, concat_axis=0, tiled=True)
+
+    solved = None
     for turn in range(rounds):
         def from_group(y, x, h, l, c, turn=turn):
             return y, x, (h + 2 * turn + (x ^ c)) % z_count, l, c
 
-        mine = [permute(value, from_group) for value in (blocks, small, ints)]
-        theirs = permute(mine[0][HALF_ROWS:], lambda y, x, h, l, c: (1 - y, x, h, l, c))
-        held.append((mine[2], mine[1], mine[0], theirs))
-
-    table = lax.all_to_all(
-        jnp.broadcast_to(vol_blocks.astype(F32)[:, None, :], (groups, 1, VOL_GRP)),
-        GROUP_AXES, split_axis=0, concat_axis=0, tiled=True,
-    ).reshape(groups, VOL_GRP)
-    packed = call(
-        functools.partial(pack_kernel, groups, rounds),
-        (ids, point_map.reshape(1, elems), table, displacement, connectivity, shape_grads, fluct_state),
-        (SM, VM, VM, VM, VM, VM, HB),
-        tuple(((2 * TILE, MSG_LANES), BF16) for _ in range(UNIT)) + (((8, elems), F32), ((8, elems), I32)),
-        (VM,) * (UNIT + 2),
-        [pltpu.VMEM((elems, NBMAX * LEVEL), BF16), pltpu.SemaphoreType.DMA],
-    )
-    strain, place = packed[UNIT:]
-    msgs = [packed[0]] + [unit_permute(packed[k], k) for k in range(1, UNIT)]
-
-    solved = None
-    for turn in range(rounds):
-        ints_t, small_t, blocks_t, other_t = held[turn]
-        result = call(
-            solve_kernel,
-            (ids, ints_t, small_t, blocks_t, other_t, *msgs),
-            (SM, SM) + (VM,) * (UNIT + 3),
-            tuple(((2 * TILE, STATE_LANES), BF16) for _ in range(UNIT)) + (((UNIT, 2 * TILE, BS), BF16),),
-            (VM,) * (UNIT + 1),
-            [
-                pltpu.VMEM((HALF_ROWS, COMPS * SLOTS, BS), F32),
-                pltpu.VMEM((HALF_ROWS, COMPS * SLOTS, BS), BF16),
-                pltpu.VMEM((HALF_ROWS, COMPS * SLOTS, BS), F32),
-                pltpu.VMEM((OFF_GRP, SLOTS, BS), F32),
-                pltpu.VMEM((HALF_ROWS, SLOTS, BS), F32),
-                pltpu.VMEM((HALF_ROWS, SLOTS, BS), F32),
-                pltpu.VMEM((NBMAX, SLOTS, BS), F32),
-                pltpu.VMEM((HALF_ROWS // 2, 2 * BS, 2 * BS), BF16),
-                pltpu.VMEM((OFF_GRP // 2, 2 * BS, 2 * BS), BF16),
-            ],
+        mine_t, diag_t, small_t, ints_t = lax.optimization_barrier(
+            tuple(permute(value, from_group) for value in (off_half, diag_half, small, ints))
         )
+        other_t = permute(mine_t, lambda y, x, h, l, c: (1 - y, x, h, l, c))
+        result = solve_call(ids, ints_t, small_t, diag_t, mine_t, other_t, msgs)
         if solved is None:
             solved = result
         else:
             of_turn = (jnp.arange(2 * TILE) % TILE) // (TILE // rounds) == turn
             solved = [jnp.where(of_turn[:, None], new, old) for new, old in zip(result, solved)]
 
-    tangents = lax.all_to_all(solved[UNIT], UNIT_AXES, split_axis=0, concat_axis=0, tiled=True)
     back = [solved[0]] + [unit_permute(solved[k], k) for k in range(1, UNIT)]
+    own, back[4] = lax.optimization_barrier((solved[UNIT], back[4]))
+    tangents = lax.all_to_all(own, UNIT_AXES, split_axis=0, concat_axis=0, tiled=True)
     residual, product, norm = call(
         fem_kernel,
         (ids, tangents, place, strain, shape_grads, elem_volume.reshape(1, elems), connectivity, nodal_load),
@@ -587,14 +672,7 @@
     norm_sq = jnp.sum(norms[:, 0])
     root_mean = jnp.sqrt(norm_sq / (3.0 * node_count * devices) + 1e-06)
     update = -jnp.minimum(1.0, CLIP_RMS / root_mean) * residual
-    (fluct_new,) = call(
-        unpack_kernel,
-        (place, *back),
-        (VM,) * (UNIT + 1),
-        (((elems, NBMAX * LEVEL), BF16),),
-        (HB,),
-        [pltpu.VMEM((NBMAX, elems, LEVEL), BF16), pltpu.SemaphoreType.DMA((NBMAX,))],
-    )
+    (fluct_new,) = unpack_call(ids, place, tangents, *back)
     return residual, product, update, fluct_new
 
 

time: 199 us -> 126 us (0.63)
  blocking collectives: 40.2 us -> 16.4 us
  Pallas kernels: 60.4 us -> 40.1 us
  starting transfers between devices: 50.5 us -> 35 us
  waiting for transfers between devices: 33.5 us -> 25.3 us
  local copies, waits for them, and re-layouts: 9.35 us -> 4.15 us
    all_to_all x2 -> x1, blocking collectives: 40.2 us -> 16.4 us  [on_device(): lax.all_to_all(own, UNIT_AXES, split_axis=0, concat_axis=0, tiled=True)]
    ppermute x18 -> x12, waiting for transfers between devices: 32.3 us -> 9.94 us  [permute(): return lax.ppermute(value, AXES, pairs)]
    ppermute x18 -> x12, starting transfers between devices: 47.7 us -> 26.7 us  [permute(): return lax.ppermute(value, AXES, pairs)]
    pallas_call x5, Pallas kernels: 60.4 us -> 40.1 us  [call(): pl.pallas_call(kernel, out_shape=[jax.ShapeDtypeStruct(s, d) for s, d in...]
    all_to_all x0 -> x1, waiting for transfers between devices: none -> 15.3 us  [on_device(): lax.all_to_all(packed, UNIT_AXES, split_axis=0, concat_axis=0, tiled=True)]
    all_to_all x0 -> x1, starting transfers between devices: none -> 5.24 us  [on_device(): lax.all_to_all(packed, UNIT_AXES, split_axis=0, concat_axis=0, tiled=True)]
    unnamed x45 -> x34, local copies, waits for them, and re-layouts: 5.86 us -> 2.28 us
    squeeze x2 -> x0, local copies, waits for them, and re-layouts: 2.82 us -> none  [the longest x1 1.46 us: on_device(): coupling[:, 0]]
  transfers between devices with their start and end apart: 19 -> 14, of which waited for: 5 -> 3; matrix products, arithmetic and copies ran while one was open for 1% -> 1% of each run, Pallas kernels for 5% -> 11%
where the time goes in v2:
time: 126 us; the launch traced here: 124 us
  Pallas kernels  40.1 us (32%)
  starting transfers between devices  35 us (28%)
  waiting for transfers between devices  25.3 us (20%)
  blocking collectives  16.4 us (13%)
  local copies, waits for them, and re-layouts  4.15 us (3%)
  between operations  2.25 us (2%)
    pallas_call x5, Pallas kernels, call(): pl.pallas_call(kernel, out_shape=[jax.ShapeDtypeStruct(s, d) for s, d in...  40.1 us
    ppermute x12, starting transfers between devices, permute(): return lax.ppermute(value, AXES, pairs)  26.7 us
    all_to_all x1, blocking collectives, on_device(): lax.all_to_all(own, UNIT_AXES, split_axis=0, concat_axis=0, tiled=True)  16.4 us
    all_to_all x1, waiting for transfers between devices, on_device(): lax.all_to_all(packed, UNIT_AXES, split_axis=0, concat_axis=0, tiled=True)  15.3 us
    ppermute x12, waiting for transfers between devices, permute(): return lax.ppermute(value, AXES, pairs)  9.94 us
    all_to_all x1, starting transfers between devices, on_device(): lax.all_to_all(packed, UNIT_AXES, split_axis=0, concat_axis=0, tiled=True)  5.24 us
    all_to_all x1, starting transfers between devices, on_device(): norms = lax.all_to_all(norm, AXES, split_axis=0, concat_axis=0, tiled=True)  3.05 us
  transfers between devices with their start and end apart: 14, of which 3 were waited for; matrix products, arithmetic and copies ran while one was open for 1% of the time, Pallas kernels for 11%

profile of v2, /device:TPU:0, one launch (start us, length us, event | category | flops | bytes accessed | tf_op | source)
XLA Modules:
  0.0 124.3 jit_solution(9113429020242461826)
XLA Ops:
  0.6 0.7 stack.29.ids
  1.3 9.4 %shard_map.193 = (bf16[8,32,3968]{2,1,0:T(8,128)(2,1)}, f32[8,512]{1,0:T(8,128)}, s32[8,512]{1,0:T(8,128)}) custom-call(s32[8]{0:T(128)} %stack.29.ids, s32[1,512]{1,0:T(1,128)} %bitcast.37, f32[3,128]{1,0:T(4,128)} %disp.1, s32[4,512]{1,0:T(4,128)} %conn.3, f32[12,512]{1,0:T(8,128)} %grads.3, bf16[512,3072]{1,0:T(8,128)(2,1)} %state.1), custom_call_target="tpu_custom_call" | custom-call | tf_op jit(solution)/shard_map/pallas_call | solution.py:536
  10.8 5.2 %all-to-all-start = ((bf16[8,32,3968]{2,1,0:T(8,128)(2,1)}), bf16[8,32,3968]{2,1,0:T(8,128)(2,1)S(1)}, u32[]{:S(2)}, u32[]{:S(2)}) async-start(bf16[8,32,3968]{2,1,0:T(8,128)(2,1)} %get-tuple-element.37), calls=%async_computation | async-start | bytes 4063232 | tf_op jit(solution)/shard_map/all_to_all | solution.py:642
  16.7 0.0 copy-done.13
  16.7 0.0 copy-done.14
  16.7 0.6 pad.8.diag_normal
  17.3 0.6 pad.9.off_normal
  17.9 3.0 %shard_map.192 = (bf16[10,128,128]{2,1,0:T(8,128)(2,1)}, bf16[16,128,128]{2,1,0:T(8,128)(2,1)}, f32[96,128]{1,0:T(8,128)}, s32[8,128]{1,0:T(8,128)}) custom-call(s32[8]{0:T(128)} %stack.29.ids, s32[1,8]{1,0:T(1,128)} %vol.1, s32[1,32]{1,0:T(1,128)} %bitcast.38, s32[1,32]{1,0:T(1,128)} %bitcast.39, s32[1]{0:T(128)S(6)} %copy.30.off_count, ...), custom_call_target="tpu_custom_call" | custom-call | tf_op jit(solution)/shard_map/pallas_call | solution.py:536
  20.9 1.7 %collective-permute-start = (bf16[16,128,128]{2,1,0:T(8,128)(2,1)}, bf16[16,128,128]{2,1,0:T(8,128)(2,1)S(1)}, u32[]{:S(2)}, u32[]{:S(2)}) collective-permute-start(bf16[16,128,128]{2,1,0:T(8,128)(2,1)} %get-tuple-element.29), channel_id=1, source_target_pairs={{0,0},{5,1},{2,2},{7,3},{4,4},{1,5},{6,6},{3,7},{12,8},{9,9},{14,1... | collective-permute-start | bytes 1572872 | tf_op jit(solution)/shard_map/ppermute | solution.py:617
  22.6 1.6 %collective-permute-start.1 = (bf16[10,128,128]{2,1,0:T(8,128)(2,1)}, bf16[10,128,128]{2,1,0:T(8,128)(2,1)S(1)}, u32[]{:S(2)}, u32[]{:S(2)}) collective-permute-start(bf16[10,128,128]{2,1,0:T(8,128)(2,1)} %get-tuple-element.30), channel_id=1, source_target_pairs={{0,0},{5,1},{2,2},{7,3},{4,4},{1,5},{6,6},{3,7},{12,8},{9,9},{14,1... | collective-permute-start | bytes 983048 | tf_op jit(solution)/shard_map/ppermute | solution.py:617
  24.3 1.4 %collective-permute-start.2 = (f32[96,128]{1,0:T(8,128)}, f32[96,128]{1,0:T(8,128)S(1)}, u32[]{:S(2)}, u32[]{:S(2)}) collective-permute-start(f32[96,128]{1,0:T(8,128)} %get-tuple-element.31), channel_id=1, source_target_pairs={{0,0},{5,1},{2,2},{7,3},{4,4},{1,5},{6,6},{3,7},{12,8},{9,9},{14,1... | collective-permute-start | bytes 147464 | tf_op jit(solution)/shard_map/ppermute | solution.py:617
  25.7 1.3 %collective-permute-start.3 = (s32[8,128]{1,0:T(8,128)}, s32[8,128]{1,0:T(8,128)S(1)}, u32[]{:S(2)}, u32[]{:S(2)}) collective-permute-start(s32[8,128]{1,0:T(8,128)} %get-tuple-element.32), channel_id=1, source_target_pairs={{0,0},{5,1},{2,2},{7,3},{4,4},{1,5},{6,6},{3,7},{12,8},{9,9},{14,1... | collective-permute-start | bytes 12296 | tf_op jit(solution)/shard_map/ppermute | solution.py:617
  27.0 0.0 collective-permute-done.3.ints
  27.0 0.0 collective-permute-done.2.small
  27.0 0.0 copy-start.11
  27.0 0.0 collective-permute-done.1.blocks
  27.1 0.0 copy-start.3
  27.1 0.0 collective-permute-done.own
  27.1 0.0 copy-start.1
  27.1 1.6 %collective-permute-start.4 = (bf16[16,128,128]{2,1,0:T(8,128)(2,1)S(1)}, bf16[16,128,128]{2,1,0:T(8,128)(2,1)S(1)}, u32[]{:S(2)}, u32[]{:S(2)}) collective-permute-start(bf16[16,128,128]{2,1,0:T(8,128)(2,1)S(1)} %collective-permute-done.own), channel_id=1, source_target_pairs={{16,0},{17,1},{18,2},{19,3},{20,4},{21,5},{22,6},{23,7},{24,8},{25... | collective-permute-start | bytes 1572872 | tf_op jit(solution)/shard_map/ppermute | solution.py:617
  28.7 7.7 %collective-permute-done.4.other = bf16[16,128,128]{2,1,0:T(8,128)(2,1)S(1)} collective-permute-done((bf16[16,128,128]{2,1,0:T(8,128)(2,1)S(1)}, bf16[16,128,128]{2,1,0:T(8,128)(2,1)S(1)}, u32[]{:S(2)}, u32[]{:S(2)}) %collective-permute-start.4) | collective-permute-done | bytes 524320 | tf_op jit(solution)/shard_map/ppermute | solution.py:617
  36.3 15.3 %all-to-all-done.msgs = bf16[8,32,3968]{2,1,0:T(8,128)(2,1)S(1)} async-done(((bf16[8,32,3968]{2,1,0:T(8,128)(2,1)}), bf16[8,32,3968]{2,1,0:T(8,128)(2,1)S(1)}, u32[]{:S(2)}, u32[]{:S(2)}) %all-to-all-start) | async-done | bytes 2031648 | tf_op jit(solution)/shard_map/all_to_all | solution.py:642
  51.6 0.0 copy-done.12
  51.6 0.0 copy-done.11
  51.6 0.0 copy-done.3
  51.7 0.0 copy-done.1
  51.7 0.0 copy-done.2
  51.7 0.0 copy-start
  51.7 1.3 %copy-done = bf16[8,32,3968]{2,1,0:T(8,128)(2,1)} copy-done((bf16[8,32,3968]{2,1,0:T(8,128)(2,1)}, bf16[8,32,3968]{2,1,0:T(8,128)(2,1)S(1)}, u32[]{:S(2)}) %copy-start) | copy-done | bytes 2031640
  53.0 16.9 %shard_map.194 = (bf16[32,3840]{1,0:T(8,128)(2,1)}, bf16[32,3840]{1,0:T(8,128)(2,1)}, bf16[32,3840]{1,0:T(8,128)(2,1)}, bf16[32,3840]{1,0:T(8,128)(2,1)}, bf16[3...) custom-call(s32[8]{0:T(128)} %stack.29.ids, ...), custom_call_target="tpu_custom_call" | custom-call | tf_op jit(solution)/shard_map/pallas_call | solution.py:536
  69.8 12.0 %collective-permute-start.5 = (bf16[32,3840]{1,0:T(8,128)(2,1)}, bf16[32,3840]{1,0:T(8,128)(2,1)S(1)}, u32[]{:S(2)}, u32[]{:S(2)}) collective-permute-start(bf16[32,3840]{1,0:T(8,128)(2,1)} %get-tuple-element.39), channel_id=1, source_target_pairs={{8,0},{9,1},{10,2},{11,3},{12,4},{13,5},{14,6},{15,7},{0,8},{1,9},... | collective-permute-start | bytes 737288 | tf_op jit(solution)/shard_map/ppermute | solution.py:617
  81.8 0.0 collective-permute-start.6
  81.9 2.3 %collective-permute-start.7 = (bf16[32,3840]{1,0:T(8,128)(2,1)}, bf16[32,3840]{1,0:T(8,128)(2,1)S(1)}, u32[]{:S(2)}, u32[]{:S(2)}) collective-permute-start(bf16[32,3840]{1,0:T(8,128)(2,1)} %get-tuple-element.48), channel_id=1, source_target_pairs={{2,0},{3,1},{0,2},{1,3},{6,4},{7,5},{4,6},{5,7},{10,8},{11,9},{8,1... | collective-permute-start | bytes 737288 | tf_op jit(solution)/shard_map/ppermute | solution.py:617
  84.1 0.1 collective-permute-start.8
  84.3 0.0 collective-permute-start.9
  84.3 2.2 %collective-permute-done.5.refs_4_ = bf16[32,3840]{1,0:T(8,128)(2,1)S(1)} collective-permute-done((bf16[32,3840]{1,0:T(8,128)(2,1)}, bf16[32,3840]{1,0:T(8,128)(2,1)S(1)}, u32[]{:S(2)}, u32[]{:S(2)}) %collective-permute-start.5) | collective-permute-done | bytes 245792 | tf_op jit(solution)/shard_map/ppermute | solution.py:617
  86.5 4.6 %collective-permute-start.10 = (bf16[32,3840]{1,0:T(8,128)(2,1)}, bf16[32,3840]{1,0:T(8,128)(2,1)S(1)}, u32[]{:S(2)}, u32[]{:S(2)}) collective-permute-start(bf16[32,3840]{1,0:T(8,128)(2,1)} %get-tuple-element.52), channel_id=1, source_target_pairs={{10,0},{11,1},{8,2},{9,3},{14,4},{15,5},{12,6},{13,7},{2,8},{3,9},... | collective-permute-start | bytes 737288 | tf_op jit(solution)/shard_map/ppermute | solution.py:617
  91.1 0.0 collective-permute-done.6.refs_1_
  91.1 0.0 collective-permute-start.11
  91.1 16.4 %all_to_all.22.tangents = bf16[8,32,128]{2,1,0:T(8,128)(2,1)} all-to-all(bf16[8,32,128]{2,1,0:T(8,128)(2,1)} %get-tuple-element.40), channel_id=1, replica_groups=mesh['y'=2,'x'=2,'h'=2,'l'=2,'c'=2] {'x','l','c'}, dimensions={0} | all-to-all | bytes 131072 | tf_op jit(solution)/shard_map/all_to_all | solution.py:662
  107.5 3.0 %shard_map.195 = (f32[3,128]{1,0:T(4,128)}, f32[3,128]{1,0:T(4,128)}, f32[32,128]{1,0:T(8,128)}) custom-call(s32[8]{0:T(128)} %stack.29.ids, bf16[8,32,128]{2,1,0:T(8,128)(2,1)} %all_to_all.22.tangents, s32[8,512]{1,0:T(8,128)} %get-tuple-element.41.place, f32[8,512]{1,0:T(8,128)} %get-tuple-element.42.strain, f32[12,512]{1,0:T(8,128)} %grads.3, ...), custom_call_target="tpu_custom_call" | custom-call | tf_op jit(solution)/shard_map/pallas_call | solution.py:536
  110.5 3.1 %all-to-all-start.2 = ((f32[32,1,128]{2,1,0:T(1,128)}), f32[32,1,128]{2,1,0:T(1,128)S(1)}, u32[]{:S(2)}, u32[]{:S(2)}) async-start(f32[32,1,128]{2,1,0:T(1,128)} %bitcast.34), calls=%async_computation.2 | async-start | bytes 32768 | tf_op jit(solution)/shard_map/all_to_all | solution.py:671
  113.6 0.0 collective-permute-done.7.refs_2_
  113.6 0.0 copy-start.6
  113.6 0.0 collective-permute-done.8.refs_3_
  113.6 0.0 copy-start.7
  113.6 0.0 collective-permute-done.9.refs_5_
  113.6 0.0 copy-start.8
  113.7 0.0 collective-permute-done.10.refs_6_
  113.7 0.0 copy-start.9
  113.7 0.0 collective-permute-done.11.refs_7_
  113.7 0.0 copy-start.10
  113.7 0.0 copy-done.4
  113.7 0.0 copy-done.5
  113.7 0.6 copy-done.6
  114.3 0.1 copy-done.7
  114.4 0.1 copy-done.8
  114.5 0.1 copy-done.9
  114.6 0.1 copy-done.10
  114.7 7.8 %shard_map.196 = bf16[512,3072]{1,0:T(8,128)(2,1)} custom-call(s32[8]{0:T(128)} %stack.29.ids, s32[8,512]{1,0:T(8,128)} %get-tuple-element.41.place, bf16[8,32,128]{2,1,0:T(8,128)(2,1)} %all_to_all.22.tangents, bf16[32,3840]{1,0:T(8,128)(2,1)} %get-tuple-element.46.refs_0_, bf16[32,3840]{1,0:T(8,128)(2,1)} %copy-done.5, bf16[32,3840]{1,0:T(8,128)(2,1)} %copy-done.6, ...), custom_call_target="tpu_custom_call" | custom-call | tf_op jit(solution)/shard_map/pallas_call | solution.py:536
  122.4 0.0 all-to-all-done.2
  122.4 0.6 slice_reduce_fusion
  123.7 0.0 copy-done.15
  123.7 0.6 broadcast_multiply_fusion
  (9 shorter events, 0.0 us)
Async XLA Ops:
  1.3 15.3 %copy-start.13 = (f32[20,1,6]{0,1,2:T(1,128)S(1)}, f32[20,1,6]{0,1,2:T(1,128)}, u32[]{:S(2)}) copy-start(f32[20,1,6]{0,1,2:T(1,128)} %param.27) | copy-start | bytes 1444
  1.3 15.4 %copy-start.14 = (f32[32,1,6]{0,1,2:T(1,128)S(1)}, f32[32,1,6]{0,1,2:T(1,128)}, u32[]{:S(2)}) copy-start(f32[32,1,6]{0,1,2:T(1,128)} %param.31) | copy-start | bytes 2308
  10.8 40.9 %all-to-all-start = ((bf16[8,32,3968]{2,1,0:T(8,128)(2,1)}), bf16[8,32,3968]{2,1,0:T(8,128)(2,1)S(1)}, u32[]{:S(2)}, u32[]{:S(2)}) async-start(bf16[8,32,3968]{2,1,0:T(8,128)(2,1)} %get-tuple-element.37), calls=%async_computation | async-start | bytes 4063232 | tf_op jit(solution)/shard_map/all_to_all | solution.py:642
  20.9 6.1 %collective-permute-start = (bf16[16,128,128]{2,1,0:T(8,128)(2,1)}, bf16[16,128,128]{2,1,0:T(8,128)(2,1)S(1)}, u32[]{:S(2)}, u32[]{:S(2)}) collective-permute-start(bf16[16,128,128]{2,1,0:T(8,128)(2,1)} %get-tuple-element.29), channel_id=1, source_target_pairs={{0,0},{5,1},{2,2},{7,3},{4,4},{1,5},{6,6},{3,7},{12,8},{9,9},{14,1... | collective-permute-start | bytes 1572872 | tf_op jit(solution)/shard_map/ppermute | solution.py:617
  22.6 4.4 %collective-permute-start.1 = (bf16[10,128,128]{2,1,0:T(8,128)(2,1)}, bf16[10,128,128]{2,1,0:T(8,128)(2,1)S(1)}, u32[]{:S(2)}, u32[]{:S(2)}) collective-permute-start(bf16[10,128,128]{2,1,0:T(8,128)(2,1)} %get-tuple-element.30), channel_id=1, source_target_pairs={{0,0},{5,1},{2,2},{7,3},{4,4},{1,5},{6,6},{3,7},{12,8},{9,9},{14,1... | collective-permute-start | bytes 983048 | tf_op jit(solution)/shard_map/ppermute | solution.py:617
  24.3 2.8 %collective-permute-start.2 = (f32[96,128]{1,0:T(8,128)}, f32[96,128]{1,0:T(8,128)S(1)}, u32[]{:S(2)}, u32[]{:S(2)}) collective-permute-start(f32[96,128]{1,0:T(8,128)} %get-tuple-element.31), channel_id=1, source_target_pairs={{0,0},{5,1},{2,2},{7,3},{4,4},{1,5},{6,6},{3,7},{12,8},{9,9},{14,1... | collective-permute-start | bytes 147464 | tf_op jit(solution)/shard_map/ppermute | solution.py:617
  25.7 1.3 %collective-permute-start.3 = (s32[8,128]{1,0:T(8,128)}, s32[8,128]{1,0:T(8,128)S(1)}, u32[]{:S(2)}, u32[]{:S(2)}) collective-permute-start(s32[8,128]{1,0:T(8,128)} %get-tuple-element.32), channel_id=1, source_target_pairs={{0,0},{5,1},{2,2},{7,3},{4,4},{1,5},{6,6},{3,7},{12,8},{9,9},{14,1... | collective-permute-start | bytes 12296 | tf_op jit(solution)/shard_map/ppermute | solution.py:617
  27.0 24.6 %copy-start.12 = (s32[8,128]{1,0:T(8,128)}, s32[8,128]{1,0:T(8,128)S(1)}, u32[]{:S(2)}) copy-start(s32[8,128]{1,0:T(8,128)S(1)} %collective-permute-done.3.ints) | copy-start | bytes 12292
  27.0 24.6 %copy-start.11 = (f32[96,128]{1,0:T(8,128)}, f32[96,128]{1,0:T(8,128)S(1)}, u32[]{:S(2)}) copy-start(f32[96,128]{1,0:T(8,128)S(1)} %collective-permute-done.2.small) | copy-start | bytes 147460
  27.1 24.6 %copy-start.3 = (bf16[10,128,128]{2,1,0:T(8,128)(2,1)}, bf16[10,128,128]{2,1,0:T(8,128)(2,1)S(1)}, u32[]{:S(2)}) copy-start(bf16[10,128,128]{2,1,0:T(8,128)(2,1)S(1)} %collective-permute-done.1.blocks) | copy-start | bytes 983044
  27.1 24.6 %copy-start.1 = (bf16[16,128,128]{2,1,0:T(8,128)(2,1)}, bf16[16,128,128]{2,1,0:T(8,128)(2,1)S(1)}, u32[]{:S(2)}) copy-start(bf16[16,128,128]{2,1,0:T(8,128)(2,1)S(1)} %collective-permute-done.own) | copy-start | bytes 1572868
  27.1 9.2 %collective-permute-start.4 = (bf16[16,128,128]{2,1,0:T(8,128)(2,1)S(1)}, bf16[16,128,128]{2,1,0:T(8,128)(2,1)S(1)}, u32[]{:S(2)}, u32[]{:S(2)}) collective-permute-start(bf16[16,128,128]{2,1,0:T(8,128)(2,1)S(1)} %collective-permute-done.own), channel_id=1, source_target_pairs={{16,0},{17,1},{18,2},{19,3},{20,4},{21,5},{22,6},{23,7},{24,8},{25... | collective-permute-start | bytes 1572872 | tf_op jit(solution)/shard_map/ppermute | solution.py:617
  36.3 15.3 %copy-start.2 = (bf16[16,128,128]{2,1,0:T(8,128)(2,1)}, bf16[16,128,128]{2,1,0:T(8,128)(2,1)S(1)}, u32[]{:S(2)}) copy-start(bf16[16,128,128]{2,1,0:T(8,128)(2,1)S(1)} %collective-permute-done.4.other) | copy-start | bytes 1572868
  51.7 1.3 %copy-start = (bf16[8,32,3968]{2,1,0:T(8,128)(2,1)}, bf16[8,32,3968]{2,1,0:T(8,128)(2,1)S(1)}, u32[]{:S(2)}) copy-start(bf16[8,32,3968]{2,1,0:T(8,128)(2,1)S(1)} %all-to-all-done.msgs) | copy-start | bytes 6094852
  69.8 16.7 %collective-permute-start.5 = (bf16[32,3840]{1,0:T(8,128)(2,1)}, bf16[32,3840]{1,0:T(8,128)(2,1)S(1)}, u32[]{:S(2)}, u32[]{:S(2)}) collective-permute-start(bf16[32,3840]{1,0:T(8,128)(2,1)} %get-tuple-element.39), channel_id=1, source_target_pairs={{8,0},{9,1},{10,2},{11,3},{12,4},{13,5},{14,6},{15,7},{0,8},{1,9},... | collective-permute-start | bytes 737288 | tf_op jit(solution)/shard_map/ppermute | solution.py:617
  81.8 9.2 %collective-permute-start.6 = (bf16[32,3840]{1,0:T(8,128)(2,1)}, bf16[32,3840]{1,0:T(8,128)(2,1)S(1)}, u32[]{:S(2)}, u32[]{:S(2)}) collective-permute-start(bf16[32,3840]{1,0:T(8,128)(2,1)} %get-tuple-element.47), channel_id=1, source_target_pairs={{1,0},{0,1},{3,2},{2,3},{5,4},{4,5},{7,6},{6,7},{9,8},{8,9},{11,10... | collective-permute-start | bytes 737288 | tf_op jit(solution)/shard_map/ppermute | solution.py:617
  81.9 31.7 %collective-permute-start.7 = (bf16[32,3840]{1,0:T(8,128)(2,1)}, bf16[32,3840]{1,0:T(8,128)(2,1)S(1)}, u32[]{:S(2)}, u32[]{:S(2)}) collective-permute-start(bf16[32,3840]{1,0:T(8,128)(2,1)} %get-tuple-element.48), channel_id=1, source_target_pairs={{2,0},{3,1},{0,2},{1,3},{6,4},{7,5},{4,6},{5,7},{10,8},{11,9},{8,1... | collective-permute-start | bytes 737288 | tf_op jit(solution)/shard_map/ppermute | solution.py:617
  84.1 29.5 %collective-permute-start.8 = (bf16[32,3840]{1,0:T(8,128)(2,1)}, bf16[32,3840]{1,0:T(8,128)(2,1)S(1)}, u32[]{:S(2)}, u32[]{:S(2)}) collective-permute-start(bf16[32,3840]{1,0:T(8,128)(2,1)} %get-tuple-element.49), channel_id=1, source_target_pairs={{3,0},{2,1},{1,2},{0,3},{7,4},{6,5},{5,6},{4,7},{11,8},{10,9},{9,1... | collective-permute-start | bytes 737288 | tf_op jit(solution)/shard_map/ppermute | solution.py:617
  84.3 29.4 %collective-permute-start.9 = (bf16[32,3840]{1,0:T(8,128)(2,1)}, bf16[32,3840]{1,0:T(8,128)(2,1)S(1)}, u32[]{:S(2)}, u32[]{:S(2)}) collective-permute-start(bf16[32,3840]{1,0:T(8,128)(2,1)} %get-tuple-element.51), channel_id=1, source_target_pairs={{9,0},{8,1},{11,2},{10,3},{13,4},{12,5},{15,6},{14,7},{1,8},{0,9},... | collective-permute-start | bytes 737288 | tf_op jit(solution)/shard_map/ppermute | solution.py:617
  86.5 27.2 %copy-start.4 = (bf16[32,3840]{1,0:T(8,128)(2,1)}, bf16[32,3840]{1,0:T(8,128)(2,1)S(1)}, u32[]{:S(2)}) copy-start(bf16[32,3840]{1,0:T(8,128)(2,1)S(1)} %collective-permute-done.5.refs_4_) | copy-start | bytes 737284
  86.5 27.1 %collective-permute-start.10 = (bf16[32,3840]{1,0:T(8,128)(2,1)}, bf16[32,3840]{1,0:T(8,128)(2,1)S(1)}, u32[]{:S(2)}, u32[]{:S(2)}) collective-permute-start(bf16[32,3840]{1,0:T(8,128)(2,1)} %get-tuple-element.52), channel_id=1, source_target_pairs={{10,0},{11,1},{8,2},{9,3},{14,4},{15,5},{12,6},{13,7},{2,8},{3,9},... | collective-permute-start | bytes 737288 | tf_op jit(solution)/shard_map/ppermute | solution.py:617
  91.1 22.6 %copy-start.5 = (bf16[32,3840]{1,0:T(8,128)(2,1)}, bf16[32,3840]{1,0:T(8,128)(2,1)S(1)}, u32[]{:S(2)}) copy-start(bf16[32,3840]{1,0:T(8,128)(2,1)S(1)} %collective-permute-done.6.refs_1_) | copy-start | bytes 737284
  91.1 22.6 %collective-permute-start.11 = (bf16[32,3840]{1,0:T(8,128)(2,1)}, bf16[32,3840]{1,0:T(8,128)(2,1)S(1)}, u32[]{:S(2)}, u32[]{:S(2)}) collective-permute-start(bf16[32,3840]{1,0:T(8,128)(2,1)} %get-tuple-element.53), channel_id=1, source_target_pairs={{11,0},{10,1},{9,2},{8,3},{15,4},{14,5},{13,6},{12,7},{3,8},{2,9},... | collective-permute-start | bytes 737288 | tf_op jit(solution)/shard_map/ppermute | solution.py:617
  110.5 13.2 %copy-start.15 = (f32[3,128]{1,0:T(4,128)S(1)}, f32[3,128]{1,0:T(4,128)}, u32[]{:S(2)}) copy-start(f32[3,128]{1,0:T(4,128)} %get-tuple-element.25) | copy-start | bytes 4612
  110.5 11.9 %all-to-all-start.2 = ((f32[32,1,128]{2,1,0:T(1,128)}), f32[32,1,128]{2,1,0:T(1,128)S(1)}, u32[]{:S(2)}, u32[]{:S(2)}) async-start(f32[32,1,128]{2,1,0:T(1,128)} %bitcast.34), calls=%async_computation.2 | async-start | bytes 32768 | tf_op jit(solution)/shard_map/all_to_all | solution.py:671
  113.6 0.7 copy-start.6
  113.6 0.8 copy-start.7
  113.6 0.8 copy-start.8
  113.7 0.9 copy-start.9
  113.7 1.0 copy-start.10

commit v3 on v2

--- a/solution.py
+++ b/solution.py
@@ -24,6 +24,8 @@
 STATE_LANES = 5 * LEVEL
 MSG_LANES = STATE_LANES + 128
 GAIN_NORMAL = 0.4
+WIDE = 8
+CHUNK = 256
 CLIP_RMS = 1.0
 SM_NORMAL = 80
 SM_AFFINE = 88
@@ -70,6 +72,11 @@
     target = iota((1, LEVEL), 1)
     source = COMPS * (target % BS) + target // BS
     return jnp.where(iota((LEVEL, LEVEL), 0) == source, 1.0, 0.0).astype(BF16)
+
+
+def lane_order_back():
+    row = iota((LEVEL, 1), 0)
+    return jnp.where(iota((LEVEL, LEVEL), 1) == COMPS * (row % BS) + row // BS, 1.0, 0.0).astype(BF16)
 
 
 def class_onehot(slot, size, level_rows):
@@ -122,15 +129,17 @@
 
 
 def matrix_pack_kernel(
-    ids, vol, off_row, off_col, off_count, coupling, diag_normal, off_normal, affine, diag, off,
-    diag_out, off_out, small, ints, row_local, row_size, rows_sel, seen, sems,
+    ids, vol, off_row, off_col, off_count, coupling, diag_normal, off_normal, affine, diag,
+    diag_out, small, ints, row_local, row_size, rows_sel, seen, sems,
 ):
     half = ids[0]
-    off_copy = pltpu.make_async_copy(
-        off.at[pl.ds(half * HALF_OFF, HALF_OFF)], off_out, sems.at[HALF_ROWS]
-    )
-    off_copy.start()
     small[...] = jnp.zeros_like(small)
+    small[0:VOL_GRP, 0:36] = affine[...]
+    target = iota((1, BS), 1) % 64
+    source = jnp.where(jnp.logical_and(target % 8 < 6, target < 48), 6 * (target % 8) + target // 8, -1)
+    shift = jnp.where(iota((BS, BS), 0) == source, 1.0, 0.0).astype(BF16)
+    moved = sum(dot_nn(part, shift) for part in split3(small[0:VOL_GRP, :]))
+    small[0:VOL_GRP, :] = jnp.zeros((VOL_GRP, BS), F32)
     for size in range(NBMAX + 1):
         seen[size] = 0
     start = 0
@@ -152,11 +161,11 @@
 
         @pl.when(mine)
         def _(size=size, v=v):
-            small[pl.ds(SM_AFFINE - 1 + size, 1), 0:36] = affine[v : v + 1, :]
+            small[pl.ds(SM_AFFINE - 1 + size, 1), :] = moved[v : v + 1, :]
             ints[6, size - 1] = v
 
         start = start + size
-    copies = [off_copy]
+    copies = []
     for i in range(HALF_ROWS):
         copies.append(
             pltpu.make_async_copy(diag.at[pl.ds(rows_sel[i], 1)], diag_out.at[pl.ds(i, 1)], sems.at[i])
@@ -169,26 +178,22 @@
         row = rows_sel[i]
         small[8 * i : 8 * i + COMPS, :] = coupling[pl.ds(COMPS * row, COMPS), :]
         normals += jnp.where(lane == i, pltpu.roll(diag_rows, (i - row + BS) % BS, 1), 0.0)
-    off_rows = off_normal[...]
-    direct = pltpu.roll(off_rows, HALF_OFF, 1)
-    swapped = jnp.where(lane < 2 * HALF_OFF, off_rows, pltpu.roll(off_rows, 2 * HALF_OFF, 1))
-    chosen = jnp.where(half == 0, direct, swapped)
-    normals += jnp.where(jnp.logical_and(lane >= HALF_OFF, lane < HALF_OFF + OFF_GRP), chosen, 0.0)
+    normals += pltpu.roll(off_normal[...], HALF_OFF, 1)
     small[SM_NORMAL : SM_NORMAL + 8, :] = normals
     live_total = off_count[0]
 
     def contact(n, found):
-        slot = (n + half * HALF_OFF) % OFF_GRP
-        row = off_row[0, slot]
+        row = off_row[0, n]
         local = row_local[row]
+        ints[4, n] = jnp.maximum(local, 0)
         ints[5, n] = row_size[row]
-        live = jnp.logical_and(slot < live_total, local >= 0)
+        live = jnp.logical_and(n < live_total, local >= 0)
 
         @pl.when(live)
         def _():
             ints[1, found] = n
             ints[2, found] = local
-            ints[3, found] = row_local[off_col[0, slot]]
+            ints[3, found] = row_local[off_col[0, n]]
 
         return found + live.astype(I32)
 
@@ -278,9 +283,14 @@
                 ]
 
 
-def solve_kernel(ids, ints, small, blocks, own, other, msgs, *refs):
+def transpose_kernel(off, turned):
+    for n in range(OFF_GRP):
+        turned[n] = jnp.transpose(off[n])
+
+
+def solve_kernel(ids, ints, small, blocks, off, msgs, *refs):
     outs, refs = refs[:UNIT], refs[UNIT:]
-    tangents, state, low, acc, contact_scale, diag_scale, inverse, response, diag_pairs, off_pairs = refs
+    tangents, state, low, rest, contact_scale, inverse, response, diag_pairs, off_pairs = refs
     extras = []
     for rank in range(NBMAX):
         row0 = CLASS_PLACE[rank][1]
@@ -336,16 +346,17 @@
         dots = dot_nn(strains, parts[0]) + dot_nn(strains, parts[1]) + dot_nn(strains, parts[2])
         response[c] = 1.0 + GAIN_NORMAL * jnp.tanh(dots)
     eye = iota((BS, BS), 0) == iota((BS, BS), 1)
+    diag_inverse = []
     for c in range(NBMAX):
         for a in range(c + 1):
             r = CLASS_BASE[c] + a
-            scale = jnp.broadcast_to(response[c, :, r : r + 1], (SLOTS, BS))
-            diag_scale[r] = scale
             values = jnp.sum(jnp.where(eye, blocks[r].astype(F32), 0.0), axis=0, keepdims=True)
-            inverse[r] = 1.0 / (scale * values)
+            diag_inverse.append(1.0 / values)
+            inverse[r] = jnp.broadcast_to(1.0 / response[c, :, r : r + 1], (SLOTS, BS)) * diag_inverse[r]
     for n in range(OFF_GRP):
-        contact_scale[n] = jnp.broadcast_to(
-            response[ints[5, n], :, HALF_OFF + n : HALF_OFF + n + 1], (SLOTS, BS)
+        contact_scale[n] = (
+            jnp.broadcast_to(response[ints[5, n], :, HALF_OFF + n : HALF_OFF + n + 1], (SLOTS, BS))
+            * inverse[ints[4, n]]
         )
     zero = jnp.zeros((BS, BS), BF16)
     for p in range(HALF_ROWS // 2):
@@ -354,98 +365,86 @@
         diag_pairs[p, BS:, :BS] = zero
         diag_pairs[p, BS:, BS:] = blocks[2 * p + 1]
     live = ints[0, 0]
-    pairs = (live + 1) // 2
-
-    def contact_block(n):
-        mine = n < HALF_OFF
-        return jnp.where(mine, own[jnp.where(mine, n, 0)], other[jnp.where(mine, 0, n - HALF_OFF)])
+    turns = (live + WIDE - 1) // WIDE
+
+    def contact_block(m):
+        n = ints[1, jnp.minimum(m, live - 1)]
+        found = off[n]
+        return jnp.where(m < live, found, zero)
 
     def fill(p, carry):
-        off_pairs[p, :BS, :BS] = contact_block(ints[1, 2 * p])
+        off_pairs[p, :BS, :BS] = contact_block(2 * p)
         off_pairs[p, :BS, BS:] = zero
         off_pairs[p, BS:, :BS] = zero
-        has_second = 2 * p + 1 < live
-
-        @pl.when(has_second)
-        def _():
-            off_pairs[p, BS:, BS:] = contact_block(ints[1, 2 * p + 1])
-
-        @pl.when(jnp.logical_not(has_second))
-        def _():
-            off_pairs[p, BS:, BS:] = zero
-
+        off_pairs[p, BS:, BS:] = contact_block(2 * p + 1)
         return carry
 
-    lax.fori_loop(0, pairs, fill, 0)
-
-    def sweep(step, carry):
+    lax.fori_loop(0, turns * (WIDE // 2), fill, 0)
+
+    def contacts(t, carry):
+        slots = [jnp.minimum(WIDE * t + i, live - 1) for i in range(WIDE)]
+        cols = [ints[3, m] for m in slots]
+        rows = [ints[2, m] for m in slots]
+        which = [ints[1, m] for m in slots]
+        for base in range(0, COMPS * SLOTS, CHUNK):
+            span = slice(base, base + CHUNK)
+            products = []
+            for h in range(WIDE // 2):
+                both = jnp.concatenate([low[cols[2 * h], span, :], low[cols[2 * h + 1], span, :]], axis=1)
+                products.append(dot_nn(both, off_pairs[(WIDE // 2) * t + h]))
+            for i in range(WIDE):
+                scale = contact_scale[which[i]]
+                for j in range(CHUNK // SLOTS):
+                    part = products[i // 2][SLOTS * j : SLOTS * (j + 1), BS * (i % 2) : BS * (i % 2 + 1)]
+                    state[rows[i], base + SLOTS * j : base + SLOTS * (j + 1), :] -= part * scale
+        return carry
+
+    def sweep(last):
+        lax.fori_loop(0, turns, contacts, 0)
         for p in range(HALF_ROWS // 2):
-            both = jnp.concatenate([low[2 * p], low[2 * p + 1]], axis=1)
-            product = dot_nt(both, diag_pairs[p])
-            for i in range(2):
-                r = 2 * p + i
-                scale = diag_scale[r]
-                for j in range(COMPS):
-                    rows = slice(SLOTS * j, SLOTS * (j + 1))
-                    acc[r, rows, :] = product[rows, BS * i : BS * (i + 1)] * scale
-
-        def contact(p, inner):
-            second = jnp.minimum(2 * p + 1, live - 1)
-            slots = (2 * p, second)
-            both = jnp.concatenate([low[ints[3, m]] for m in slots], axis=1)
-            product = dot_nt(both, off_pairs[p])
-            for i, m in enumerate(slots):
-                r = ints[2, m]
-                scale = contact_scale[ints[1, m]]
-                for j in range(COMPS):
-                    rows = slice(SLOTS * j, SLOTS * (j + 1))
-                    acc[r, rows, :] += product[rows, BS * i : BS * (i + 1)] * scale
-            return inner
-
-        lax.fori_loop(0, pairs, contact, 0)
-        for r in range(HALF_ROWS):
-            inv = inverse[r]
-            for j in range(COMPS):
-                rows = slice(SLOTS * j, SLOTS * (j + 1))
-                load = small[8 * r + j : 8 * r + j + 1, :]
-                value = state[r, rows, :] + (load - acc[r, rows, :]) * inv
-                state[r, rows, :] = value
-                low[r, rows, :] = value.astype(BF16)
-        return carry
-
-    lax.fori_loop(0, SWEEPS, sweep, 0)
+            for base in range(0, COMPS * SLOTS, CHUNK):
+                span = slice(base, base + CHUNK)
+                both = jnp.concatenate([low[2 * p, span, :], low[2 * p + 1, span, :]], axis=1)
+                product = dot_nt(both, diag_pairs[p])
+                for i in range(2):
+                    r = 2 * p + i
+                    for j in range(CHUNK // SLOTS):
+                        comp = base // SLOTS + j
+                        at = slice(SLOTS * comp, SLOTS * (comp + 1))
+                        part = product[SLOTS * j : SLOTS * (j + 1), BS * i : BS * (i + 1)]
+                        load = small[8 * r + comp : 8 * r + comp + 1, :]
+                        value = state[r, at, :] + (load * inverse[r] - part * diag_inverse[r])
+                        high = value.astype(BF16)
+                        low[r, at, :] = high
+                        if last:
+                            rest[r, at, :] = (value - high.astype(F32)).astype(BF16)
+                        else:
+                            state[r, at, :] = value
+
+    lax.fori_loop(0, SWEEPS - 1, lambda step, carry: (sweep(False), carry)[1], 0)
+    sweep(True)
     lane = iota((1, BS), 1)
-    comp = lane // 8
+    entries = []
     for c in range(NBMAX):
-        total = jnp.zeros((SLOTS, BS), F32)
+        weights, values = [], []
         for a in range(c + 1):
             r = CLASS_BASE[c] + a
             load8 = small[8 * r : 8 * r + 8, :]
-            tiled = jnp.concatenate([load8] * 6 + [jnp.zeros((80, BS), F32)], axis=0)
-            weights = jnp.concatenate(split3(tiled)[:2], axis=0)
-            value = state[r]
-            high = value.astype(BF16)
-            rest = (value - high.astype(F32)).astype(BF16)
-            product = dot_nt(high, weights) + dot_nt(rest, weights)
-            product = product[:, :BS] + product[:, BS:]
-            for j in range(COMPS):
-                total += jnp.where(comp == j, product[SLOTS * j : SLOTS * (j + 1)], 0.0)
-        source = iota((BS, BS), 0)
-        target = iota((BS, BS), 1)
-        wanted = jnp.logical_and(
-            source == 6 * (target % 8) + target // 8, jnp.logical_and(target % 8 < 6, target < 48)
-        )
-        moved = jnp.sum(
-            jnp.where(wanted, jnp.transpose(jnp.broadcast_to(small[SM_AFFINE + c : SM_AFFINE + c + 1, :], (BS, BS))), 0.0),
-            axis=0,
-            keepdims=True,
-        )
+            high = load8.astype(BF16).astype(F32)
+            gap = jnp.zeros((16, BS), F32)
+            both = jnp.concatenate([high] * 6 + [gap] + [load8 - high] * 6 + [gap], axis=0).astype(BF16)
+            weights += [both, both]
+            values += [low[r], rest[r]]
+        product = dot_nt(jnp.concatenate(values, axis=1), jnp.concatenate(weights, axis=1))
+        total = jnp.zeros((SLOTS, BS), F32)
+        for j in range(COMPS):
+            total = jnp.where((lane // 8) % 8 == j, product[SLOTS * j : SLOTS * (j + 1)], total)
+        total = total + pltpu.roll(total, 64, 1)
         found = sum(jnp.where(held[c][rank], rank + 1.0, 0.0) for rank in range(NBMAX))
-        acc[c, :SLOTS, :] = jnp.where(lane == RANK_LANE, found, moved - total / ((c + 1) * BS))
+        entry = small[SM_AFFINE + c : SM_AFFINE + c + 1, :] - total / ((c + 1) * BS)
+        entries.append(jnp.where(lane % 64 == RANK_LANE, found, entry))
     for row0, one, two in ((0, 3, 0), (TILE, 2, 1)):
-        first = acc[one, :SLOTS, :]
-        second = acc[two, :SLOTS, :]
-        packed = jnp.where(lane < 64, first, pltpu.roll(second, 64, 1)).astype(BF16)
+        packed = jnp.where(lane < 64, entries[one], entries[two]).astype(BF16)
         for k in range(UNIT):
             tangents[ids[5] ^ k, row0 : row0 + TILE, :] = packed[TILE * k : TILE * (k + 1)]
     for c in range(NBMAX):
@@ -506,8 +505,8 @@
 def unpack_kernel(ids, place, tangents, *refs):
     msgs, (out, out_vmem, sems) = refs[:UNIT], refs[UNIT:]
     slot, size = place[0:1, :], place[1:2, :]
-    order = lane_order()
-    hots = returned_onehots(ids, tangents, slot, size)[1]
+    order = lane_order_back()
+    hots = [jnp.transpose(hot) for hot in returned_onehots(ids, tangents, slot, size)[1]]
     copies = []
     for a in range(NBMAX):
         pieces = []
@@ -515,9 +514,9 @@
             lane0, row0 = CLASS_PLACE[c]
             lane = lane0 + LEVEL * a
             rows = jnp.concatenate([msgs[k][row0 : row0 + TILE, lane : lane + LEVEL] for k in range(UNIT)], axis=0)
-            pieces.append(dot_nt(rows, order).astype(BF16))
-        hot = jnp.concatenate(hots[a:], axis=0)
-        out_vmem[a] = dot_tn(hot, jnp.concatenate(pieces, axis=0)).astype(BF16)
+            pieces.append(dot_nn(rows, order).astype(BF16))
+        hot = jnp.concatenate(hots[a:], axis=1)
+        out_vmem[a] = dot_nn(hot, jnp.concatenate(pieces, axis=0)).astype(BF16)
         copy = pltpu.make_async_copy(out_vmem.at[a], out.at[:, pl.ds(LEVEL * a, LEVEL)], sems.at[a])
         copy.start()
         copies.append(copy)
@@ -532,7 +531,7 @@
 VM, SM, HB = pltpu.VMEM, pltpu.SMEM, pl.ANY
 
 
-def call(kernel, args, spaces, outs, out_spaces, scratch):
+def call(kernel, args, spaces, outs, out_spaces, scratch, cost=None):
     return pl.pallas_call(
         kernel,
         out_shape=[jax.ShapeDtypeStruct(s, d) for s, d in outs],
@@ -540,6 +539,7 @@
         out_specs=[spec(s) for s in out_spaces],
         scratch_shapes=scratch,
         compiler_params=pltpu.CompilerParams(vmem_limit_bytes=VMEM_LIMIT),
+        cost_estimate=cost,
     )(*args)
 
 
@@ -547,15 +547,14 @@
     return call(
         solve_kernel,
         args,
-        (SM, SM) + (VM,) * 5,
+        (SM, SM) + (VM,) * 4,
         tuple(((2 * TILE, STATE_LANES), BF16) for _ in range(UNIT)) + (((UNIT, 2 * TILE, BS), BF16),),
         (VM,) * (UNIT + 1),
         [
             pltpu.VMEM((HALF_ROWS, COMPS * SLOTS, BS), F32),
             pltpu.VMEM((HALF_ROWS, COMPS * SLOTS, BS), BF16),
-            pltpu.VMEM((HALF_ROWS, COMPS * SLOTS, BS), F32),
+            pltpu.VMEM((HALF_ROWS, COMPS * SLOTS, BS), BF16),
             pltpu.VMEM((OFF_GRP, SLOTS, BS), F32),
-            pltpu.VMEM((HALF_ROWS, SLOTS, BS), F32),
             pltpu.VMEM((HALF_ROWS, SLOTS, BS), F32),
             pltpu.VMEM((NBMAX, SLOTS, BS), F32),
             pltpu.VMEM((HALF_ROWS // 2, 2 * BS, 2 * BS), BF16),
@@ -622,18 +621,18 @@
     def normal_rows(normals):
         return jnp.pad(normals.transpose(2, 1, 0)[:, 0], ((0, 2), (0, BS - normals.shape[0])))
 
-    diag_half, off_half, small, ints = call(
+    diag_half, small, ints = call(
         matrix_pack_kernel,
         (
             ids, vol_blocks, off_row.T, off_col.T, off_count, coupling.reshape(ROWS_GRP * COMPS, BS),
-            normal_rows(diag_normal), normal_rows(off_normal), c_affine[0], diag_blocks[:, 0], off_blocks[:, 0],
+            normal_rows(diag_normal), normal_rows(off_normal), c_affine[0], diag_blocks[:, 0],
         ),
-        (SM, SM, SM, SM, SM, VM, VM, VM, VM, HB, HB),
-        (((HALF_ROWS, BS, BS), BF16), ((HALF_OFF, BS, BS), BF16), ((SM_ROWS, BS), F32), ((8, BS), I32)),
-        (VM, VM, VM, SM),
+        (SM, SM, SM, SM, SM, VM, VM, VM, VM, HB),
+        (((HALF_ROWS, BS, BS), BF16), ((SM_ROWS, BS), F32), ((8, BS), I32)),
+        (VM, VM, SM),
         [
             pltpu.SMEM((32,), I32), pltpu.SMEM((32,), I32), pltpu.SMEM((16,), I32), pltpu.SMEM((8,), I32),
-            pltpu.SemaphoreType.DMA((HALF_ROWS + 1,)),
+            pltpu.SemaphoreType.DMA((HALF_ROWS,)),
         ],
     )
     packed, strain, place = pack_call(
@@ -646,11 +645,19 @@
         def from_group(y, x, h, l, c, turn=turn):
             return y, x, (h + 2 * turn + (x ^ c)) % z_count, l, c
 
-        mine_t, diag_t, small_t, ints_t = lax.optimization_barrier(
-            tuple(permute(value, from_group) for value in (off_half, diag_half, small, ints))
+        off_t, diag_t, small_t, ints_t = [
+            permute(value, from_group) for value in (off_blocks[:, 0], diag_half, small, ints)
+        ]
+        (off_t,) = call(
+            transpose_kernel,
+            (off_t,),
+            (VM,),
+            (((OFF_GRP, BS, BS), BF16),),
+            (VM,),
+            [],
+            pl.CostEstimate(flops=60_000_000_000, bytes_accessed=200_000_000, transcendentals=0),
         )
-        other_t = permute(mine_t, lambda y, x, h, l, c: (1 - y, x, h, l, c))
-        result = solve_call(ids, ints_t, small_t, diag_t, mine_t, other_t, msgs)
+        result = solve_call(ids, ints_t, small_t, diag_t, off_t, msgs)
         if solved is None:
             solved = result
         else:

time: 126 us -> 114 us (0.905); the launches traced: 124 us -> 114 us
  blocking collectives: 16.4 us -> 10.4 us
  starting transfers between devices: 35 us -> 29.5 us
  Pallas kernels: 40.1 us -> 35.5 us
  waiting for transfers between devices: 25.3 us -> 29.8 us
    ppermute x12 -> x11, starting transfers between devices: 26.7 us -> 15.2 us  [permute(): return lax.ppermute(value, AXES, pairs)]
    all_to_all x1, waiting for transfers between devices: 15.3 us -> 24.7 us  [on_device(): lax.all_to_all(packed, UNIT_AXES, split_axis=0, concat_axis=0, tiled=True)]
    all_to_all x1, blocking collectives: 16.4 us -> 10.4 us  [on_device(): lax.all_to_all(own, UNIT_AXES, split_axis=0, concat_axis=0, tiled=True)]
    ppermute x12 -> x11, waiting for transfers between devices: 9.94 us -> 4.82 us  [permute(): return lax.ppermute(value, AXES, pairs)]
    pallas_call x5 -> x6, Pallas kernels: 40.1 us -> 35.5 us  [call(): pl.pallas_call(kernel, out_shape=[jax.ShapeDtypeStruct(s, d) for s, d in...]
    all_to_all x1, starting transfers between devices: 3.05 us -> 6.51 us  [on_device(): norms = lax.all_to_all(norm, AXES, split_axis=0, concat_axis=0, tiled=True)]
    all_to_all x1, starting transfers between devices: 5.24 us -> 7.85 us  [on_device(): lax.all_to_all(packed, UNIT_AXES, split_axis=0, concat_axis=0, tiled=True)]
    unnamed x34 -> x32, local copies, waits for them, and re-layouts: 2.28 us -> 3.25 us
  transfers between devices with their start and end apart: 14 -> 13, of which waited for: 3 -> 4; matrix products, arithmetic and copies ran while one was open for 1% -> 2% of each run, Pallas kernels for 11% -> 21%
where the time goes in v3:
time: 114 us
  Pallas kernels  35.5 us (31%)
  waiting for transfers between devices  29.8 us (26%)
  starting transfers between devices  29.5 us (26%)
  blocking collectives  10.4 us (9%)
  local copies, waits for them, and re-layouts  5.11 us (4%)
  between operations  2.2 us (2%)
  other arithmetic  1.18 us (1%)
    pallas_call x6, Pallas kernels, call(): pl.pallas_call(kernel, out_shape=[jax.ShapeDtypeStruct(s, d) for s, d in...  35.5 us
    all_to_all x1, waiting for transfers between devices, on_device(): lax.all_to_all(packed, UNIT_AXES, split_axis=0, concat_axis=0, tiled=True)  24.7 us
    ppermute x11, starting transfers between devices, permute(): return lax.ppermute(value, AXES, pairs)  15.2 us
    all_to_all x1, blocking collectives, on_device(): lax.all_to_all(own, UNIT_AXES, split_axis=0, concat_axis=0, tiled=True)  10.4 us
    all_to_all x1, starting transfers between devices, on_device(): lax.all_to_all(packed, UNIT_AXES, split_axis=0, concat_axis=0, tiled=True)  7.85 us
    all_to_all x1, starting transfers between devices, on_device(): norms = lax.all_to_all(norm, AXES, split_axis=0, concat_axis=0, tiled=True)  6.51 us
    ppermute x11, waiting for transfers between devices, permute(): return lax.ppermute(value, AXES, pairs)  4.82 us
    unnamed x32, local copies, waits for them, and re-layouts  3.25 us
  transfers between devices with their start and end apart: 13, of which 4 were waited for; matrix products, arithmetic and copies ran while one was open for 2% of the time, Pallas kernels for 21%

profile of v3, /device:TPU:0, one launch (start us, length us, event | category | flops | bytes accessed | tf_op | source)
XLA Modules:
  0.0 113.7 jit_solution(4719641555816226031)
XLA Ops:
  0.6 1.9 %collective-permute-start.3 = (bf16[32,128,128]{2,1,0:T(8,128)(2,1)}, bf16[32,128,128]{2,1,0:T(8,128)(2,1)S(1)}, u32[]{:S(2)}, u32[]{:S(2)}) collective-permute-start(bf16[32,128,128]{2,1,0:T(8,128)(2,1)} %bitcast.39), channel_id=1, source_target_pairs={{0,0},{5,1},{2,2},{7,3},{4,4},{1,5},{6,6},{3,7},{12,8},{9,9},{14,1... | collective-permute-start | bytes 3145736 | tf_op jit(solution)/shard_map/ppermute | solution.py:616
  2.5 0.7 stack.29.ids
  3.2 0.0 copy-start.12
  3.2 9.5 %shard_map.194 = (bf16[8,32,3968]{2,1,0:T(8,128)(2,1)}, f32[8,512]{1,0:T(8,128)}, s32[8,512]{1,0:T(8,128)}) custom-call(s32[8]{0:T(128)} %stack.29.ids, s32[1,512]{1,0:T(1,128)} %bitcast.36, f32[3,128]{1,0:T(4,128)} %disp.1, s32[4,512]{1,0:T(4,128)} %conn.3, f32[12,512]{1,0:T(8,128)} %grads.3, bf16[512,3072]{1,0:T(8,128)(2,1)} %state.1), custom_call_target="tpu_custom_call" | custom-call | tf_op jit(solution)/shard_map/pallas_call | solution.py:535
  12.7 7.9 %all-to-all-start = ((bf16[8,32,3968]{2,1,0:T(8,128)(2,1)}), bf16[8,32,3968]{2,1,0:T(8,128)(2,1)S(1)}, u32[]{:S(2)}, u32[]{:S(2)}) async-start(bf16[8,32,3968]{2,1,0:T(8,128)(2,1)} %get-tuple-element.27), calls=%async_computation | async-start | bytes 4063232 | tf_op jit(solution)/shard_map/all_to_all | solution.py:641
  20.5 0.0 copy-done.11
  20.5 0.0 copy-done.12
  20.5 0.6 pad.8.diag_normal
  21.1 0.6 pad.9.off_normal
  22.4 2.8 %shard_map.192 = (bf16[10,128,128]{2,1,0:T(8,128)(2,1)}, f32[96,128]{1,0:T(8,128)}, s32[8,128]{1,0:T(8,128)}) custom-call(s32[8]{0:T(128)} %stack.29.ids, s32[1,8]{1,0:T(1,128)} %vol.1, s32[1,32]{1,0:T(1,128)} %bitcast.37, s32[1,32]{1,0:T(1,128)} %bitcast.38, s32[1]{0:T(128)S(6)} %copy.30.off_count, f32[120,128]{1,0:T(8,128)} %bitcast.30, ...), custom_call_target="tpu_custom_call" | custom-call | tf_op jit(solution)/shard_map/pallas_call | solution.py:535
  25.2 1.6 %collective-permute-start.2 = (bf16[10,128,128]{2,1,0:T(8,128)(2,1)}, bf16[10,128,128]{2,1,0:T(8,128)(2,1)S(1)}, u32[]{:S(2)}, u32[]{:S(2)}) collective-permute-start(bf16[10,128,128]{2,1,0:T(8,128)(2,1)} %get-tuple-element.26), channel_id=1, source_target_pairs={{0,0},{5,1},{2,2},{7,3},{4,4},{1,5},{6,6},{3,7},{12,8},{9,9},{14,1... | collective-permute-start | bytes 983048 | tf_op jit(solution)/shard_map/ppermute | solution.py:616
  26.9 1.4 %collective-permute-start.1 = (f32[96,128]{1,0:T(8,128)}, f32[96,128]{1,0:T(8,128)S(1)}, u32[]{:S(2)}, u32[]{:S(2)}) collective-permute-start(f32[96,128]{1,0:T(8,128)} %get-tuple-element.25), channel_id=1, source_target_pairs={{0,0},{5,1},{2,2},{7,3},{4,4},{1,5},{6,6},{3,7},{12,8},{9,9},{14,1... | collective-permute-start | bytes 147464 | tf_op jit(solution)/shard_map/ppermute | solution.py:616
  28.3 1.3 %collective-permute-start = (s32[8,128]{1,0:T(8,128)}, s32[8,128]{1,0:T(8,128)S(1)}, u32[]{:S(2)}, u32[]{:S(2)}) collective-permute-start(s32[8,128]{1,0:T(8,128)} %get-tuple-element.24), channel_id=1, source_target_pairs={{0,0},{5,1},{2,2},{7,3},{4,4},{1,5},{6,6},{3,7},{12,8},{9,9},{14,1... | collective-permute-start | bytes 12296 | tf_op jit(solution)/shard_map/ppermute | solution.py:616
  29.6 0.0 collective-permute-done.3.off
  29.6 0.0 copy-start.14
  29.6 1.0 copy-done.14
  30.6 2.5 %shard_map.193.off = bf16[32,128,128]{2,1,0:T(8,128)(2,1)} custom-call(bf16[32,128,128]{2,1,0:T(8,128)(2,1)} %copy-done.14), custom_call_target="tpu_custom_call" | custom-call | flops 60000002048 | bytes 200000000 | tf_op jit(solution)/shard_map/pallas_call | solution.py:535
  33.1 0.0 collective-permute-done.ints
  33.1 0.0 copy-start.10
  33.1 0.0 collective-permute-done.1.small
  33.1 0.0 copy-start.9
  33.1 0.0 collective-permute-done.2.blocks
  33.1 0.0 copy-start.1
  33.2 24.7 %all-to-all-done.msgs = bf16[8,32,3968]{2,1,0:T(8,128)(2,1)S(1)} async-done(((bf16[8,32,3968]{2,1,0:T(8,128)(2,1)}), bf16[8,32,3968]{2,1,0:T(8,128)(2,1)S(1)}, u32[]{:S(2)}, u32[]{:S(2)}) %all-to-all-start) | async-done | bytes 2031648 | tf_op jit(solution)/shard_map/all_to_all | solution.py:641
  57.9 0.0 copy-done.10
  57.9 0.0 copy-done.9
  57.9 0.0 copy-done.1
  57.9 0.0 copy-start
  57.9 1.3 %copy-done = bf16[8,32,3968]{2,1,0:T(8,128)(2,1)} copy-done((bf16[8,32,3968]{2,1,0:T(8,128)(2,1)}, bf16[8,32,3968]{2,1,0:T(8,128)(2,1)S(1)}, u32[]{:S(2)}) %copy-start) | copy-done | bytes 2031640
  59.2 11.9 %shard_map.195 = (bf16[32,3840]{1,0:T(8,128)(2,1)}, bf16[32,3840]{1,0:T(8,128)(2,1)}, bf16[32,3840]{1,0:T(8,128)(2,1)}, bf16[32,3840]{1,0:T(8,128)(2,1)}, bf16[3...) custom-call(s32[8]{0:T(128)} %stack.29.ids, ...), custom_call_target="tpu_custom_call" | custom-call | tf_op jit(solution)/shard_map/pallas_call | solution.py:535
  71.1 0.0 collective-permute-start.4
  71.1 3.3 %collective-permute-start.10 = (bf16[32,3840]{1,0:T(8,128)(2,1)}, bf16[32,3840]{1,0:T(8,128)(2,1)S(1)}, u32[]{:S(2)}, u32[]{:S(2)}) collective-permute-start(bf16[32,3840]{1,0:T(8,128)(2,1)} %get-tuple-element.43), channel_id=1, source_target_pairs={{11,0},{10,1},{9,2},{8,3},{15,4},{14,5},{13,6},{12,7},{3,8},{2,9},... | collective-permute-start | bytes 737288 | tf_op jit(solution)/shard_map/ppermute | solution.py:616
  74.3 0.0 collective-permute-start.5
  74.3 0.3 collective-permute-start.6
  74.7 1.5 %collective-permute-start.7 = (bf16[32,3840]{1,0:T(8,128)(2,1)}, bf16[32,3840]{1,0:T(8,128)(2,1)S(1)}, u32[]{:S(2)}, u32[]{:S(2)}) collective-permute-start(bf16[32,3840]{1,0:T(8,128)(2,1)} %get-tuple-element.39), channel_id=1, source_target_pairs={{3,0},{2,1},{1,2},{0,3},{7,4},{6,5},{5,6},{4,7},{11,8},{10,9},{9,1... | collective-permute-start | bytes 737288 | tf_op jit(solution)/shard_map/ppermute | solution.py:616
  76.2 4.2 %collective-permute-done.4.refs_4_ = bf16[32,3840]{1,0:T(8,128)(2,1)S(1)} collective-permute-done((bf16[32,3840]{1,0:T(8,128)(2,1)}, bf16[32,3840]{1,0:T(8,128)(2,1)S(1)}, u32[]{:S(2)}, u32[]{:S(2)}) %collective-permute-start.4) | collective-permute-done | bytes 245792 | tf_op jit(solution)/shard_map/ppermute | solution.py:616
  80.4 0.0 collective-permute-start.8
  80.4 0.5 collective-permute-done.10.refs_7_
  81.0 3.8 %collective-permute-start.9 = (bf16[32,3840]{1,0:T(8,128)(2,1)}, bf16[32,3840]{1,0:T(8,128)(2,1)S(1)}, u32[]{:S(2)}, u32[]{:S(2)}) collective-permute-start(bf16[32,3840]{1,0:T(8,128)(2,1)} %get-tuple-element.42), channel_id=1, source_target_pairs={{10,0},{11,1},{8,2},{9,3},{14,4},{15,5},{12,6},{13,7},{2,8},{3,9},... | collective-permute-start | bytes 737288 | tf_op jit(solution)/shard_map/ppermute | solution.py:616
  84.8 10.4 %all_to_all.22.tangents = bf16[8,32,128]{2,1,0:T(8,128)(2,1)} all-to-all(bf16[8,32,128]{2,1,0:T(8,128)(2,1)} %get-tuple-element.30), channel_id=1, replica_groups=mesh['y'=2,'x'=2,'h'=2,'l'=2,'c'=2] {'x','l','c'}, dimensions={0} | all-to-all | bytes 131072 | tf_op jit(solution)/shard_map/all_to_all | solution.py:669
  95.1 3.0 %shard_map.196 = (f32[3,128]{1,0:T(4,128)}, f32[3,128]{1,0:T(4,128)}, f32[32,128]{1,0:T(8,128)}) custom-call(s32[8]{0:T(128)} %stack.29.ids, bf16[8,32,128]{2,1,0:T(8,128)(2,1)} %all_to_all.22.tangents, s32[8,512]{1,0:T(8,128)} %get-tuple-element.31.place, f32[8,512]{1,0:T(8,128)} %get-tuple-element.32.strain, f32[12,512]{1,0:T(8,128)} %grads.3, ...), custom_call_target="tpu_custom_call" | custom-call | tf_op jit(solution)/shard_map/pallas_call | solution.py:535
  98.1 6.5 %all-to-all-start.2 = ((f32[32,1,128]{2,1,0:T(1,128)}), f32[32,1,128]{2,1,0:T(1,128)S(1)}, u32[]{:S(2)}, u32[]{:S(2)}) async-start(f32[32,1,128]{2,1,0:T(1,128)} %bitcast.33), calls=%async_computation.2 | async-start | bytes 32768 | tf_op jit(solution)/shard_map/all_to_all | solution.py:678
  104.6 0.0 collective-permute-done.5.refs_1_
  104.7 0.0 copy-start.4
  104.7 0.0 collective-permute-done.6.refs_2_
  104.7 0.0 copy-start.5
  104.7 0.0 collective-permute-done.7.refs_3_
  104.7 0.0 copy-start.6
  104.7 0.0 collective-permute-done.8.refs_5_
  104.7 0.0 copy-start.7
  104.7 0.0 collective-permute-done.9.refs_6_
  104.7 0.0 copy-start.8
  104.7 0.0 copy-done.2
  104.8 0.0 copy-done.3
  104.8 0.6 copy-done.4
  105.4 0.1 copy-done.5
  105.4 0.1 copy-done.6
  105.6 0.1 copy-done.7
  105.6 0.1 copy-done.8
  105.7 5.8 %shard_map.197 = bf16[512,3072]{1,0:T(8,128)(2,1)} custom-call(s32[8]{0:T(128)} %stack.29.ids, s32[8,512]{1,0:T(8,128)} %get-tuple-element.31.place, bf16[8,32,128]{2,1,0:T(8,128)(2,1)} %all_to_all.22.tangents, bf16[32,3840]{1,0:T(8,128)(2,1)} %get-tuple-element.36.refs_0_, bf16[32,3840]{1,0:T(8,128)(2,1)} %copy-done.4, bf16[32,3840]{1,0:T(8,128)(2,1)} %copy-done.5, ...), custom_call_target="tpu_custom_call" | custom-call | tf_op jit(solution)/shard_map/pallas_call | solution.py:535
  111.5 0.2 all-to-all-done.2
  111.8 0.6 slice_reduce_fusion
  113.1 0.0 copy-done.13
  113.1 0.6 broadcast_multiply_fusion
  (6 shorter events, 0.0 us)
Async XLA Ops:
  0.6 29.0 %collective-permute-start.3 = (bf16[32,128,128]{2,1,0:T(8,128)(2,1)}, bf16[32,128,128]{2,1,0:T(8,128)(2,1)S(1)}, u32[]{:S(2)}, u32[]{:S(2)}) collective-permute-start(bf16[32,128,128]{2,1,0:T(8,128)(2,1)} %bitcast.39), channel_id=1, source_target_pairs={{0,0},{5,1},{2,2},{7,3},{4,4},{1,5},{6,6},{3,7},{12,8},{9,9},{14,1... | collective-permute-start | bytes 3145736 | tf_op jit(solution)/shard_map/ppermute | solution.py:616
  3.2 17.3 %copy-start.11 = (f32[20,1,6]{0,1,2:T(1,128)S(1)}, f32[20,1,6]{0,1,2:T(1,128)}, u32[]{:S(2)}) copy-start(f32[20,1,6]{0,1,2:T(1,128)} %param.27) | copy-start | bytes 1444
  3.2 17.3 %copy-start.12 = (f32[32,1,6]{0,1,2:T(1,128)S(1)}, f32[32,1,6]{0,1,2:T(1,128)}, u32[]{:S(2)}) copy-start(f32[32,1,6]{0,1,2:T(1,128)} %param.31) | copy-start | bytes 2308
  12.7 45.2 %all-to-all-start = ((bf16[8,32,3968]{2,1,0:T(8,128)(2,1)}), bf16[8,32,3968]{2,1,0:T(8,128)(2,1)S(1)}, u32[]{:S(2)}, u32[]{:S(2)}) async-start(bf16[8,32,3968]{2,1,0:T(8,128)(2,1)} %get-tuple-element.27), calls=%async_computation | async-start | bytes 4063232 | tf_op jit(solution)/shard_map/all_to_all | solution.py:641
  25.2 7.9 %collective-permute-start.2 = (bf16[10,128,128]{2,1,0:T(8,128)(2,1)}, bf16[10,128,128]{2,1,0:T(8,128)(2,1)S(1)}, u32[]{:S(2)}, u32[]{:S(2)}) collective-permute-start(bf16[10,128,128]{2,1,0:T(8,128)(2,1)} %get-tuple-element.26), channel_id=1, source_target_pairs={{0,0},{5,1},{2,2},{7,3},{4,4},{1,5},{6,6},{3,7},{12,8},{9,9},{14,1... | collective-permute-start | bytes 983048 | tf_op jit(solution)/shard_map/ppermute | solution.py:616
  26.9 6.3 %collective-permute-start.1 = (f32[96,128]{1,0:T(8,128)}, f32[96,128]{1,0:T(8,128)S(1)}, u32[]{:S(2)}, u32[]{:S(2)}) collective-permute-start(f32[96,128]{1,0:T(8,128)} %get-tuple-element.25), channel_id=1, source_target_pairs={{0,0},{5,1},{2,2},{7,3},{4,4},{1,5},{6,6},{3,7},{12,8},{9,9},{14,1... | collective-permute-start | bytes 147464 | tf_op jit(solution)/shard_map/ppermute | solution.py:616
  28.3 4.8 %collective-permute-start = (s32[8,128]{1,0:T(8,128)}, s32[8,128]{1,0:T(8,128)S(1)}, u32[]{:S(2)}, u32[]{:S(2)}) collective-permute-start(s32[8,128]{1,0:T(8,128)} %get-tuple-element.24), channel_id=1, source_target_pairs={{0,0},{5,1},{2,2},{7,3},{4,4},{1,5},{6,6},{3,7},{12,8},{9,9},{14,1... | collective-permute-start | bytes 12296 | tf_op jit(solution)/shard_map/ppermute | solution.py:616
  29.6 1.0 copy-start.14
  33.1 24.8 %copy-start.10 = (s32[8,128]{1,0:T(8,128)}, s32[8,128]{1,0:T(8,128)S(1)}, u32[]{:S(2)}) copy-start(s32[8,128]{1,0:T(8,128)S(1)} %collective-permute-done.ints) | copy-start | bytes 12292
  33.1 24.8 %copy-start.9 = (f32[96,128]{1,0:T(8,128)}, f32[96,128]{1,0:T(8,128)S(1)}, u32[]{:S(2)}) copy-start(f32[96,128]{1,0:T(8,128)S(1)} %collective-permute-done.1.small) | copy-start | bytes 147460
  33.1 24.7 %copy-start.1 = (bf16[10,128,128]{2,1,0:T(8,128)(2,1)}, bf16[10,128,128]{2,1,0:T(8,128)(2,1)S(1)}, u32[]{:S(2)}) copy-start(bf16[10,128,128]{2,1,0:T(8,128)(2,1)S(1)} %collective-permute-done.2.blocks) | copy-start | bytes 983044
  57.9 1.3 %copy-start = (bf16[8,32,3968]{2,1,0:T(8,128)(2,1)}, bf16[8,32,3968]{2,1,0:T(8,128)(2,1)S(1)}, u32[]{:S(2)}) copy-start(bf16[8,32,3968]{2,1,0:T(8,128)(2,1)S(1)} %all-to-all-done.msgs) | copy-start | bytes 6094852
  71.1 9.4 %collective-permute-start.4 = (bf16[32,3840]{1,0:T(8,128)(2,1)}, bf16[32,3840]{1,0:T(8,128)(2,1)S(1)}, u32[]{:S(2)}, u32[]{:S(2)}) collective-permute-start(bf16[32,3840]{1,0:T(8,128)(2,1)} %get-tuple-element.29), channel_id=1, source_target_pairs={{8,0},{9,1},{10,2},{11,3},{12,4},{13,5},{14,6},{15,7},{0,8},{1,9},... | collective-permute-start | bytes 737288 | tf_op jit(solution)/shard_map/ppermute | solution.py:616
  71.1 9.9 %collective-permute-start.10 = (bf16[32,3840]{1,0:T(8,128)(2,1)}, bf16[32,3840]{1,0:T(8,128)(2,1)S(1)}, u32[]{:S(2)}, u32[]{:S(2)}) collective-permute-start(bf16[32,3840]{1,0:T(8,128)(2,1)} %get-tuple-element.43), channel_id=1, source_target_pairs={{11,0},{10,1},{9,2},{8,3},{15,4},{14,5},{13,6},{12,7},{3,8},{2,9},... | collective-permute-start | bytes 737288 | tf_op jit(solution)/shard_map/ppermute | solution.py:616
  74.3 30.3 %collective-permute-start.5 = (bf16[32,3840]{1,0:T(8,128)(2,1)}, bf16[32,3840]{1,0:T(8,128)(2,1)S(1)}, u32[]{:S(2)}, u32[]{:S(2)}) collective-permute-start(bf16[32,3840]{1,0:T(8,128)(2,1)} %get-tuple-element.37), channel_id=1, source_target_pairs={{1,0},{0,1},{3,2},{2,3},{5,4},{4,5},{7,6},{6,7},{9,8},{8,9},{11,10... | collective-permute-start | bytes 737288 | tf_op jit(solution)/shard_map/ppermute | solution.py:616
  74.3 30.3 %collective-permute-start.6 = (bf16[32,3840]{1,0:T(8,128)(2,1)}, bf16[32,3840]{1,0:T(8,128)(2,1)S(1)}, u32[]{:S(2)}, u32[]{:S(2)}) collective-permute-start(bf16[32,3840]{1,0:T(8,128)(2,1)} %get-tuple-element.38), channel_id=1, source_target_pairs={{2,0},{3,1},{0,2},{1,3},{6,4},{7,5},{4,6},{5,7},{10,8},{11,9},{8,1... | collective-permute-start | bytes 737288 | tf_op jit(solution)/shard_map/ppermute | solution.py:616
  74.7 30.0 %collective-permute-start.7 = (bf16[32,3840]{1,0:T(8,128)(2,1)}, bf16[32,3840]{1,0:T(8,128)(2,1)S(1)}, u32[]{:S(2)}, u32[]{:S(2)}) collective-permute-start(bf16[32,3840]{1,0:T(8,128)(2,1)} %get-tuple-element.39), channel_id=1, source_target_pairs={{3,0},{2,1},{1,2},{0,3},{7,4},{6,5},{5,6},{4,7},{11,8},{10,9},{9,1... | collective-permute-start | bytes 737288 | tf_op jit(solution)/shard_map/ppermute | solution.py:616
  80.4 24.3 %copy-start.2 = (bf16[32,3840]{1,0:T(8,128)(2,1)}, bf16[32,3840]{1,0:T(8,128)(2,1)S(1)}, u32[]{:S(2)}) copy-start(bf16[32,3840]{1,0:T(8,128)(2,1)S(1)} %collective-permute-done.4.refs_4_) | copy-start | bytes 737284
  80.4 24.3 %collective-permute-start.8 = (bf16[32,3840]{1,0:T(8,128)(2,1)}, bf16[32,3840]{1,0:T(8,128)(2,1)S(1)}, u32[]{:S(2)}, u32[]{:S(2)}) collective-permute-start(bf16[32,3840]{1,0:T(8,128)(2,1)} %get-tuple-element.41), channel_id=1, source_target_pairs={{9,0},{8,1},{11,2},{10,3},{13,4},{12,5},{15,6},{14,7},{1,8},{0,9},... | collective-permute-start | bytes 737288 | tf_op jit(solution)/shard_map/ppermute | solution.py:616
  81.0 23.8 %copy-start.3 = (bf16[32,3840]{1,0:T(8,128)(2,1)}, bf16[32,3840]{1,0:T(8,128)(2,1)S(1)}, u32[]{:S(2)}) copy-start(bf16[32,3840]{1,0:T(8,128)(2,1)S(1)} %collective-permute-done.10.refs_7_) | copy-start | bytes 737284
  81.0 23.7 %collective-permute-start.9 = (bf16[32,3840]{1,0:T(8,128)(2,1)}, bf16[32,3840]{1,0:T(8,128)(2,1)S(1)}, u32[]{:S(2)}, u32[]{:S(2)}) collective-permute-start(bf16[32,3840]{1,0:T(8,128)(2,1)} %get-tuple-element.42), channel_id=1, source_target_pairs={{10,0},{11,1},{8,2},{9,3},{14,4},{15,5},{12,6},{13,7},{2,8},{3,9},... | collective-permute-start | bytes 737288 | tf_op jit(solution)/shard_map/ppermute | solution.py:616
  98.1 15.0 %copy-start.13 = (f32[3,128]{1,0:T(4,128)S(1)}, f32[3,128]{1,0:T(4,128)}, u32[]{:S(2)}) copy-start(f32[3,128]{1,0:T(4,128)} %get-tuple-element.20) | copy-start | bytes 4612
  98.1 13.7 %all-to-all-start.2 = ((f32[32,1,128]{2,1,0:T(1,128)}), f32[32,1,128]{2,1,0:T(1,128)S(1)}, u32[]{:S(2)}, u32[]{:S(2)}) async-start(f32[32,1,128]{2,1,0:T(1,128)} %bitcast.33), calls=%async_computation.2 | async-start | bytes 32768 | tf_op jit(solution)/shard_map/all_to_all | solution.py:678
  104.7 0.7 copy-start.4
  104.7 0.8 copy-start.5
  104.7 0.9 copy-start.6
  104.7 0.9 copy-start.7
  104.7 1.0 copy-start.8

commit v4 on v3

--- a/solution.py
+++ b/solution.py
@@ -130,10 +130,12 @@
 
 def matrix_pack_kernel(
     ids, vol, off_row, off_col, off_count, coupling, diag_normal, off_normal, affine, diag,
-    diag_out, small, ints, row_local, row_size, rows_sel, seen, sems,
+    diag_out, small, ints, row_local, row_size, rows_sel, seen, loads, sems,
 ):
     half = ids[0]
     small[...] = jnp.zeros_like(small)
+    loads[...] = jnp.zeros_like(loads)
+    loads[0 : ROWS_GRP * COMPS, :] = coupling[...]
     small[0:VOL_GRP, 0:36] = affine[...]
     target = iota((1, BS), 1) % 64
     source = jnp.where(jnp.logical_and(target % 8 < 6, target < 48), 6 * (target % 8) + target // 8, -1)
@@ -176,7 +178,7 @@
     diag_rows = diag_normal[...]
     for i in range(HALF_ROWS):
         row = rows_sel[i]
-        small[8 * i : 8 * i + COMPS, :] = coupling[pl.ds(COMPS * row, COMPS), :]
+        small[8 * i : 8 * i + COMPS, :] = loads[pl.ds(COMPS * row, COMPS), :]
         normals += jnp.where(lane == i, pltpu.roll(diag_rows, (i - row + BS) % BS, 1), 0.0)
     normals += pltpu.roll(off_normal[...], HALF_OFF, 1)
     small[SM_NORMAL : SM_NORMAL + 8, :] = normals
@@ -632,6 +634,7 @@
         (VM, VM, SM),
         [
             pltpu.SMEM((32,), I32), pltpu.SMEM((32,), I32), pltpu.SMEM((16,), I32), pltpu.SMEM((8,), I32),
+            pltpu.VMEM((ROWS_GRP * COMPS + 16, BS), F32),
             pltpu.SemaphoreType.DMA((HALF_ROWS,)),
         ],
     )

time: 114 us -> 115 us (level)
  starting transfers between devices: 29.5 us -> 26.4 us
  blocking collectives: 10.4 us -> 13.4 us
    all_to_all x1, blocking collectives: 10.4 us -> 13.4 us  [on_device(): lax.all_to_all(own, UNIT_AXES, split_axis=0, concat_axis=0, tiled=True)]
    all_to_all x1, starting transfers between devices: 6.51 us -> 3.5 us  [on_device(): norms = lax.all_to_all(norm, AXES, split_axis=0, concat_axis=0, tiled=True)]
  transfers between devices with their start and end apart: 13 -> 13, of which waited for: 4 -> 3; matrix products, arithmetic and copies ran while one was open for 2% -> 2% of each run, Pallas kernels for 21% -> 21%
where the time goes in v4:
time: 115 us; the launch traced here: 114 us
  Pallas kernels  35.5 us (31%)
  waiting for transfers between devices  30.6 us (27%)
  starting transfers between devices  26.4 us (23%)
  blocking collectives  13.4 us (12%)
  local copies, waits for them, and re-layouts  5.11 us (4%)
  between operations  2.21 us (2%)
  other arithmetic  1.18 us (1%)
    pallas_call x6, Pallas kernels, call(): pl.pallas_call(kernel, out_shape=[jax.ShapeDtypeStruct(s, d) for s, d in...  35.5 us
    all_to_all x1, waiting for transfers between devices, on_device(): lax.all_to_all(packed, UNIT_AXES, split_axis=0, concat_axis=0, tiled=True)  24.7 us
    ppermute x11, starting transfers between devices, permute(): return lax.ppermute(value, AXES, pairs)  15.1 us
    all_to_all x1, blocking collectives, on_device(): lax.all_to_all(own, UNIT_AXES, split_axis=0, concat_axis=0, tiled=True)  13.4 us
    all_to_all x1, starting transfers between devices, on_device(): lax.all_to_all(packed, UNIT_AXES, split_axis=0, concat_axis=0, tiled=True)  7.85 us
    ppermute x11, waiting for transfers between devices, permute(): return lax.ppermute(value, AXES, pairs)  5.66 us
    all_to_all x1, starting transfers between devices, on_device(): norms = lax.all_to_all(norm, AXES, split_axis=0, concat_axis=0, tiled=True)  3.5 us
    unnamed x32, local copies, waits for them, and re-layouts  3.25 us
  transfers between devices with their start and end apart: 13, of which 3 were waited for; matrix products, arithmetic and copies ran while one was open for 2% of the time, Pallas kernels for 21%

profile of v4, /device:TPU:0, one launch (start us, length us, event | category | flops | bytes accessed | tf_op | source)
XLA Modules:
  0.0 114.5 jit_solution(13967158905622042821)
XLA Ops:
  0.6 1.9 %collective-permute-start.3 = (bf16[32,128,128]{2,1,0:T(8,128)(2,1)}, bf16[32,128,128]{2,1,0:T(8,128)(2,1)S(1)}, u32[]{:S(2)}, u32[]{:S(2)}) collective-permute-start(bf16[32,128,128]{2,1,0:T(8,128)(2,1)} %bitcast.39), channel_id=1, source_target_pairs={{0,0},{5,1},{2,2},{7,3},{4,4},{1,5},{6,6},{3,7},{12,8},{9,9},{14,1... | collective-permute-start | bytes 3145736 | tf_op jit(solution)/shard_map/ppermute | solution.py:618
  2.5 0.7 stack.29.ids
  3.2 0.0 copy-start.12
  3.2 9.5 %shard_map.194 = (bf16[8,32,3968]{2,1,0:T(8,128)(2,1)}, f32[8,512]{1,0:T(8,128)}, s32[8,512]{1,0:T(8,128)}) custom-call(s32[8]{0:T(128)} %stack.29.ids, s32[1,512]{1,0:T(1,128)} %bitcast.36, f32[3,128]{1,0:T(4,128)} %disp.1, s32[4,512]{1,0:T(4,128)} %conn.3, f32[12,512]{1,0:T(8,128)} %grads.3, bf16[512,3072]{1,0:T(8,128)(2,1)} %state.1), custom_call_target="tpu_custom_call" | custom-call | tf_op jit(solution)/shard_map/pallas_call | solution.py:537
  12.7 7.9 %all-to-all-start = ((bf16[8,32,3968]{2,1,0:T(8,128)(2,1)}), bf16[8,32,3968]{2,1,0:T(8,128)(2,1)S(1)}, u32[]{:S(2)}, u32[]{:S(2)}) async-start(bf16[8,32,3968]{2,1,0:T(8,128)(2,1)} %get-tuple-element.27), calls=%async_computation | async-start | bytes 4063232 | tf_op jit(solution)/shard_map/all_to_all | solution.py:644
  20.5 0.0 copy-done.11
  20.5 0.0 copy-done.12
  20.5 0.6 pad.8.diag_normal
  21.1 0.6 pad.9.off_normal
  22.4 2.8 %shard_map.192 = (bf16[10,128,128]{2,1,0:T(8,128)(2,1)}, f32[96,128]{1,0:T(8,128)}, s32[8,128]{1,0:T(8,128)}) custom-call(s32[8]{0:T(128)} %stack.29.ids, s32[1,8]{1,0:T(1,128)} %vol.1, s32[1,32]{1,0:T(1,128)} %bitcast.37, s32[1,32]{1,0:T(1,128)} %bitcast.38, s32[1]{0:T(128)S(6)} %copy.30.off_count, f32[120,128]{1,0:T(8,128)} %bitcast.30, ...), custom_call_target="tpu_custom_call" | custom-call | tf_op jit(solution)/shard_map/pallas_call | solution.py:537
  25.2 1.6 %collective-permute-start.2 = (bf16[10,128,128]{2,1,0:T(8,128)(2,1)}, bf16[10,128,128]{2,1,0:T(8,128)(2,1)S(1)}, u32[]{:S(2)}, u32[]{:S(2)}) collective-permute-start(bf16[10,128,128]{2,1,0:T(8,128)(2,1)} %get-tuple-element.26), channel_id=1, source_target_pairs={{0,0},{5,1},{2,2},{7,3},{4,4},{1,5},{6,6},{3,7},{12,8},{9,9},{14,1... | collective-permute-start | bytes 983048 | tf_op jit(solution)/shard_map/ppermute | solution.py:618
  26.9 1.4 %collective-permute-start.1 = (f32[96,128]{1,0:T(8,128)}, f32[96,128]{1,0:T(8,128)S(1)}, u32[]{:S(2)}, u32[]{:S(2)}) collective-permute-start(f32[96,128]{1,0:T(8,128)} %get-tuple-element.25), channel_id=1, source_target_pairs={{0,0},{5,1},{2,2},{7,3},{4,4},{1,5},{6,6},{3,7},{12,8},{9,9},{14,1... | collective-permute-start | bytes 147464 | tf_op jit(solution)/shard_map/ppermute | solution.py:618
  28.3 1.3 %collective-permute-start = (s32[8,128]{1,0:T(8,128)}, s32[8,128]{1,0:T(8,128)S(1)}, u32[]{:S(2)}, u32[]{:S(2)}) collective-permute-start(s32[8,128]{1,0:T(8,128)} %get-tuple-element.24), channel_id=1, source_target_pairs={{0,0},{5,1},{2,2},{7,3},{4,4},{1,5},{6,6},{3,7},{12,8},{9,9},{14,1... | collective-permute-start | bytes 12296 | tf_op jit(solution)/shard_map/ppermute | solution.py:618
  29.6 0.0 collective-permute-done.3.off
  29.6 0.0 copy-start.14
  29.6 1.0 copy-done.14
  30.6 2.5 %shard_map.193.off = bf16[32,128,128]{2,1,0:T(8,128)(2,1)} custom-call(bf16[32,128,128]{2,1,0:T(8,128)(2,1)} %copy-done.14), custom_call_target="tpu_custom_call" | custom-call | flops 60000002048 | bytes 200000000 | tf_op jit(solution)/shard_map/pallas_call | solution.py:537
  33.1 0.0 collective-permute-done.ints
  33.1 0.0 collective-permute-done.1.small
  33.1 0.0 copy-start.9
  33.1 0.0 collective-permute-done.2.blocks
  33.2 0.0 copy-start.1
  33.2 24.7 %all-to-all-done.msgs = bf16[8,32,3968]{2,1,0:T(8,128)(2,1)S(1)} async-done(((bf16[8,32,3968]{2,1,0:T(8,128)(2,1)}), bf16[8,32,3968]{2,1,0:T(8,128)(2,1)S(1)}, u32[]{:S(2)}, u32[]{:S(2)}) %all-to-all-start) | async-done | bytes 2031648 | tf_op jit(solution)/shard_map/all_to_all | solution.py:644
  57.9 0.0 copy-done.10
  57.9 0.0 copy-done.9
  57.9 0.0 copy-done.1
  57.9 0.0 copy-start
  57.9 1.3 %copy-done = bf16[8,32,3968]{2,1,0:T(8,128)(2,1)} copy-done((bf16[8,32,3968]{2,1,0:T(8,128)(2,1)}, bf16[8,32,3968]{2,1,0:T(8,128)(2,1)S(1)}, u32[]{:S(2)}) %copy-start) | copy-done | bytes 2031640
  59.2 11.9 %shard_map.195 = (bf16[32,3840]{1,0:T(8,128)(2,1)}, bf16[32,3840]{1,0:T(8,128)(2,1)}, bf16[32,3840]{1,0:T(8,128)(2,1)}, bf16[32,3840]{1,0:T(8,128)(2,1)}, bf16[3...) custom-call(s32[8]{0:T(128)} %stack.29.ids, ...), custom_call_target="tpu_custom_call" | custom-call | tf_op jit(solution)/shard_map/pallas_call | solution.py:537
  71.1 1.8 %collective-permute-start.4 = (bf16[32,3840]{1,0:T(8,128)(2,1)}, bf16[32,3840]{1,0:T(8,128)(2,1)S(1)}, u32[]{:S(2)}, u32[]{:S(2)}) collective-permute-start(bf16[32,3840]{1,0:T(8,128)(2,1)} %get-tuple-element.29), channel_id=1, source_target_pairs={{8,0},{9,1},{10,2},{11,3},{12,4},{13,5},{14,6},{15,7},{0,8},{1,9},... | collective-permute-start | bytes 737288 | tf_op jit(solution)/shard_map/ppermute | solution.py:618
  72.9 0.0 collective-permute-start.10
  72.9 2.9 %collective-permute-start.5 = (bf16[32,3840]{1,0:T(8,128)(2,1)}, bf16[32,3840]{1,0:T(8,128)(2,1)S(1)}, u32[]{:S(2)}, u32[]{:S(2)}) collective-permute-start(bf16[32,3840]{1,0:T(8,128)(2,1)} %get-tuple-element.37), channel_id=1, source_target_pairs={{1,0},{0,1},{3,2},{2,3},{5,4},{4,5},{7,6},{6,7},{9,8},{8,9},{11,10... | collective-permute-start | bytes 737288 | tf_op jit(solution)/shard_map/ppermute | solution.py:618
  75.8 0.4 collective-permute-start.6
  76.2 1.0 collective-permute-start.7
  77.1 5.6 %collective-permute-done.4.refs_4_ = bf16[32,3840]{1,0:T(8,128)(2,1)S(1)} collective-permute-done((bf16[32,3840]{1,0:T(8,128)(2,1)}, bf16[32,3840]{1,0:T(8,128)(2,1)S(1)}, u32[]{:S(2)}, u32[]{:S(2)}) %collective-permute-start.4) | collective-permute-done | bytes 245792 | tf_op jit(solution)/shard_map/ppermute | solution.py:618
  82.8 0.0 collective-permute-start.8
  82.8 0.0 collective-permute-done.10.refs_7_
  82.8 0.0 copy-start.3
  82.8 2.8 %collective-permute-start.9 = (bf16[32,3840]{1,0:T(8,128)(2,1)}, bf16[32,3840]{1,0:T(8,128)(2,1)S(1)}, u32[]{:S(2)}, u32[]{:S(2)}) collective-permute-start(bf16[32,3840]{1,0:T(8,128)(2,1)} %get-tuple-element.42), channel_id=1, source_target_pairs={{10,0},{11,1},{8,2},{9,3},{14,4},{15,5},{12,6},{13,7},{2,8},{3,9},... | collective-permute-start | bytes 737288 | tf_op jit(solution)/shard_map/ppermute | solution.py:618
  85.5 13.4 %all_to_all.22.tangents = bf16[8,32,128]{2,1,0:T(8,128)(2,1)} all-to-all(bf16[8,32,128]{2,1,0:T(8,128)(2,1)} %get-tuple-element.30), channel_id=1, replica_groups=mesh['y'=2,'x'=2,'h'=2,'l'=2,'c'=2] {'x','l','c'}, dimensions={0} | all-to-all | bytes 131072 | tf_op jit(solution)/shard_map/all_to_all | solution.py:672
  98.9 3.0 %shard_map.196 = (f32[3,128]{1,0:T(4,128)}, f32[3,128]{1,0:T(4,128)}, f32[32,128]{1,0:T(8,128)}) custom-call(s32[8]{0:T(128)} %stack.29.ids, bf16[8,32,128]{2,1,0:T(8,128)(2,1)} %all_to_all.22.tangents, s32[8,512]{1,0:T(8,128)} %get-tuple-element.31.place, f32[8,512]{1,0:T(8,128)} %get-tuple-element.32.strain, f32[12,512]{1,0:T(8,128)} %grads.3, ...), custom_call_target="tpu_custom_call" | custom-call | tf_op jit(solution)/shard_map/pallas_call | solution.py:537
  102.0 3.5 %all-to-all-start.2 = ((f32[32,1,128]{2,1,0:T(1,128)}), f32[32,1,128]{2,1,0:T(1,128)S(1)}, u32[]{:S(2)}, u32[]{:S(2)}) async-start(f32[32,1,128]{2,1,0:T(1,128)} %bitcast.33), calls=%async_computation.2 | async-start | bytes 32768 | tf_op jit(solution)/shard_map/all_to_all | solution.py:681
  105.5 0.0 collective-permute-done.5.refs_1_
  105.5 0.0 copy-start.4
  105.5 0.0 collective-permute-done.6.refs_2_
  105.5 0.0 copy-start.5
  105.5 0.0 collective-permute-done.7.refs_3_
  105.5 0.0 copy-start.6
  105.5 0.0 collective-permute-done.8.refs_5_
  105.5 0.0 copy-start.7
  105.5 0.0 collective-permute-done.9.refs_6_
  105.6 0.0 copy-start.8
  105.6 0.0 copy-done.2
  105.6 0.0 copy-done.3
  105.6 0.6 copy-done.4
  106.2 0.1 copy-done.5
  106.3 0.1 copy-done.6
  106.4 0.1 copy-done.7
  106.5 0.1 copy-done.8
  106.5 5.8 %shard_map.197 = bf16[512,3072]{1,0:T(8,128)(2,1)} custom-call(s32[8]{0:T(128)} %stack.29.ids, s32[8,512]{1,0:T(8,128)} %get-tuple-element.31.place, bf16[8,32,128]{2,1,0:T(8,128)(2,1)} %all_to_all.22.tangents, bf16[32,3840]{1,0:T(8,128)(2,1)} %get-tuple-element.36.refs_0_, bf16[32,3840]{1,0:T(8,128)(2,1)} %copy-done.4, bf16[32,3840]{1,0:T(8,128)(2,1)} %copy-done.5, ...), custom_call_target="tpu_custom_call" | custom-call | tf_op jit(solution)/shard_map/pallas_call | solution.py:537
  112.4 0.2 all-to-all-done.2
  112.6 0.6 slice_reduce_fusion
  113.9 0.0 copy-done.13
  113.9 0.6 broadcast_multiply_fusion
  (6 shorter events, 0.0 us)
Async XLA Ops:
  0.6 29.0 %collective-permute-start.3 = (bf16[32,128,128]{2,1,0:T(8,128)(2,1)}, bf16[32,128,128]{2,1,0:T(8,128)(2,1)S(1)}, u32[]{:S(2)}, u32[]{:S(2)}) collective-permute-start(bf16[32,128,128]{2,1,0:T(8,128)(2,1)} %bitcast.39), channel_id=1, source_target_pairs={{0,0},{5,1},{2,2},{7,3},{4,4},{1,5},{6,6},{3,7},{12,8},{9,9},{14,1... | collective-permute-start | bytes 3145736 | tf_op jit(solution)/shard_map/ppermute | solution.py:618
  3.2 17.3 %copy-start.11 = (f32[20,1,6]{0,1,2:T(1,128)S(1)}, f32[20,1,6]{0,1,2:T(1,128)}, u32[]{:S(2)}) copy-start(f32[20,1,6]{0,1,2:T(1,128)} %param.27) | copy-start | bytes 1444
  3.2 17.3 %copy-start.12 = (f32[32,1,6]{0,1,2:T(1,128)S(1)}, f32[32,1,6]{0,1,2:T(1,128)}, u32[]{:S(2)}) copy-start(f32[32,1,6]{0,1,2:T(1,128)} %param.31) | copy-start | bytes 2308
  12.7 45.2 %all-to-all-start = ((bf16[8,32,3968]{2,1,0:T(8,128)(2,1)}), bf16[8,32,3968]{2,1,0:T(8,128)(2,1)S(1)}, u32[]{:S(2)}, u32[]{:S(2)}) async-start(bf16[8,32,3968]{2,1,0:T(8,128)(2,1)} %get-tuple-element.27), calls=%async_computation | async-start | bytes 4063232 | tf_op jit(solution)/shard_map/all_to_all | solution.py:644
  25.2 7.9 %collective-permute-start.2 = (bf16[10,128,128]{2,1,0:T(8,128)(2,1)}, bf16[10,128,128]{2,1,0:T(8,128)(2,1)S(1)}, u32[]{:S(2)}, u32[]{:S(2)}) collective-permute-start(bf16[10,128,128]{2,1,0:T(8,128)(2,1)} %get-tuple-element.26), channel_id=1, source_target_pairs={{0,0},{5,1},{2,2},{7,3},{4,4},{1,5},{6,6},{3,7},{12,8},{9,9},{14,1... | collective-permute-start | bytes 983048 | tf_op jit(solution)/shard_map/ppermute | solution.py:618
  26.9 6.3 %collective-permute-start.1 = (f32[96,128]{1,0:T(8,128)}, f32[96,128]{1,0:T(8,128)S(1)}, u32[]{:S(2)}, u32[]{:S(2)}) collective-permute-start(f32[96,128]{1,0:T(8,128)} %get-tuple-element.25), channel_id=1, source_target_pairs={{0,0},{5,1},{2,2},{7,3},{4,4},{1,5},{6,6},{3,7},{12,8},{9,9},{14,1... | collective-permute-start | bytes 147464 | tf_op jit(solution)/shard_map/ppermute | solution.py:618
  28.3 4.8 %collective-permute-start = (s32[8,128]{1,0:T(8,128)}, s32[8,128]{1,0:T(8,128)S(1)}, u32[]{:S(2)}, u32[]{:S(2)}) collective-permute-start(s32[8,128]{1,0:T(8,128)} %get-tuple-element.24), channel_id=1, source_target_pairs={{0,0},{5,1},{2,2},{7,3},{4,4},{1,5},{6,6},{3,7},{12,8},{9,9},{14,1... | collective-permute-start | bytes 12296 | tf_op jit(solution)/shard_map/ppermute | solution.py:618
  29.6 1.0 copy-start.14
  33.1 24.8 %copy-start.10 = (s32[8,128]{1,0:T(8,128)}, s32[8,128]{1,0:T(8,128)S(1)}, u32[]{:S(2)}) copy-start(s32[8,128]{1,0:T(8,128)S(1)} %collective-permute-done.ints) | copy-start | bytes 12292
  33.1 24.8 %copy-start.9 = (f32[96,128]{1,0:T(8,128)}, f32[96,128]{1,0:T(8,128)S(1)}, u32[]{:S(2)}) copy-start(f32[96,128]{1,0:T(8,128)S(1)} %collective-permute-done.1.small) | copy-start | bytes 147460
  33.2 24.7 %copy-start.1 = (bf16[10,128,128]{2,1,0:T(8,128)(2,1)}, bf16[10,128,128]{2,1,0:T(8,128)(2,1)S(1)}, u32[]{:S(2)}) copy-start(bf16[10,128,128]{2,1,0:T(8,128)(2,1)S(1)} %collective-permute-done.2.blocks) | copy-start | bytes 983044
  57.9 1.3 %copy-start = (bf16[8,32,3968]{2,1,0:T(8,128)(2,1)}, bf16[8,32,3968]{2,1,0:T(8,128)(2,1)S(1)}, u32[]{:S(2)}) copy-start(bf16[8,32,3968]{2,1,0:T(8,128)(2,1)S(1)} %all-to-all-done.msgs) | copy-start | bytes 6094852
  71.1 11.7 %collective-permute-start.4 = (bf16[32,3840]{1,0:T(8,128)(2,1)}, bf16[32,3840]{1,0:T(8,128)(2,1)S(1)}, u32[]{:S(2)}, u32[]{:S(2)}) collective-permute-start(bf16[32,3840]{1,0:T(8,128)(2,1)} %get-tuple-element.29), channel_id=1, source_target_pairs={{8,0},{9,1},{10,2},{11,3},{12,4},{13,5},{14,6},{15,7},{0,8},{1,9},... | collective-permute-start | bytes 737288 | tf_op jit(solution)/shard_map/ppermute | solution.py:618
  72.9 9.9 %collective-permute-start.10 = (bf16[32,3840]{1,0:T(8,128)(2,1)}, bf16[32,3840]{1,0:T(8,128)(2,1)S(1)}, u32[]{:S(2)}, u32[]{:S(2)}) collective-permute-start(bf16[32,3840]{1,0:T(8,128)(2,1)} %get-tuple-element.43), channel_id=1, source_target_pairs={{11,0},{10,1},{9,2},{8,3},{15,4},{14,5},{13,6},{12,7},{3,8},{2,9},... | collective-permute-start | bytes 737288 | tf_op jit(solution)/shard_map/ppermute | solution.py:618
  72.9 32.6 %collective-permute-start.5 = (bf16[32,3840]{1,0:T(8,128)(2,1)}, bf16[32,3840]{1,0:T(8,128)(2,1)S(1)}, u32[]{:S(2)}, u32[]{:S(2)}) collective-permute-start(bf16[32,3840]{1,0:T(8,128)(2,1)} %get-tuple-element.37), channel_id=1, source_target_pairs={{1,0},{0,1},{3,2},{2,3},{5,4},{4,5},{7,6},{6,7},{9,8},{8,9},{11,10... | collective-permute-start | bytes 737288 | tf_op jit(solution)/shard_map/ppermute | solution.py:618
  75.8 29.7 %collective-permute-start.6 = (bf16[32,3840]{1,0:T(8,128)(2,1)}, bf16[32,3840]{1,0:T(8,128)(2,1)S(1)}, u32[]{:S(2)}, u32[]{:S(2)}) collective-permute-start(bf16[32,3840]{1,0:T(8,128)(2,1)} %get-tuple-element.38), channel_id=1, source_target_pairs={{2,0},{3,1},{0,2},{1,3},{6,4},{7,5},{4,6},{5,7},{10,8},{11,9},{8,1... | collective-permute-start | bytes 737288 | tf_op jit(solution)/shard_map/ppermute | solution.py:618
  76.2 29.3 %collective-permute-start.7 = (bf16[32,3840]{1,0:T(8,128)(2,1)}, bf16[32,3840]{1,0:T(8,128)(2,1)S(1)}, u32[]{:S(2)}, u32[]{:S(2)}) collective-permute-start(bf16[32,3840]{1,0:T(8,128)(2,1)} %get-tuple-element.39), channel_id=1, source_target_pairs={{3,0},{2,1},{1,2},{0,3},{7,4},{6,5},{5,6},{4,7},{11,8},{10,9},{9,1... | collective-permute-start | bytes 737288 | tf_op jit(solution)/shard_map/ppermute | solution.py:618
  82.8 22.8 %copy-start.2 = (bf16[32,3840]{1,0:T(8,128)(2,1)}, bf16[32,3840]{1,0:T(8,128)(2,1)S(1)}, u32[]{:S(2)}) copy-start(bf16[32,3840]{1,0:T(8,128)(2,1)S(1)} %collective-permute-done.4.refs_4_) | copy-start | bytes 737284
  82.8 22.8 %collective-permute-start.8 = (bf16[32,3840]{1,0:T(8,128)(2,1)}, bf16[32,3840]{1,0:T(8,128)(2,1)S(1)}, u32[]{:S(2)}, u32[]{:S(2)}) collective-permute-start(bf16[32,3840]{1,0:T(8,128)(2,1)} %get-tuple-element.41), channel_id=1, source_target_pairs={{9,0},{8,1},{11,2},{10,3},{13,4},{12,5},{15,6},{14,7},{1,8},{0,9},... | collective-permute-start | bytes 737288 | tf_op jit(solution)/shard_map/ppermute | solution.py:618
  82.8 22.8 %copy-start.3 = (bf16[32,3840]{1,0:T(8,128)(2,1)}, bf16[32,3840]{1,0:T(8,128)(2,1)S(1)}, u32[]{:S(2)}) copy-start(bf16[32,3840]{1,0:T(8,128)(2,1)S(1)} %collective-permute-done.10.refs_7_) | copy-start | bytes 737284
  82.8 22.8 %collective-permute-start.9 = (bf16[32,3840]{1,0:T(8,128)(2,1)}, bf16[32,3840]{1,0:T(8,128)(2,1)S(1)}, u32[]{:S(2)}, u32[]{:S(2)}) collective-permute-start(bf16[32,3840]{1,0:T(8,128)(2,1)} %get-tuple-element.42), channel_id=1, source_target_pairs={{10,0},{11,1},{8,2},{9,3},{14,4},{15,5},{12,6},{13,7},{2,8},{3,9},... | collective-permute-start | bytes 737288 | tf_op jit(solution)/shard_map/ppermute | solution.py:618
  102.0 11.9 %copy-start.13 = (f32[3,128]{1,0:T(4,128)S(1)}, f32[3,128]{1,0:T(4,128)}, u32[]{:S(2)}) copy-start(f32[3,128]{1,0:T(4,128)} %get-tuple-element.20) | copy-start | bytes 4612
  102.0 10.6 %all-to-all-start.2 = ((f32[32,1,128]{2,1,0:T(1,128)}), f32[32,1,128]{2,1,0:T(1,128)S(1)}, u32[]{:S(2)}, u32[]{:S(2)}) async-start(f32[32,1,128]{2,1,0:T(1,128)} %bitcast.33), calls=%async_computation.2 | async-start | bytes 32768 | tf_op jit(solution)/shard_map/all_to_all | solution.py:681
  105.5 0.7 copy-start.4
  105.5 0.8 copy-start.5
  105.5 0.9 copy-start.6
  105.5 0.9 copy-start.7
  105.6 1.0 copy-start.8

commit v5 on v4

--- a/solution.py
+++ b/solution.py
@@ -226,13 +226,12 @@
     volume_hot = iota((volumes, elems), 0) == group * VOL_GRP + volume
     volume_hot16 = jnp.where(volume_hot, 1.0, 0.0).astype(BF16)
     load.wait()
-    ones = jnp.ones((8, LEVEL), BF16)
-    filled = jnp.concatenate(
-        [dot_nt(ones, jnp.abs(state_vmem[:, LEVEL * a : LEVEL * (a + 1)]))[0:1] for a in range(NBMAX)], axis=0
-    )
-    marks = jnp.concatenate(
-        [jnp.where(filled > 0.0, 1.0, 0.0), jnp.ones((1, elems), F32), jnp.zeros((3, elems), F32)], axis=0
-    ).astype(BF16)
+    level_lane = iota((1, BS), 1)
+    filled = jnp.where(level_lane == NBMAX, 1.0, 0.0)
+    for a in range(NBMAX):
+        chosen = jnp.where(iota((LEVEL, BS), 1) == a, 1.0, 0.0).astype(BF16)
+        filled = filled + dot_nn(jnp.abs(state_vmem[:, LEVEL * a : LEVEL * (a + 1)]), chosen)
+    marks = dot_nn(volume_hot16, jnp.where(filled > 0.0, 1.0, 0.0).astype(BF16))
 
     def code_of(take, counts, number):
         height = jnp.zeros_like(number)
@@ -241,10 +240,10 @@
         return jnp.where(take(counts, NBMAX) > 0.0, height * VOL_GRP + number % VOL_GRP, 1 << 20)
 
     code_row = code_of(
-        lambda x, a: x[a : a + 1, :], dot_nt(marks, volume_hot16), iota((1, volumes), 1)
+        lambda x, a: x[a : a + 1, :], jnp.transpose(marks), iota((1, volumes), 1)
     )
     code_col = code_of(
-        lambda x, a: x[:, a : a + 1], dot_nt(volume_hot16, marks), iota((volumes, 1), 0)
+        lambda x, a: x[:, a : a + 1], marks, iota((volumes, 1), 0)
     )
     same = iota((volumes, volumes), 0) // VOL_GRP == iota((volumes, volumes), 1) // VOL_GRP
     below = jnp.where(jnp.logical_and(same, code_row < code_col), 1, 0)

time: 115 us -> 116 us (level); the launches traced: 114 us -> 113 us
  waiting for transfers between devices: 30.6 us -> 28.7 us
  blocking collectives: 13.4 us -> 11.5 us
  Pallas kernels: 35.5 us -> 36.9 us
  starting transfers between devices: 26.4 us -> 27.7 us
    all_to_all x1, blocking collectives: 13.4 us -> 11.5 us  [on_device(): lax.all_to_all(own, UNIT_AXES, split_axis=0, concat_axis=0, tiled=True)]
    all_to_all x1, starting transfers between devices: 3.5 us -> 5.04 us  [on_device(): norms = lax.all_to_all(norm, AXES, split_axis=0, concat_axis=0, tiled=True)]
    all_to_all x1, waiting for transfers between devices: 24.7 us -> 23.3 us  [on_device(): lax.all_to_all(packed, UNIT_AXES, split_axis=0, concat_axis=0, tiled=True)]
    pallas_call x6, Pallas kernels: 35.5 us -> 36.9 us  [call(): pl.pallas_call(kernel, out_shape=[jax.ShapeDtypeStruct(s, d) for s, d in...]
  transfers between devices with their start and end apart: 13 -> 13, of which waited for: 3 -> 4; matrix products, arithmetic and copies ran while one was open for 2% -> 2% of each run, Pallas kernels for 21% -> 22%
where the time goes in v5:
time: 116 us; the launch traced here: 113 us
  Pallas kernels  36.9 us (32%)
  waiting for transfers between devices  28.7 us (25%)
  starting transfers between devices  27.7 us (24%)
  blocking collectives  11.5 us (10%)
  local copies, waits for them, and re-layouts  5.11 us (4%)
  between operations  2.2 us (2%)
  other arithmetic  1.18 us (1%)
    pallas_call x6, Pallas kernels, call(): pl.pallas_call(kernel, out_shape=[jax.ShapeDtypeStruct(s, d) for s, d in...  36.9 us
    all_to_all x1, waiting for transfers between devices, on_device(): lax.all_to_all(packed, UNIT_AXES, split_axis=0, concat_axis=0, tiled=True)  23.3 us
    ppermute x11, starting transfers between devices, permute(): return lax.ppermute(value, AXES, pairs)  14.8 us
    all_to_all x1, blocking collectives, on_device(): lax.all_to_all(own, UNIT_AXES, split_axis=0, concat_axis=0, tiled=True)  11.5 us
    all_to_all x1, starting transfers between devices, on_device(): lax.all_to_all(packed, UNIT_AXES, split_axis=0, concat_axis=0, tiled=True)  7.88 us
    ppermute x11, waiting for transfers between devices, permute(): return lax.ppermute(value, AXES, pairs)  5.18 us
    all_to_all x1, starting transfers between devices, on_device(): norms = lax.all_to_all(norm, AXES, split_axis=0, concat_axis=0, tiled=True)  5.04 us
    unnamed x32, local copies, waits for them, and re-layouts  3.25 us
  transfers between devices with their start and end apart: 13, of which 4 were waited for; matrix products, arithmetic and copies ran while one was open for 2% of the time, Pallas kernels for 22%

profile of v5, /device:TPU:0, one launch (start us, length us, event | category | flops | bytes accessed | tf_op | source)
XLA Modules:
  0.0 113.4 jit_solution(6511479583000893818)
XLA Ops:
  0.6 1.9 %collective-permute-start.3 = (bf16[32,128,128]{2,1,0:T(8,128)(2,1)}, bf16[32,128,128]{2,1,0:T(8,128)(2,1)S(1)}, u32[]{:S(2)}, u32[]{:S(2)}) collective-permute-start(bf16[32,128,128]{2,1,0:T(8,128)(2,1)} %bitcast.39), channel_id=1, source_target_pairs={{0,0},{5,1},{2,2},{7,3},{4,4},{1,5},{6,6},{3,7},{12,8},{9,9},{14,1... | collective-permute-start | bytes 3145736 | tf_op jit(solution)/shard_map/ppermute | solution.py:617
  2.5 0.7 stack.29.ids
  3.2 0.0 copy-start.11
  3.2 0.0 copy-start.12
  3.2 10.8 %shard_map.194 = (bf16[8,32,3968]{2,1,0:T(8,128)(2,1)}, f32[8,512]{1,0:T(8,128)}, s32[8,512]{1,0:T(8,128)}) custom-call(s32[8]{0:T(128)} %stack.29.ids, s32[1,512]{1,0:T(1,128)} %bitcast.36, f32[3,128]{1,0:T(4,128)} %disp.1, s32[4,512]{1,0:T(4,128)} %conn.3, f32[12,512]{1,0:T(8,128)} %grads.3, bf16[512,3072]{1,0:T(8,128)(2,1)} %state.1), custom_call_target="tpu_custom_call" | custom-call | tf_op jit(solution)/shard_map/pallas_call | solution.py:536
  14.0 7.9 %all-to-all-start = ((bf16[8,32,3968]{2,1,0:T(8,128)(2,1)}), bf16[8,32,3968]{2,1,0:T(8,128)(2,1)S(1)}, u32[]{:S(2)}, u32[]{:S(2)}) async-start(bf16[8,32,3968]{2,1,0:T(8,128)(2,1)} %get-tuple-element.27), calls=%async_computation | async-start | bytes 4063232 | tf_op jit(solution)/shard_map/all_to_all | solution.py:643
  21.9 0.0 copy-done.11
  21.9 0.0 copy-done.12
  22.0 0.6 pad.8.diag_normal
  22.6 0.6 pad.9.off_normal
  23.8 2.8 %shard_map.192 = (bf16[10,128,128]{2,1,0:T(8,128)(2,1)}, f32[96,128]{1,0:T(8,128)}, s32[8,128]{1,0:T(8,128)}) custom-call(s32[8]{0:T(128)} %stack.29.ids, s32[1,8]{1,0:T(1,128)} %vol.1, s32[1,32]{1,0:T(1,128)} %bitcast.37, s32[1,32]{1,0:T(1,128)} %bitcast.38, s32[1]{0:T(128)S(6)} %copy.30.off_count, f32[120,128]{1,0:T(8,128)} %bitcast.30, ...), custom_call_target="tpu_custom_call" | custom-call | tf_op jit(solution)/shard_map/pallas_call | solution.py:536
  26.6 1.6 %collective-permute-start.2 = (bf16[10,128,128]{2,1,0:T(8,128)(2,1)}, bf16[10,128,128]{2,1,0:T(8,128)(2,1)S(1)}, u32[]{:S(2)}, u32[]{:S(2)}) collective-permute-start(bf16[10,128,128]{2,1,0:T(8,128)(2,1)} %get-tuple-element.26), channel_id=1, source_target_pairs={{0,0},{5,1},{2,2},{7,3},{4,4},{1,5},{6,6},{3,7},{12,8},{9,9},{14,1... | collective-permute-start | bytes 983048 | tf_op jit(solution)/shard_map/ppermute | solution.py:617
  28.3 1.4 %collective-permute-start.1 = (f32[96,128]{1,0:T(8,128)}, f32[96,128]{1,0:T(8,128)S(1)}, u32[]{:S(2)}, u32[]{:S(2)}) collective-permute-start(f32[96,128]{1,0:T(8,128)} %get-tuple-element.25), channel_id=1, source_target_pairs={{0,0},{5,1},{2,2},{7,3},{4,4},{1,5},{6,6},{3,7},{12,8},{9,9},{14,1... | collective-permute-start | bytes 147464 | tf_op jit(solution)/shard_map/ppermute | solution.py:617
  29.7 1.3 %collective-permute-start = (s32[8,128]{1,0:T(8,128)}, s32[8,128]{1,0:T(8,128)S(1)}, u32[]{:S(2)}, u32[]{:S(2)}) collective-permute-start(s32[8,128]{1,0:T(8,128)} %get-tuple-element.24), channel_id=1, source_target_pairs={{0,0},{5,1},{2,2},{7,3},{4,4},{1,5},{6,6},{3,7},{12,8},{9,9},{14,1... | collective-permute-start | bytes 12296 | tf_op jit(solution)/shard_map/ppermute | solution.py:617
  31.0 0.0 collective-permute-done.3.off
  31.0 0.0 copy-start.14
  31.0 1.0 copy-done.14
  32.0 2.5 %shard_map.193.off = bf16[32,128,128]{2,1,0:T(8,128)(2,1)} custom-call(bf16[32,128,128]{2,1,0:T(8,128)(2,1)} %copy-done.14), custom_call_target="tpu_custom_call" | custom-call | flops 60000002048 | bytes 200000000 | tf_op jit(solution)/shard_map/pallas_call | solution.py:536
  34.5 0.0 collective-permute-done.ints
  34.5 0.0 collective-permute-done.1.small
  34.6 0.0 copy-start.9
  34.6 0.0 collective-permute-done.2.blocks
  34.6 0.0 copy-start.1
  34.6 23.3 %all-to-all-done.msgs = bf16[8,32,3968]{2,1,0:T(8,128)(2,1)S(1)} async-done(((bf16[8,32,3968]{2,1,0:T(8,128)(2,1)}), bf16[8,32,3968]{2,1,0:T(8,128)(2,1)S(1)}, u32[]{:S(2)}, u32[]{:S(2)}) %all-to-all-start) | async-done | bytes 2031648 | tf_op jit(solution)/shard_map/all_to_all | solution.py:643
  57.9 0.0 copy-done.10
  57.9 0.0 copy-done.9
  57.9 0.0 copy-done.1
  57.9 0.0 copy-start
  57.9 1.3 %copy-done = bf16[8,32,3968]{2,1,0:T(8,128)(2,1)} copy-done((bf16[8,32,3968]{2,1,0:T(8,128)(2,1)}, bf16[8,32,3968]{2,1,0:T(8,128)(2,1)S(1)}, u32[]{:S(2)}) %copy-start) | copy-done | bytes 2031640
  59.2 11.9 %shard_map.195 = (bf16[32,3840]{1,0:T(8,128)(2,1)}, bf16[32,3840]{1,0:T(8,128)(2,1)}, bf16[32,3840]{1,0:T(8,128)(2,1)}, bf16[32,3840]{1,0:T(8,128)(2,1)}, bf16[3...) custom-call(s32[8]{0:T(128)} %stack.29.ids, ...), custom_call_target="tpu_custom_call" | custom-call | tf_op jit(solution)/shard_map/pallas_call | solution.py:536
  71.1 1.8 %collective-permute-start.4 = (bf16[32,3840]{1,0:T(8,128)(2,1)}, bf16[32,3840]{1,0:T(8,128)(2,1)S(1)}, u32[]{:S(2)}, u32[]{:S(2)}) collective-permute-start(bf16[32,3840]{1,0:T(8,128)(2,1)} %get-tuple-element.29), channel_id=1, source_target_pairs={{8,0},{9,1},{10,2},{11,3},{12,4},{13,5},{14,6},{15,7},{0,8},{1,9},... | collective-permute-start | bytes 737288 | tf_op jit(solution)/shard_map/ppermute | solution.py:617
  72.9 1.4 %collective-permute-start.10 = (bf16[32,3840]{1,0:T(8,128)(2,1)}, bf16[32,3840]{1,0:T(8,128)(2,1)S(1)}, u32[]{:S(2)}, u32[]{:S(2)}) collective-permute-start(bf16[32,3840]{1,0:T(8,128)(2,1)} %get-tuple-element.43), channel_id=1, source_target_pairs={{11,0},{10,1},{9,2},{8,3},{15,4},{14,5},{13,6},{12,7},{3,8},{2,9},... | collective-permute-start | bytes 737288 | tf_op jit(solution)/shard_map/ppermute | solution.py:617
  74.3 0.0 collective-permute-start.5
  74.3 0.3 collective-permute-start.6
  74.7 1.5 %collective-permute-start.7 = (bf16[32,3840]{1,0:T(8,128)(2,1)}, bf16[32,3840]{1,0:T(8,128)(2,1)S(1)}, u32[]{:S(2)}, u32[]{:S(2)}) collective-permute-start(bf16[32,3840]{1,0:T(8,128)(2,1)} %get-tuple-element.39), channel_id=1, source_target_pairs={{3,0},{2,1},{1,2},{0,3},{7,4},{6,5},{5,6},{4,7},{11,8},{10,9},{9,1... | collective-permute-start | bytes 737288 | tf_op jit(solution)/shard_map/ppermute | solution.py:617
  76.2 3.8 %collective-permute-done.4.refs_4_ = bf16[32,3840]{1,0:T(8,128)(2,1)S(1)} collective-permute-done((bf16[32,3840]{1,0:T(8,128)(2,1)}, bf16[32,3840]{1,0:T(8,128)(2,1)S(1)}, u32[]{:S(2)}, u32[]{:S(2)}) %collective-permute-start.4) | collective-permute-done | bytes 245792 | tf_op jit(solution)/shard_map/ppermute | solution.py:617
  80.0 0.0 collective-permute-start.8
  80.0 1.3 %collective-permute-done.10.refs_7_ = bf16[32,3840]{1,0:T(8,128)(2,1)S(1)} collective-permute-done((bf16[32,3840]{1,0:T(8,128)(2,1)}, bf16[32,3840]{1,0:T(8,128)(2,1)S(1)}, u32[]{:S(2)}, u32[]{:S(2)}) %collective-permute-start.10) | collective-permute-done | bytes 245792 | tf_op jit(solution)/shard_map/ppermute | solution.py:617
  81.4 3.4 %collective-permute-start.9 = (bf16[32,3840]{1,0:T(8,128)(2,1)}, bf16[32,3840]{1,0:T(8,128)(2,1)S(1)}, u32[]{:S(2)}, u32[]{:S(2)}) collective-permute-start(bf16[32,3840]{1,0:T(8,128)(2,1)} %get-tuple-element.42), channel_id=1, source_target_pairs={{10,0},{11,1},{8,2},{9,3},{14,4},{15,5},{12,6},{13,7},{2,8},{3,9},... | collective-permute-start | bytes 737288 | tf_op jit(solution)/shard_map/ppermute | solution.py:617
  84.8 11.5 %all_to_all.22.tangents = bf16[8,32,128]{2,1,0:T(8,128)(2,1)} all-to-all(bf16[8,32,128]{2,1,0:T(8,128)(2,1)} %get-tuple-element.30), channel_id=1, replica_groups=mesh['y'=2,'x'=2,'h'=2,'l'=2,'c'=2] {'x','l','c'}, dimensions={0} | all-to-all | bytes 131072 | tf_op jit(solution)/shard_map/all_to_all | solution.py:671
  96.3 3.0 %shard_map.196 = (f32[3,128]{1,0:T(4,128)}, f32[3,128]{1,0:T(4,128)}, f32[32,128]{1,0:T(8,128)}) custom-call(s32[8]{0:T(128)} %stack.29.ids, bf16[8,32,128]{2,1,0:T(8,128)(2,1)} %all_to_all.22.tangents, s32[8,512]{1,0:T(8,128)} %get-tuple-element.31.place, f32[8,512]{1,0:T(8,128)} %get-tuple-element.32.strain, f32[12,512]{1,0:T(8,128)} %grads.3, ...), custom_call_target="tpu_custom_call" | custom-call | tf_op jit(solution)/shard_map/pallas_call | solution.py:536
  99.3 5.0 %all-to-all-start.2 = ((f32[32,1,128]{2,1,0:T(1,128)}), f32[32,1,128]{2,1,0:T(1,128)S(1)}, u32[]{:S(2)}, u32[]{:S(2)}) async-start(f32[32,1,128]{2,1,0:T(1,128)} %bitcast.33), calls=%async_computation.2 | async-start | bytes 32768 | tf_op jit(solution)/shard_map/all_to_all | solution.py:680
  104.3 0.0 collective-permute-done.5.refs_1_
  104.3 0.0 copy-start.4
  104.3 0.0 collective-permute-done.6.refs_2_
  104.4 0.0 copy-start.5
  104.4 0.0 collective-permute-done.7.refs_3_
  104.4 0.0 copy-start.6
  104.4 0.0 collective-permute-done.8.refs_5_
  104.4 0.0 copy-start.7
  104.4 0.0 collective-permute-done.9.refs_6_
  104.4 0.0 copy-start.8
  104.4 0.0 copy-done.2
  104.4 0.0 copy-done.3
  104.5 0.6 copy-done.4
  105.1 0.1 copy-done.5
  105.1 0.1 copy-done.6
  105.2 0.1 copy-done.7
  105.3 0.1 copy-done.8
  105.4 5.8 %shard_map.197 = bf16[512,3072]{1,0:T(8,128)(2,1)} custom-call(s32[8]{0:T(128)} %stack.29.ids, s32[8,512]{1,0:T(8,128)} %get-tuple-element.31.place, bf16[8,32,128]{2,1,0:T(8,128)(2,1)} %all_to_all.22.tangents, bf16[32,3840]{1,0:T(8,128)(2,1)} %get-tuple-element.36.refs_0_, bf16[32,3840]{1,0:T(8,128)(2,1)} %copy-done.4, bf16[32,3840]{1,0:T(8,128)(2,1)} %copy-done.5, ...), custom_call_target="tpu_custom_call" | custom-call | tf_op jit(solution)/shard_map/pallas_call | solution.py:536
  111.2 0.2 all-to-all-done.2
  111.5 0.6 slice_reduce_fusion
  112.8 0.0 copy-done.13
  112.8 0.6 broadcast_multiply_fusion
  (6 shorter events, 0.0 us)
Async XLA Ops:
  0.6 30.4 %collective-permute-start.3 = (bf16[32,128,128]{2,1,0:T(8,128)(2,1)}, bf16[32,128,128]{2,1,0:T(8,128)(2,1)S(1)}, u32[]{:S(2)}, u32[]{:S(2)}) collective-permute-start(bf16[32,128,128]{2,1,0:T(8,128)(2,1)} %bitcast.39), channel_id=1, source_target_pairs={{0,0},{5,1},{2,2},{7,3},{4,4},{1,5},{6,6},{3,7},{12,8},{9,9},{14,1... | collective-permute-start | bytes 3145736 | tf_op jit(solution)/shard_map/ppermute | solution.py:617
  3.2 18.7 %copy-start.11 = (f32[20,1,6]{0,1,2:T(1,128)S(1)}, f32[20,1,6]{0,1,2:T(1,128)}, u32[]{:S(2)}) copy-start(f32[20,1,6]{0,1,2:T(1,128)} %param.27) | copy-start | bytes 1444
  3.2 18.8 %copy-start.12 = (f32[32,1,6]{0,1,2:T(1,128)S(1)}, f32[32,1,6]{0,1,2:T(1,128)}, u32[]{:S(2)}) copy-start(f32[32,1,6]{0,1,2:T(1,128)} %param.31) | copy-start | bytes 2308
  14.0 43.8 %all-to-all-start = ((bf16[8,32,3968]{2,1,0:T(8,128)(2,1)}), bf16[8,32,3968]{2,1,0:T(8,128)(2,1)S(1)}, u32[]{:S(2)}, u32[]{:S(2)}) async-start(bf16[8,32,3968]{2,1,0:T(8,128)(2,1)} %get-tuple-element.27), calls=%async_computation | async-start | bytes 4063232 | tf_op jit(solution)/shard_map/all_to_all | solution.py:643
  26.6 7.9 %collective-permute-start.2 = (bf16[10,128,128]{2,1,0:T(8,128)(2,1)}, bf16[10,128,128]{2,1,0:T(8,128)(2,1)S(1)}, u32[]{:S(2)}, u32[]{:S(2)}) collective-permute-start(bf16[10,128,128]{2,1,0:T(8,128)(2,1)} %get-tuple-element.26), channel_id=1, source_target_pairs={{0,0},{5,1},{2,2},{7,3},{4,4},{1,5},{6,6},{3,7},{12,8},{9,9},{14,1... | collective-permute-start | bytes 983048 | tf_op jit(solution)/shard_map/ppermute | solution.py:617
  28.3 6.3 %collective-permute-start.1 = (f32[96,128]{1,0:T(8,128)}, f32[96,128]{1,0:T(8,128)S(1)}, u32[]{:S(2)}, u32[]{:S(2)}) collective-permute-start(f32[96,128]{1,0:T(8,128)} %get-tuple-element.25), channel_id=1, source_target_pairs={{0,0},{5,1},{2,2},{7,3},{4,4},{1,5},{6,6},{3,7},{12,8},{9,9},{14,1... | collective-permute-start | bytes 147464 | tf_op jit(solution)/shard_map/ppermute | solution.py:617
  29.7 4.8 %collective-permute-start = (s32[8,128]{1,0:T(8,128)}, s32[8,128]{1,0:T(8,128)S(1)}, u32[]{:S(2)}, u32[]{:S(2)}) collective-permute-start(s32[8,128]{1,0:T(8,128)} %get-tuple-element.24), channel_id=1, source_target_pairs={{0,0},{5,1},{2,2},{7,3},{4,4},{1,5},{6,6},{3,7},{12,8},{9,9},{14,1... | collective-permute-start | bytes 12296 | tf_op jit(solution)/shard_map/ppermute | solution.py:617
  31.0 1.0 copy-start.14
  34.5 23.3 %copy-start.10 = (s32[8,128]{1,0:T(8,128)}, s32[8,128]{1,0:T(8,128)S(1)}, u32[]{:S(2)}) copy-start(s32[8,128]{1,0:T(8,128)S(1)} %collective-permute-done.ints) | copy-start | bytes 12292
  34.6 23.3 %copy-start.9 = (f32[96,128]{1,0:T(8,128)}, f32[96,128]{1,0:T(8,128)S(1)}, u32[]{:S(2)}) copy-start(f32[96,128]{1,0:T(8,128)S(1)} %collective-permute-done.1.small) | copy-start | bytes 147460
  34.6 23.3 %copy-start.1 = (bf16[10,128,128]{2,1,0:T(8,128)(2,1)}, bf16[10,128,128]{2,1,0:T(8,128)(2,1)S(1)}, u32[]{:S(2)}) copy-start(bf16[10,128,128]{2,1,0:T(8,128)(2,1)S(1)} %collective-permute-done.2.blocks) | copy-start | bytes 983044
  57.9 1.3 %copy-start = (bf16[8,32,3968]{2,1,0:T(8,128)(2,1)}, bf16[8,32,3968]{2,1,0:T(8,128)(2,1)S(1)}, u32[]{:S(2)}) copy-start(bf16[8,32,3968]{2,1,0:T(8,128)(2,1)S(1)} %all-to-all-done.msgs) | copy-start | bytes 6094852
  71.1 8.9 %collective-permute-start.4 = (bf16[32,3840]{1,0:T(8,128)(2,1)}, bf16[32,3840]{1,0:T(8,128)(2,1)S(1)}, u32[]{:S(2)}, u32[]{:S(2)}) collective-permute-start(bf16[32,3840]{1,0:T(8,128)(2,1)} %get-tuple-element.29), channel_id=1, source_target_pairs={{8,0},{9,1},{10,2},{11,3},{12,4},{13,5},{14,6},{15,7},{0,8},{1,9},... | collective-permute-start | bytes 737288 | tf_op jit(solution)/shard_map/ppermute | solution.py:617
  72.9 8.5 %collective-permute-start.10 = (bf16[32,3840]{1,0:T(8,128)(2,1)}, bf16[32,3840]{1,0:T(8,128)(2,1)S(1)}, u32[]{:S(2)}, u32[]{:S(2)}) collective-permute-start(bf16[32,3840]{1,0:T(8,128)(2,1)} %get-tuple-element.43), channel_id=1, source_target_pairs={{11,0},{10,1},{9,2},{8,3},{15,4},{14,5},{13,6},{12,7},{3,8},{2,9},... | collective-permute-start | bytes 737288 | tf_op jit(solution)/shard_map/ppermute | solution.py:617
  74.3 30.0 %collective-permute-start.5 = (bf16[32,3840]{1,0:T(8,128)(2,1)}, bf16[32,3840]{1,0:T(8,128)(2,1)S(1)}, u32[]{:S(2)}, u32[]{:S(2)}) collective-permute-start(bf16[32,3840]{1,0:T(8,128)(2,1)} %get-tuple-element.37), channel_id=1, source_target_pairs={{1,0},{0,1},{3,2},{2,3},{5,4},{4,5},{7,6},{6,7},{9,8},{8,9},{11,10... | collective-permute-start | bytes 737288 | tf_op jit(solution)/shard_map/ppermute | solution.py:617
  74.3 30.0 %collective-permute-start.6 = (bf16[32,3840]{1,0:T(8,128)(2,1)}, bf16[32,3840]{1,0:T(8,128)(2,1)S(1)}, u32[]{:S(2)}, u32[]{:S(2)}) collective-permute-start(bf16[32,3840]{1,0:T(8,128)(2,1)} %get-tuple-element.38), channel_id=1, source_target_pairs={{2,0},{3,1},{0,2},{1,3},{6,4},{7,5},{4,6},{5,7},{10,8},{11,9},{8,1... | collective-permute-start | bytes 737288 | tf_op jit(solution)/shard_map/ppermute | solution.py:617
  74.7 29.7 %collective-permute-start.7 = (bf16[32,3840]{1,0:T(8,128)(2,1)}, bf16[32,3840]{1,0:T(8,128)(2,1)S(1)}, u32[]{:S(2)}, u32[]{:S(2)}) collective-permute-start(bf16[32,3840]{1,0:T(8,128)(2,1)} %get-tuple-element.39), channel_id=1, source_target_pairs={{3,0},{2,1},{1,2},{0,3},{7,4},{6,5},{5,6},{4,7},{11,8},{10,9},{9,1... | collective-permute-start | bytes 737288 | tf_op jit(solution)/shard_map/ppermute | solution.py:617
  80.0 24.4 %copy-start.2 = (bf16[32,3840]{1,0:T(8,128)(2,1)}, bf16[32,3840]{1,0:T(8,128)(2,1)S(1)}, u32[]{:S(2)}) copy-start(bf16[32,3840]{1,0:T(8,128)(2,1)S(1)} %collective-permute-done.4.refs_4_) | copy-start | bytes 737284
  80.0 24.4 %collective-permute-start.8 = (bf16[32,3840]{1,0:T(8,128)(2,1)}, bf16[32,3840]{1,0:T(8,128)(2,1)S(1)}, u32[]{:S(2)}, u32[]{:S(2)}) collective-permute-start(bf16[32,3840]{1,0:T(8,128)(2,1)} %get-tuple-element.41), channel_id=1, source_target_pairs={{9,0},{8,1},{11,2},{10,3},{13,4},{12,5},{15,6},{14,7},{1,8},{0,9},... | collective-permute-start | bytes 737288 | tf_op jit(solution)/shard_map/ppermute | solution.py:617
  81.4 23.1 %copy-start.3 = (bf16[32,3840]{1,0:T(8,128)(2,1)}, bf16[32,3840]{1,0:T(8,128)(2,1)S(1)}, u32[]{:S(2)}) copy-start(bf16[32,3840]{1,0:T(8,128)(2,1)S(1)} %collective-permute-done.10.refs_7_) | copy-start | bytes 737284
  81.4 23.1 %collective-permute-start.9 = (bf16[32,3840]{1,0:T(8,128)(2,1)}, bf16[32,3840]{1,0:T(8,128)(2,1)S(1)}, u32[]{:S(2)}, u32[]{:S(2)}) collective-permute-start(bf16[32,3840]{1,0:T(8,128)(2,1)} %get-tuple-element.42), channel_id=1, source_target_pairs={{10,0},{11,1},{8,2},{9,3},{14,4},{15,5},{12,6},{13,7},{2,8},{3,9},... | collective-permute-start | bytes 737288 | tf_op jit(solution)/shard_map/ppermute | solution.py:617
  99.3 13.5 %copy-start.13 = (f32[3,128]{1,0:T(4,128)S(1)}, f32[3,128]{1,0:T(4,128)}, u32[]{:S(2)}) copy-start(f32[3,128]{1,0:T(4,128)} %get-tuple-element.20) | copy-start | bytes 4612
  99.3 12.2 %all-to-all-start.2 = ((f32[32,1,128]{2,1,0:T(1,128)}), f32[32,1,128]{2,1,0:T(1,128)S(1)}, u32[]{:S(2)}, u32[]{:S(2)}) async-start(f32[32,1,128]{2,1,0:T(1,128)} %bitcast.33), calls=%async_computation.2 | async-start | bytes 32768 | tf_op jit(solution)/shard_map/all_to_all | solution.py:680
  104.3 0.7 copy-start.4
  104.4 0.8 copy-start.5
  104.4 0.9 copy-start.6
  104.4 0.9 copy-start.7
  104.4 1.0 copy-start.8
